TPU v7x, 32 devices: a whole 2x2x4 slice. The times are simulated.
32 devices in a mesh: member: 2 (over y), row: 4 (over z), col: 2 (over x), sub: 2 (over core).
Axes of the slice: x: 2, y: 2, z: 4, core: 2. Of those that a mesh axis runs over, the one named last changes fastest.
Arguments:
- kernel: float32 [12288, 12288], P('row', ('col', 'sub')), may hold values from -0.0546875 to 0.0546875
- log_rate: float32 [512, 12288], P(('member', 'col', 'sub'), 'row'), parts along dimension 0, may hold values from -1 to 1
- state: float32 [512, 12288], P(('member', 'col', 'sub'), 'row'), parts along dimension 0, may hold values from -1 to 1
- base_stress: float32 [512, 12288], P(('member', 'col', 'sub'), 'row'), parts along dimension 0, may hold values from 1 to 4
- friction: float32 [12288], P('row'), may hold values from 0.5 to 2
- region: int32 [12288], P('row'), may hold values 0 or 1
- adjacency: int32 [12288], P('row'), may hold values from 0 to 12287, as said below
Outputs:
- final_rate: float32 [512, 12288], P(('member', 'col', 'sub'), 'row'), parts along dimension 0
- stress: float32 [512, 12288], P(('member', 'col', 'sub'), 'row'), parts along dimension 0
There are 2 independent parts, one for each index of `member`. A program takes and returns all parts, laid end to end along the dimension named above; an argument that names none is the same for every part. Nothing has to cross between parts.
Inputs may be any that keep to these rules, and one draw needn't show every extreme that they name: `region`: 1 marks a volume cell, 0 a fault patch. `adjacency`: each unknown's partner lies in the same aligned block of 3072 unknowns.
All inputs are finite; a program needn't handle non-finite values. No bound on the sum of `region` on one device may be relied on, other than what follows from the above.
Results may differ from a plain program's by a relative error of at most 0.0003.
Values sent between devices are 32-bit elements; how exact they have to be, the bound alone decides.
No kernel may reach another device: no remote copies, remote signals or barrier semaphores. Data moves between devices by JAX's collectives and lax.ppermute only.
A program may use at most 128 MiB of HBM per device.

v0:
```python
import jax
import jax.numpy as jnp
from jax import lax
from jax.sharding import PartitionSpec as P

NEWTON = 4


coupling = 0.3
step_size = 0.5


def from_root(shard, axis, root):
    mine = lax.axis_index(axis) == root
    return lax.psum(jnp.where(mine, shard, jnp.zeros_like(shard)), axis)


def couple(stress, partner):
    return stress + coupling * (jnp.take(stress, partner, axis=1) - stress)


def solve(log_rate, state, stress, friction, volume):
    value = log_rate
    for turn in range(NEWTON):
        expo = jnp.exp(value)
        slipx = jnp.exp(value + state)
        root = jnp.sqrt(1.0 + slipx * slipx)
        fault_f = friction * jnp.log(slipx + root)
        fault_d = friction * slipx / root
        creep = jnp.exp(state + value / 3.0)
        cell_f = friction * creep
        cell_d = friction * creep / 3.0
        resid = jnp.where(volume, cell_f, fault_f) + expo - stress
        deriv = jnp.where(volume, cell_d, fault_d) + expo
        value = value - jnp.clip(resid / deriv, -1.0, 1.0)
    return value


def rates_times(rates, kernel):
    return lax.dot_general(
        rates,
        kernel,
        (((1,), (1,)), ((), ())),
        precision=lax.Precision.HIGHEST,
        preferred_element_type=jnp.float32,
    )


def per_device(kernel, log_rate, state, base_stress, friction, region, adjacency):
    rows = kernel.shape[0]
    partner = adjacency - lax.axis_index("row") * rows
    volume = (region == 1)[None, :]
    fric = friction[None, :]

    def spread(rates):
        whole = lax.all_gather(rates, ("col", "sub"), axis=0, tiled=True)
        return from_root(whole, "row", lax.axis_index(("col", "sub")))

    def total(columns):
        return lax.psum_scatter(
            rates_times(columns, kernel), ("col", "sub"), scatter_dimension=0, tiled=True
        )

    first = total(spread(jnp.exp(log_rate)))
    section_one = solve(
        log_rate, state, couple(base_stress + step_size * first, partner), fric, volume
    )
    second = total(spread(jnp.exp(section_one)))
    stress = couple(base_stress + 0.5 * step_size * (first + second), partner)
    final_rate = solve(section_one, state, stress, fric, volume)
    return (final_rate, stress)


def solution(mesh):
    in_specs = (
        P("row", ("col", "sub")),
        P(("member", "col", "sub"), "row"),
        P(("member", "col", "sub"), "row"),
        P(("member", "col", "sub"), "row"),
        P("row"),
        P("row"),
        P("row"),
    )
    out_specs = (P(("member", "col", "sub"), "row"), P(("member", "col", "sub"), "row"))
    return jax.shard_map(
        per_device, mesh=mesh, in_specs=in_specs, out_specs=out_specs, check_vma=False
    )
```

profile of v0, /device:TPU:0, one launch (start us, length us, event | category | flops | bytes accessed | tf_op | source)
XLA Modules:
  0.0 509.2 jit_solution(4099974846927331563)
XLA Ops:
  7.2 0.0 all-gather.3.cloned.1.call-start
  7.2 2.1 exp.76
  9.4 0.0 all-reduce.3.cloned.1.call-start
  9.4 32.0 %all-gather.3.cloned.1.call-done = f32[256,3072]{1,0:T(8,128)} async-done(((f32[64,3072]{1,0:T(8,128)}), f32[256,3072]{1,0:T(8,128)}) %all-gather.3.cloned.1.call-update) | async-done | bytes 3145744 | tf_op jit(solution)/shard_map/all_gather | solution.py:56
  41.4 3.9 broadcast_select_fusion.1
  45.3 0.0 all-reduce.3.cloned.1.call-update
  45.3 0.0 reduce-scatter.3.cloned.1.call-start
  45.4 121.1 %all-reduce.3.cloned.1.call-done = f32[256,3072]{1,0:T(8,128)} async-done(((f32[256,3072]{1,0:T(8,128)}), f32[256,3072]{1,0:T(8,128)}) %all-reduce.3.cloned.1.call-update) | async-done | bytes 3145744 | tf_op jit(solution)/shard_map/psum | solution.py:15
  166.4 36.7 %fusion.7 = f32[256,3072]{1,0:T(8,128)} fusion(f32[256,3072]{1,0:T(8,128)} %all-reduce.3.cloned.1.call-done, f32[3072,3072]{1,0:T(8,128)} %param.9), kind=kOutput, calls=%fused_computation.19 | convolution fusion | flops 28991029248 | bytes 44040192 | tf_op jit(solution)/shard_map/dot_general | solution.py:40
  203.2 0.0 reduce-scatter.3.cloned.1.call-update
  203.2 0.0 all-gather.5.cloned.1.call-start
  203.3 0.6 copy-done.6
  203.9 36.4 %reduce-scatter.3.cloned.1.call-done = f32[64,3072]{1,0:T(8,128)} async-done(((f32[256,3072]{1,0:T(8,128)}), f32[64,3072]{1,0:T(8,128)}) %reduce-scatter.3.cloned.1.call-update) | async-done | bytes 786448 | tf_op jit(solution)/shard_map/reduce_scatter | solution.py:60
  240.3 1.2 multiply_add_fusion.1
  241.5 0.9 copy-done.4
  242.4 0.5 copy.9
  242.9 8.1 %gather_fusion = f32[3072,64]{1,0:T(8,128)S(1)} fusion(f32[64,3072]{0,1:T(8,128)S(1)} %copy.9, s32[3072]{0:T(1024)S(1)} %fusion.4), kind=kCustom, calls=%fused_computation.clone | custom fusion | bytes 1585152 | tf_op jit(solution)/shard_map/jit(_take)/gather | solution.py:19
  251.0 0.4 copy.10
  251.5 6.1 %fusion.6 = (f32[64,3072]{1,0:T(8,128)}, f32[64,3072]{1,0:T(8,128)}) fusion(f32[64,3072]{1,0:T(8,128)} %param.11, f32[64,3072]{1,0:T(8,128)} %param.10, f32[64,3072]{1,0:T(8,128)} %copy-done.4, f32[3072,64]{0,1:T(8,128)S(1)} %copy.10, pred[3072]{0:T(1024)(128)(4,1)S(1)} %compare_and_fusion, f32[3072]{0:T(1024)S(1)} %copy-done.7, ...), kind=kLoop, calls=%fused_computation.18 | loop fusion | flops 15728640 | bytes 4737024 | tf_op jit(solution)/shard_map/exp | solution.py:25
  257.6 0.0 all-reduce.5.cloned.1.call-start
  257.7 28.6 %all-gather.5.cloned.1.call-done = f32[256,3072]{1,0:T(8,128)} async-done(((f32[64,3072]{1,0:T(8,128)}), f32[256,3072]{1,0:T(8,128)}) %all-gather.5.cloned.1.call-update) | async-done | bytes 3145744 | tf_op jit(solution)/shard_map/all_gather | solution.py:56
  286.3 3.9 broadcast_select_fusion
  290.2 0.2 reduce-scatter.5.cloned.1.call-start
  290.4 120.9 %all-reduce.5.cloned.1.call-done = f32[256,3072]{1,0:T(8,128)} async-done(((f32[256,3072]{1,0:T(8,128)}), f32[256,3072]{1,0:T(8,128)}) %all-reduce.5.cloned.1.call-update) | async-done | bytes 3145744 | tf_op jit(solution)/shard_map/psum | solution.py:15
  411.3 36.7 %fusion.8 = f32[256,3072]{1,0:T(8,128)} fusion(f32[256,3072]{1,0:T(8,128)} %all-reduce.5.cloned.1.call-done, f32[3072,3072]{1,0:T(8,128)} %param.9), kind=kOutput, calls=%fused_computation.20 | convolution fusion | flops 28991029248 | bytes 44040192 | tf_op jit(solution)/shard_map/dot_general | solution.py:40
  448.1 37.1 %reduce-scatter.5.cloned.1.call-done = f32[64,3072]{1,0:T(8,128)} async-done(((f32[256,3072]{1,0:T(8,128)}), f32[64,3072]{1,0:T(8,128)}) %reduce-scatter.5.cloned.1.call-update) | async-done | bytes 786448 | tf_op jit(solution)/shard_map/reduce_scatter | solution.py:60
  485.2 1.3 multiply_add_fusion
  486.5 0.9 copy-done.3
  487.3 0.5 copy.11
  487.8 8.1 %gather_fusion.1 = f32[3072,64]{1,0:T(8,128)S(1)} fusion(f32[64,3072]{0,1:T(8,128)S(1)} %copy.11, s32[3072]{0:T(1024)S(1)} %fusion.4), kind=kCustom, calls=%fused_computation.1.clone | custom fusion | bytes 1585152 | tf_op jit(solution)/shard_map/jit(_take)/gather | solution.py:19
  495.9 0.4 copy.12
  496.4 6.0 %clamp_subtract_fusion = (f32[64,3072]{1,0:T(8,128)}, f32[64,3072]{1,0:T(8,128)}) fusion(f32[64,3072]{1,0:T(8,128)} %param.11, f32[64,3072]{1,0:T(8,128)} %get-tuple-element.6, f32[3072]{0:T(1024)S(1)} %copy-done.7, pred[3072]{0:T(1024)(128)(4,1)S(1)} %broadcast_compare_fusion, f32[64,3072]{1,0:T(8,128)} %copy-done.3, f32[3072,64]{0,1:T(8,128)S(1)} %copy.12, ...), kind=kLoop, calls=%fused_computation.10 | loop fusion | flops 15728640 | bytes 4737024 | tf_op jit(solution)/shard_map/sub | solution.py:35
  (20 shorter events, 0.1 us)
Async XLA Ops:
  7.2 34.2 %all-gather.3.cloned.1.call-start = ((), (), s32[]{:S(2)}) async-start(), calls=%async_computation.2 | async-start | bytes 3932160 | tf_op jit(solution)/shard_map/all_gather | solution.py:56
  9.4 157.1 %all-reduce.3.cloned.1.call-start = ((), (), s32[]{:S(2)}) async-start(), calls=%async_computation.3 | async-start | bytes 6291456 | tf_op jit(solution)/shard_map/psum | solution.py:15
  45.3 195.0 %reduce-scatter.3.cloned.1.call-start = ((), (), s32[]{:S(2)}) async-start(), calls=%async_computation.4 | async-start | bytes 3932160 | tf_op jit(solution)/shard_map/reduce_scatter | solution.py:60
  203.2 0.7 copy-start.6
  203.2 0.7 copy-start.5
  203.2 37.1 %copy-start = (f32[64,3072]{1,0:T(8,128)S(1)}, f32[64,3072]{1,0:T(8,128)}, u32[]{:S(2)}) copy-start(f32[64,3072]{1,0:T(8,128)} %param.12) | copy-start | bytes 2359300
  203.2 83.1 %all-gather.5.cloned.1.call-start = ((), (), s32[]{:S(2)}) async-start(), calls=%async_computation.5 | async-start | bytes 3932160 | tf_op jit(solution)/shard_map/all_gather | solution.py:56
  241.5 0.9 copy-start.4
  242.9 8.6 %copy-start.7 = (f32[3072]{0:T(1024)S(1)}, f32[3072]{0:T(1024)}, u32[]{:S(2)}) copy-start(f32[3072]{0:T(1024)} %param.13) | copy-start | bytes 36868
  257.6 153.7 %all-reduce.5.cloned.1.call-start = ((), (), s32[]{:S(2)}) async-start(), calls=%async_computation.6 | async-start | bytes 6291456 | tf_op jit(solution)/shard_map/psum | solution.py:15
  290.2 195.0 %reduce-scatter.5.cloned.1.call-start = ((), (), s32[]{:S(2)}) async-start(), calls=%async_computation.7 | async-start | bytes 3932160 | tf_op jit(solution)/shard_map/reduce_scatter | solution.py:60
  448.1 37.1 %copy-start.1 = (f32[64,3072]{1,0:T(8,128)S(1)}, f32[64,3072]{1,0:T(8,128)}, u32[]{:S(2)}) copy-start(f32[64,3072]{1,0:T(8,128)} %param.12) | copy-start | bytes 2359300
  448.1 37.1 %copy-start.2 = (f32[64,3072]{1,0:T(8,128)S(1)}, f32[64,3072]{1,0:T(8,128)}, u32[]{:S(2)}) copy-start(f32[64,3072]{1,0:T(8,128)} %reduce-scatter.3.cloned.1.call-done) | copy-start | bytes 2359300
  486.4 0.9 copy-start.3
Sparse Core Ops, SparseCore 0:
  10.1 31.2 all-gather.2
  45.4 120.9 all-reduce.2
  203.3 36.9 reduce-scatter.2
  257.7 28.5 all-gather.4
  290.3 120.9 all-reduce.4
  448.2 36.9 reduce-scatter.4
where the time goes:
time: 510 us; the launch traced here: 509 us
  waiting for transfers between devices  376 us (74%)
  matrix products  73.4 us (14%)
  local copies, waits for them, and re-layouts  22.6 us (4%)
  other arithmetic  22.4 us (4%)
  between operations  14.2 us (3%)
    psum x2, waiting for transfers between devices, from_root(): return lax.psum(jnp.where(mine, shard, jnp.zeros_like(shard)), axis)  242 us
    reduce_scatter x2, waiting for transfers between devices, total(): lax.psum_scatter(rates_times(columns, kernel), ('col', 'sub'), scatter_di...  73.5 us
    dot_general x2, matrix products, rates_times(): lax.dot_general(rates, kernel, (((1,), (1,)), ((), ())), precision=lax.Pr...  73.4 us
    all_gather x2, waiting for transfers between devices, spread(): whole = lax.all_gather(rates, ('col', 'sub'), axis=0, tiled=True)  60.6 us
    gather x4, local copies, waits for them, and re-layouts, couple(): return stress + coupling * (jnp.take(stress, partner, axis=1) - stress)  17.1 us
  transfers between devices with their start and end apart: 6, of which 6 were waited for; matrix products, arithmetic and copies ran while one was open for 0% of the time, Pallas kernels for 0%

commit v1 on v0

v1 whole, which is shorter than its diff:
```python
import jax
import jax.numpy as jnp
from jax import lax
from jax.experimental import pallas as pl
from jax.experimental.pallas import tpu as pltpu
from jax.sharding import PartitionSpec as P

NEWTON = 4
CHUNKS = 2
LANES = 128
SLOTS = 4

coupling = 0.3
step_size = 0.5

f32 = jnp.float32
bf16 = jnp.bfloat16
NT = (((1,), (1,)), ((), ()))
VMEM = pl.BlockSpec(memory_space=pltpu.VMEM)
ANY = pl.BlockSpec(memory_space=pl.ANY)


def newton(value, state, stress, friction, volume):
    grow = jnp.exp(state)
    for turn in range(NEWTON):
        expo = jnp.exp(value)
        slipx = expo * grow
        square = 1.0 + slipx * slipx
        inverse = lax.rsqrt(square)
        fault_f = jnp.log(slipx + square * inverse)
        fault_d = slipx * inverse
        creep = grow * jnp.exp(value * (1.0 / 3.0))
        part_f = friction * jnp.where(volume, creep, fault_f)
        part_d = friction * jnp.where(volume, creep * (1.0 / 3.0), fault_d)
        value = value - jnp.clip((part_f + expo - stress) / (part_d + expo), -1.0, 1.0)
    return value


def step_kernel(scale, n_sum, last, base, value, state, sums, friction, region, partner):
    high, wide = base.shape
    tiles = wide // LANES

    def body(*refs):
        base_ref, value_ref, state_ref = refs[:3]
        sum_refs = refs[3 : 3 + n_sum]
        friction_ref, region_ref, partner_ref = refs[3 + n_sum : 6 + n_sum]
        outs = refs[6 + n_sum : -1]
        raw = refs[-1]
        total = sum_refs[0][...]
        for ref in sum_refs[1:]:
            total = total + ref[...]
        if not last:
            outs[2][...] = total
        raw[...] = base_ref[...] + scale * total

        def tile(j, _):
            cols = pl.ds(pl.multiple_of(j * LANES, LANES), LANES)
            where = jnp.broadcast_to(partner_ref[:, cols], (8, LANES))
            lane = where % LANES
            block = where // LANES
            groups = high // 8
            moved = [jnp.zeros((8, LANES), f32) for _ in range(groups)]
            for k in range(tiles):
                here = block == k
                for g in range(groups):
                    got = jnp.take_along_axis(
                        raw[pl.ds(g * 8, 8), pl.ds(k * LANES, LANES)], lane, axis=1, mode="promise_in_bounds"
                    )
                    moved[g] = jnp.where(here, got, moved[g])
            fric = jnp.broadcast_to(friction_ref[:, cols], (8, LANES))
            volume = jnp.broadcast_to(region_ref[:, cols], (8, LANES)) == 1
            for g in range(groups):
                rows = pl.ds(g * 8, 8)
                own = raw[rows, cols]
                stress = own + coupling * (moved[g] - own)
                new = newton(value_ref[rows, cols], state_ref[rows, cols], stress, fric, volume)
                outs[0][rows, cols] = new
                outs[1][rows, cols] = stress if last else jnp.exp(new)
            return 0

        lax.fori_loop(0, tiles, tile, 0)

    return pl.pallas_call(
        body,
        in_specs=[VMEM] * (6 + n_sum),
        out_specs=[VMEM] * (2 if last else 3),
        out_shape=[jax.ShapeDtypeStruct((high, wide), f32)] * (2 if last else 3),
        scratch_shapes=[pltpu.VMEM((high, wide), f32)],
        compiler_params=pltpu.CompilerParams(vmem_limit_bytes=24 << 20),
        cost_estimate=pl.CostEstimate(flops=200 * high * wide, bytes_accessed=28 * high * wide, transcendentals=20 * high * wide),
    )(base, value, state, *sums, friction, region, partner)


def rates_times(pieces, kernel, tile=128):
    count = len(pieces)
    high, depth = pieces[0].shape
    rows = kernel.shape[0]
    much = count * high
    steps = rows // tile
    slots = min(SLOTS, steps)

    def body(*refs):
        parts, kernel_ref, outs = refs[:count], refs[count], refs[count + 1 : 2 * count + 1]
        stacked, held, sem = refs[2 * count + 1 :]

        def fetch(i, slot):
            return pltpu.make_async_copy(
                kernel_ref.at[pl.ds(pl.multiple_of(i * tile, tile), tile), :], held.at[slot], sem.at[slot]
            )

        for i in range(slots - 1):
            fetch(i, i).start()
        for p in range(count):
            whole = parts[p][...]
            upper = whole.astype(bf16)
            stacked[pl.ds(p * high, high), :] = upper
            stacked[pl.ds(much + p * high, high), :] = (whole - upper.astype(f32)).astype(bf16)

        def step(i, _):
            slot = lax.rem(i, slots)

            @pl.when(i + slots - 1 < steps)
            def _():
                fetch(i + slots - 1, lax.rem(i + slots - 1, slots)).start()

            fetch(i, slot).wait()
            whole = held[slot]
            upper = whole.astype(bf16)
            lower = (whole - upper.astype(f32)).astype(bf16)
            both = lax.dot_general(stacked[...], upper, NT, preferred_element_type=f32)
            rest = lax.dot_general(stacked[pl.ds(0, much), :], lower, NT, preferred_element_type=f32)
            total = both[:much] + both[much:] + rest
            cols = pl.ds(pl.multiple_of(i * tile, tile), tile)
            for p in range(count):
                outs[p][:, cols] = total[p * high : (p + 1) * high]
            return 0

        lax.fori_loop(0, steps, step, 0)

    return pl.pallas_call(
        body,
        in_specs=[VMEM] * count + [ANY],
        out_specs=[VMEM] * count,
        out_shape=[jax.ShapeDtypeStruct((high, rows), f32)] * count,
        scratch_shapes=[
            pltpu.VMEM((2 * much, depth), bf16),
            pltpu.VMEM((slots, tile, depth), f32),
            pltpu.SemaphoreType.DMA((slots,)),
        ],
        compiler_params=pltpu.CompilerParams(vmem_limit_bytes=32 << 20),
        cost_estimate=pl.CostEstimate(
            flops=6 * much * rows * depth, bytes_accessed=4 * rows * depth, transcendentals=0
        ),
    )(*pieces, kernel)


def spread_small(rates):
    row = lax.axis_index("row")
    here = lax.axis_index(("col", "sub"))
    up1 = lax.ppermute(rates, "row", [(0, 1), (1, 2), (2, 3)])
    down1 = lax.ppermute(rates, "row", [(1, 0), (2, 1), (3, 2)])
    up2 = lax.ppermute(up1, "row", [(1, 2), (2, 3)])
    down2 = lax.ppermute(down1, "row", [(1, 0), (2, 1)])
    far = lax.ppermute(jnp.where(row == 1, up1, down1), "row", [(1, 3), (2, 0)])
    near2 = jnp.where(row >= 2, up2, down2)
    pieces = []
    for flip in range(4):
        away = (here ^ flip) - row
        picked = jnp.where(
            away == 0,
            rates,
            jnp.where(
                away == 1,
                down1,
                jnp.where(away == -1, up1, jnp.where(jnp.abs(away) == 2, near2, far)),
            ),
        )
        if flip:
            picked = lax.ppermute(picked, ("col", "sub"), [(i, i ^ flip) for i in range(4)])
        pieces.append(picked)
    return pieces


def total_small(parts):
    other = [(i, i ^ 1) for i in range(4)]
    across = [(i, i ^ 2) for i in range(4)]
    mine = lax.ppermute(parts[1], ("col", "sub"), other)
    theirs = parts[2] + lax.ppermute(parts[3], ("col", "sub"), other)
    return [parts[0], mine, lax.ppermute(theirs, ("col", "sub"), across)]


def spread_any(rates):
    blocks = lax.all_gather(rates, "row", axis=0)
    pieces = lax.all_to_all(blocks, ("col", "sub"), 0, 0)
    return [pieces[p] for p in range(pieces.shape[0])]


def total_any(parts):
    return [lax.psum_scatter(jnp.concatenate(parts, axis=0), ("col", "sub"), scatter_dimension=0, tiled=True)]


def solution(mesh):
    small = mesh.shape["row"] == 4 and mesh.shape["col"] == 2 and mesh.shape["sub"] == 2
    spread, total = (spread_small, total_small) if small else (spread_any, total_any)

    def per_device(kernel, log_rate, state, base_stress, friction, region, adjacency):
        rows = kernel.shape[0]
        samples = log_rate.shape[0]
        partner = (adjacency - lax.axis_index("row") * rows)[None, :]
        region = region[None, :]
        friction = friction[None, :]
        chunks = CHUNKS if small else 1
        high = samples // chunks
        cut = [slice(k * high, (k + 1) * high) for k in range(chunks)]

        pieces = [spread(jnp.exp(log_rate[s])) for s in cut]
        middle = []
        for k, s in enumerate(cut):
            sums = total(rates_times(pieces[k], kernel))
            value, rates, first = step_kernel(
                step_size, len(sums), False, base_stress[s], log_rate[s], state[s], sums, friction, region, partner
            )
            middle.append((value, first, spread(rates)))
        done = []
        for k, s in enumerate(cut):
            value, first, pieces = middle[k]
            sums = [first] + total(rates_times(pieces, kernel))
            done.append(
                step_kernel(
                    0.5 * step_size, len(sums), True, base_stress[s], value, state[s], sums, friction, region, partner
                )
            )
        return (
            jnp.concatenate([d[0] for d in done], axis=0),
            jnp.concatenate([d[1] for d in done], axis=0),
        )

    in_specs = (
        P("row", ("col", "sub")),
        P(("member", "col", "sub"), "row"),
        P(("member", "col", "sub"), "row"),
        P(("member", "col", "sub"), "row"),
        P("row"),
        P("row"),
        P("row"),
    )
    out_specs = (P(("member", "col", "sub"), "row"), P(("member", "col", "sub"), "row"))
    return jax.shard_map(per_device, mesh=mesh, in_specs=in_specs, out_specs=out_specs, check_vma=False)
```

time: 510 us -> 285 us (0.56)
  waiting for transfers between devices: 376 us -> 98.2 us
  Pallas kernels: 0 us -> 111 us
  matrix products: 73.4 us -> 0 us
  starting transfers between devices: 0.43 us -> 58 us
  local copies, waits for them, and re-layouts: 22.6 us -> 4.1 us
  between operations: 14.2 us -> 1.23 us
  other arithmetic: 22.4 us -> 10 us
    psum x2 -> x0, waiting for transfers between devices: 242 us -> none  [from_root(): return lax.psum(jnp.where(mine, shard, jnp.zeros_like(shard)), axis)]
    pallas_call x0 -> x8, Pallas kernels: none -> 111 us  [the longest x4 83.4 us: rates_times(): pl.pallas_call(body, in_specs=[VMEM] * count + [ANY], out_specs=[VMEM] *...]
    ppermute x0 -> x44, waiting for transfers between devices: none -> 98.2 us  [the longest x12 26.4 us: spread_small(): lax.ppermute(picked, ('col', 'sub'), [(i, i ^ flip) for i in range(4)])]
    reduce_scatter x2 -> x0, waiting for transfers between devices: 73.5 us -> none  [total(): lax.psum_scatter(rates_times(columns, kernel), ('col', 'sub'), scatter_di...]
    dot_general x2 -> x0, matrix products: 73.4 us -> none  [rates_times(): lax.dot_general(rates, kernel, (((1,), (1,)), ((), ())), precision=lax.Pr...]
    all_gather x2 -> x0, waiting for transfers between devices: 60.6 us -> none  [spread(): whole = lax.all_gather(rates, ('col', 'sub'), axis=0, tiled=True)]
    ppermute x0 -> x44, starting transfers between devices: none -> 58 us  [the longest x4 24.7 us: spread_small(): up1 = lax.ppermute(rates, 'row', [(0, 1), (1, 2), (2, 3)])]
    gather x4 -> x0, local copies, waits for them, and re-layouts: 17.1 us -> none  [couple(): return stress + coupling * (jnp.take(stress, partner, axis=1) - stress)]
  transfers between devices with their start and end apart: 6 -> 44, of which waited for: 6 -> 19; matrix products, arithmetic and copies ran while one was open for 0% -> 2% of each run, Pallas kernels for 0% -> 37%
where the time goes in v1:
time: 285 us; the launch traced here: 283 us
  Pallas kernels  111 us (39%)
  waiting for transfers between devices  98.2 us (34%)
  starting transfers between devices  58 us (20%)
  other arithmetic  10 us (4%)
  local copies, waits for them, and re-layouts  4.1 us (1%)
    pallas_call x4, Pallas kernels, rates_times(): pl.pallas_call(body, in_specs=[VMEM] * count + [ANY], out_specs=[VMEM] *...  83.4 us
    pallas_call x4, Pallas kernels, step_kernel(): pl.pallas_call(body, in_specs=[VMEM] * (6 + n_sum), out_specs=[VMEM] * (2...  27.9 us
    ppermute x12, waiting for transfers between devices, spread_small(): lax.ppermute(picked, ('col', 'sub'), [(i, i ^ flip) for i in range(4)])  26.4 us
    ppermute x4, starting transfers between devices, spread_small(): up1 = lax.ppermute(rates, 'row', [(0, 1), (1, 2), (2, 3)])  24.7 us
    ppermute x4, waiting for transfers between devices, spread_small(): down1 = lax.ppermute(rates, 'row', [(1, 0), (2, 1), (3, 2)])  23.1 us
    ppermute x4, waiting for transfers between devices, spread_small(): far = lax.ppermute(jnp.where(row == 1, up1, down1), 'row', [(1, 3), (2, 0)])  21.4 us
    ppermute x4, waiting for transfers between devices, spread_small(): down2 = lax.ppermute(down1, 'row', [(1, 0), (2, 1)])  12.8 us
    ppermute x4, waiting for transfers between devices, total_small(): return [parts[0], mine, lax.ppermute(theirs, ('col', 'sub'), across)]  10.6 us
  transfers between devices with their start and end apart: 44, of which 19 were waited for; matrix products, arithmetic and copies ran while one was open for 2% of the time, Pallas kernels for 37%

profile of v1, /device:TPU:0, one launch (start us, length us, event | category | flops | bytes accessed | tf_op | source)
XLA Modules:
  0.0 282.8 jit_solution(2325027697374209685)
XLA Ops:
  3.1 5.6 %collective-permute-start.1 = (f32[32,3072]{1,0:T(8,128)S(1)}, f32[32,3072]{1,0:T(8,128)S(1)}, u32[]{:S(2)}, u32[]{:S(2)}) collective-permute-start(f32[32,3072]{1,0:T(8,128)S(1)} %slice_exponential_fusion.1), channel_id=1, source_target_pairs={{0,4},{4,8},{8,12},{1,5},{5,9},{9,13},{2,6},{6,10},{10,14},{3,7},{... | collective-permute-start | bytes 1179656 | tf_op jit(solution)/shard_map/ppermute | solution.py:160
  8.7 7.1 %collective-permute-done = f32[32,3072]{1,0:T(8,128)S(1)} collective-permute-done((f32[32,3072]{1,0:T(8,128)S(1)}, f32[32,3072]{1,0:T(8,128)S(1)}, u32[]{:S(2)}, u32[]{:S(2)}) %collective-permute-start) | collective-permute-done | bytes 393248 | tf_op jit(solution)/shard_map/ppermute | solution.py:161
  20.4 11.5 %collective-permute-done.4 = f32[32,3072]{1,0:T(8,128)S(1)} collective-permute-done((f32[32,3072]{1,0:T(8,128)S(1)}, f32[32,3072]{1,0:T(8,128)S(1)}, u32[]{:S(2)}, u32[]{:S(2)}) %collective-permute-start.4) | collective-permute-done | bytes 393248 | tf_op jit(solution)/shard_map/ppermute | solution.py:164
  31.9 6.4 %collective-permute-done.3 = f32[32,3072]{1,0:T(8,128)S(1)} collective-permute-done((f32[32,3072]{1,0:T(8,128)S(1)}, f32[32,3072]{1,0:T(8,128)S(1)}, u32[]{:S(2)}, u32[]{:S(2)}) %collective-permute-start.3) | collective-permute-done | bytes 393248 | tf_op jit(solution)/shard_map/ppermute | solution.py:163
  38.3 2.1 select_select_fusion.12
  41.7 4.6 %collective-permute-start.23 = (f32[32,3072]{1,0:T(8,128)S(1)}, f32[32,3072]{1,0:T(8,128)S(1)}, u32[]{:S(2)}, u32[]{:S(2)}) collective-permute-start(f32[32,3072]{1,0:T(8,128)S(1)} %get-tuple-element.74), channel_id=1, source_target_pairs={{0,4},{4,8},{8,12},{1,5},{5,9},{9,13},{2,6},{6,10},{10,14},{3,7},{... | collective-permute-start | bytes 1179656 | tf_op jit(solution)/shard_map/ppermute | solution.py:160
  47.6 1.6 collective-permute-start.6
  49.5 3.4 %collective-permute-done.22 = f32[32,3072]{1,0:T(8,128)S(1)} collective-permute-done((f32[32,3072]{1,0:T(8,128)S(1)}, f32[32,3072]{1,0:T(8,128)S(1)}, u32[]{:S(2)}, u32[]{:S(2)}) %collective-permute-start.22) | collective-permute-done | bytes 393248 | tf_op jit(solution)/shard_map/ppermute | solution.py:161
  57.4 2.2 collective-permute-done.6.refs_2_
  59.6 7.5 %collective-permute-done.7.refs_3_ = f32[32,3072]{1,0:T(8,128)S(1)} collective-permute-done((f32[32,3072]{1,0:T(8,128)S(1)}, f32[32,3072]{1,0:T(8,128)S(1)}, u32[]{:S(2)}, u32[]{:S(2)}) %collective-permute-start.7) | collective-permute-done | bytes 393248 | tf_op jit(solution)/shard_map/ppermute | solution.py:179
  67.1 21.4 %shard_map.86 = (f32[32,3072]{1,0:T(8,128)S(1)}, f32[32,3072]{1,0:T(8,128)S(1)}, f32[32,3072]{1,0:T(8,128)S(1)}, f32[32,3072]{1,0:T(8,128)}) custom-call(f32[32,3072]{1,0:T(8,128)S(1)} %get-tuple-element.64.refs_0_, f32[32,3072]{1,0:T(8,128)S(1)} %collective-permute-done.5.refs_1_, f32[32,3072]{1,0:T(8,128)S(1)} %collective-permute-done.6.refs_2_, ...), custom_call_target="tpu_custom_call" | custom-call | flops 7247757312 | bytes 37748736 | tf_op jit(solution)/shard_map/pallas_call | solution.py:140
  95.6 1.6 collective-permute-start.10
  97.1 6.3 %collective-permute-done.28.refs_2_ = f32[32,3072]{1,0:T(8,128)S(1)} collective-permute-done((f32[32,3072]{1,0:T(8,128)}, f32[32,3072]{1,0:T(8,128)S(1)}, u32[]{:S(2)}, u32[]{:S(2)}) %collective-permute-start.28) | collective-permute-done | bytes 393248 | tf_op jit(solution)/shard_map/ppermute | solution.py:179
  103.5 7.5 %collective-permute-done.29.refs_3_ = f32[32,3072]{1,0:T(8,128)S(1)} collective-permute-done((f32[32,3072]{1,0:T(8,128)}, f32[32,3072]{1,0:T(8,128)S(1)}, u32[]{:S(2)}, u32[]{:S(2)}) %collective-permute-start.29) | collective-permute-done | bytes 393248 | tf_op jit(solution)/shard_map/ppermute | solution.py:179
  111.0 20.6 %shard_map.90 = (f32[32,3072]{1,0:T(8,128)S(1)}, f32[32,3072]{1,0:T(8,128)S(1)}, f32[32,3072]{1,0:T(8,128)S(1)}, f32[32,3072]{1,0:T(8,128)S(1)}) custom-call(f32[32,3072]{1,0:T(8,128)S(1)} %get-tuple-element.67.refs_0_, f32[32,3072]{1,0:T(8,128)S(1)} %collective-permute-done.27.refs_1_, f32[32,3072]{1,0:T(8,128)S(1)} %collective-permute-done.28.refs_2_, ...), custom_call_target="tpu_custom_call" | custom-call | flops 7247757312 | bytes 37748736 | tf_op jit(solution)/shard_map/pallas_call | solution.py:140
  133.9 7.0 %shard_map.87 = (f32[32,3072]{1,0:T(8,128)S(1)}, f32[32,3072]{1,0:T(8,128)S(1)}, f32[32,3072]{1,0:T(8,128)S(1)}) custom-call(f32[32,3072]{1,0:T(8,128)S(1)} %get-tuple-element.82.refs_0_, f32[32,3072]{1,0:T(8,128)S(1)} %copy-done, f32[32,3072]{1,0:T(8,128)S(1)} %get-tuple-element.77.refs_2_, f32[32,3072]{1,0:T(8,128)S(1)} %copy-done.3, ...), custom_call_target="tpu_custom_call" | custom-call | flops 19660800 | bytes 2752512 | tf_op jit(solution)/shard_map/pallas_call | solution.py:83
  142.2 4.6 %collective-permute-start.12 = (f32[32,3072]{1,0:T(8,128)S(1)}, f32[32,3072]{1,0:T(8,128)S(1)}, u32[]{:S(2)}, u32[]{:S(2)}) collective-permute-start(f32[32,3072]{1,0:T(8,128)S(1)} %get-tuple-element.34), channel_id=1, source_target_pairs={{0,4},{4,8},{8,12},{1,5},{5,9},{9,13},{2,6},{6,10},{10,14},{3,7},{... | collective-permute-start | bytes 1179656 | tf_op jit(solution)/shard_map/ppermute | solution.py:160
  147.0 1.5 collective-permute-start.32
  148.5 5.6 %collective-permute-done.11 = f32[32,3072]{1,0:T(8,128)S(1)} collective-permute-done((f32[32,3072]{1,0:T(8,128)S(1)}, f32[32,3072]{1,0:T(8,128)S(1)}, u32[]{:S(2)}, u32[]{:S(2)}) %collective-permute-start.11) | collective-permute-done | bytes 393248 | tf_op jit(solution)/shard_map/ppermute | solution.py:161
  160.1 7.0 %shard_map.91 = (f32[32,3072]{1,0:T(8,128)S(1)}, f32[32,3072]{1,0:T(8,128)S(1)}, f32[32,3072]{1,0:T(8,128)S(1)}) custom-call(f32[32,3072]{1,0:T(8,128)S(1)} %get-tuple-element.81.refs_0_, f32[32,3072]{1,0:T(8,128)S(1)} %get-tuple-element.75.refs_1_, f32[32,3072]{1,0:T(8,128)S(1)} %get-tuple-element.78.refs_2_, f32[32,3072]{1,0:T(8,128)S(1)} %get-tuple-element.40.refs_3_, ...), custom_call_target="tpu_custom_call" | custom-call | flops 19660800 | bytes 2752512 | tf_op jit(solution)/shard_map/pallas_call | solution.py:83
  168.4 10.0 %collective-permute-start.34 = (f32[32,3072]{1,0:T(8,128)S(1)}, f32[32,3072]{1,0:T(8,128)S(1)}, u32[]{:S(2)}, u32[]{:S(2)}) collective-permute-start(f32[32,3072]{1,0:T(8,128)S(1)} %get-tuple-element.46), channel_id=1, source_target_pairs={{0,4},{4,8},{8,12},{1,5},{5,9},{9,13},{2,6},{6,10},{10,14},{3,7},{... | collective-permute-start | bytes 1179656 | tf_op jit(solution)/shard_map/ppermute | solution.py:160
  178.5 6.9 %collective-permute-done.33 = f32[32,3072]{1,0:T(8,128)S(1)} collective-permute-done((f32[32,3072]{1,0:T(8,128)S(1)}, f32[32,3072]{1,0:T(8,128)S(1)}, u32[]{:S(2)}, u32[]{:S(2)}) %collective-permute-start.33) | collective-permute-done | bytes 393248 | tf_op jit(solution)/shard_map/ppermute | solution.py:161
  189.1 1.6 collective-permute-start.17
  190.6 9.9 %collective-permute-done.37 = f32[32,3072]{1,0:T(8,128)S(1)} collective-permute-done((f32[32,3072]{1,0:T(8,128)S(1)}, f32[32,3072]{1,0:T(8,128)S(1)}, u32[]{:S(2)}, u32[]{:S(2)}) %collective-permute-start.37) | collective-permute-done | bytes 393248 | tf_op jit(solution)/shard_map/ppermute | solution.py:164
  200.5 6.4 %collective-permute-done.36 = f32[32,3072]{1,0:T(8,128)S(1)} collective-permute-done((f32[32,3072]{1,0:T(8,128)S(1)}, f32[32,3072]{1,0:T(8,128)S(1)}, u32[]{:S(2)}, u32[]{:S(2)}) %collective-permute-start.36) | collective-permute-done | bytes 393248 | tf_op jit(solution)/shard_map/ppermute | solution.py:163
  207.3 1.6 collective-permute-start.39
  209.2 2.7 collective-permute-done.18.refs_3_
  211.9 20.7 %shard_map.88 = (f32[32,3072]{1,0:T(8,128)S(1)}, f32[32,3072]{1,0:T(8,128)S(1)}, f32[32,3072]{1,0:T(8,128)S(1)}, f32[32,3072]{1,0:T(8,128)S(1)}) custom-call(f32[32,3072]{1,0:T(8,128)S(1)} %get-tuple-element.70.refs_0_, f32[32,3072]{1,0:T(8,128)S(1)} %collective-permute-done.16.refs_1_, f32[32,3072]{1,0:T(8,128)S(1)} %collective-permute-done.17.refs_2_, ...), custom_call_target="tpu_custom_call" | custom-call | flops 7247757312 | bytes 37748736 | tf_op jit(solution)/shard_map/pallas_call | solution.py:140
  232.8 20.6 %shard_map.92 = (f32[32,3072]{1,0:T(8,128)S(1)}, f32[32,3072]{1,0:T(8,128)S(1)}, f32[32,3072]{1,0:T(8,128)S(1)}, f32[32,3072]{1,0:T(8,128)S(1)}) custom-call(f32[32,3072]{1,0:T(8,128)S(1)} %get-tuple-element.73.refs_0_, f32[32,3072]{1,0:T(8,128)S(1)} %collective-permute-done.38.refs_1_, f32[32,3072]{1,0:T(8,128)S(1)} %collective-permute-done.39.refs_2_, ...), custom_call_target="tpu_custom_call" | custom-call | flops 7247757312 | bytes 37748736 | tf_op jit(solution)/shard_map/pallas_call | solution.py:140
  256.4 9.6 %collective-permute-done.21.refs_6_ = f32[32,3072]{1,0:T(8,128)S(1)} collective-permute-done((f32[32,3072]{1,0:T(8,128)S(1)}, f32[32,3072]{1,0:T(8,128)S(1)}, u32[]{:S(2)}, u32[]{:S(2)}) %collective-permute-start.21) | collective-permute-done | bytes 393248 | tf_op jit(solution)/shard_map/ppermute | solution.py:189
  266.1 6.9 %shard_map.89 = (f32[32,3072]{1,0:T(8,128)S(1)}, f32[32,3072]{1,0:T(8,128)S(1)}) custom-call(f32[32,3072]{1,0:T(8,128)S(1)} %get-tuple-element.82.refs_0_, f32[32,3072]{1,0:T(8,128)S(1)} %get-tuple-element.32.refs_1_, f32[32,3072]{1,0:T(8,128)S(1)} %get-tuple-element.77.refs_2_, f32[32,3072]{1,0:T(8,128)S(1)} %get-tuple-element.33.refs_3_, ...), custom_call_target="tpu_custom_call" | custom-call | flops 19660800 | bytes 2752512 | tf_op jit(solution)/shard_map/pallas_call | solution.py:83
  274.0 6.9 %shard_map.93 = (f32[32,3072]{1,0:T(8,128)S(1)}, f32[32,3072]{1,0:T(8,128)S(1)}) custom-call(f32[32,3072]{1,0:T(8,128)S(1)} %get-tuple-element.81.refs_0_, f32[32,3072]{1,0:T(8,128)S(1)} %get-tuple-element.44.refs_1_, f32[32,3072]{1,0:T(8,128)S(1)} %get-tuple-element.78.refs_2_, f32[32,3072]{1,0:T(8,128)S(1)} %get-tuple-element.45.refs_3_, ...), custom_call_target="tpu_custom_call" | custom-call | flops 19660800 | bytes 2752512 | tf_op jit(solution)/shard_map/pallas_call | solution.py:83
  (113 shorter events, 42.6 us)
Async XLA Ops:
  1.8 14.0 %collective-permute-start = (f32[32,3072]{1,0:T(8,128)S(1)}, f32[32,3072]{1,0:T(8,128)S(1)}, u32[]{:S(2)}, u32[]{:S(2)}) collective-permute-start(f32[32,3072]{1,0:T(8,128)S(1)} %slice_exponential_fusion.1), channel_id=1, source_target_pairs={{4,0},{8,4},{12,8},{5,1},{9,5},{13,9},{6,2},{10,6},{14,10},{7,3},{... | collective-permute-start | bytes 1179656 | tf_op jit(solution)/shard_map/ppermute | solution.py:161
  3.1 13.9 %collective-permute-start.1 = (f32[32,3072]{1,0:T(8,128)S(1)}, f32[32,3072]{1,0:T(8,128)S(1)}, u32[]{:S(2)}, u32[]{:S(2)}) collective-permute-start(f32[32,3072]{1,0:T(8,128)S(1)} %slice_exponential_fusion.1), channel_id=1, source_target_pairs={{0,4},{4,8},{8,12},{1,5},{5,9},{9,13},{2,6},{6,10},{10,14},{3,7},{... | collective-permute-start | bytes 1179656 | tf_op jit(solution)/shard_map/ppermute | solution.py:160
  17.0 14.8 %collective-permute-start.4 = (f32[32,3072]{1,0:T(8,128)S(1)}, f32[32,3072]{1,0:T(8,128)S(1)}, u32[]{:S(2)}, u32[]{:S(2)}) collective-permute-start(f32[32,3072]{1,0:T(8,128)S(1)} %broadcast_select_fusion.3), channel_id=1, source_target_pairs={{4,12},{8,0},{5,13},{9,1},{6,14},{10,2},{7,15},{11,3},{20,28},{24,... | collective-permute-start | bytes 1179656 | tf_op jit(solution)/shard_map/ppermute | solution.py:164
  18.3 13.5 %collective-permute-start.2 = (f32[32,3072]{1,0:T(8,128)S(1)}, f32[32,3072]{1,0:T(8,128)S(1)}, u32[]{:S(2)}, u32[]{:S(2)}) collective-permute-start(f32[32,3072]{1,0:T(8,128)S(1)} %collective-permute-done.1), channel_id=1, source_target_pairs={{4,8},{8,12},{5,9},{9,13},{6,10},{10,14},{7,11},{11,15},{20,24},{2... | collective-permute-start | bytes 1179656 | tf_op jit(solution)/shard_map/ppermute | solution.py:162
  19.0 19.3 %collective-permute-start.3 = (f32[32,3072]{1,0:T(8,128)S(1)}, f32[32,3072]{1,0:T(8,128)S(1)}, u32[]{:S(2)}, u32[]{:S(2)}) collective-permute-start(f32[32,3072]{1,0:T(8,128)S(1)} %collective-permute-done), channel_id=1, source_target_pairs={{4,0},{8,4},{5,1},{9,5},{6,2},{10,6},{7,3},{11,7},{20,16},{24,20},... | collective-permute-start | bytes 1179656 | tf_op jit(solution)/shard_map/ppermute | solution.py:163
  40.4 12.4 %collective-permute-start.22 = (f32[32,3072]{1,0:T(8,128)S(1)}, f32[32,3072]{1,0:T(8,128)S(1)}, u32[]{:S(2)}, u32[]{:S(2)}) collective-permute-start(f32[32,3072]{1,0:T(8,128)S(1)} %get-tuple-element.74), channel_id=1, source_target_pairs={{4,0},{8,4},{12,8},{5,1},{9,5},{13,9},{6,2},{10,6},{14,10},{7,3},{... | collective-permute-start | bytes 1179656 | tf_op jit(solution)/shard_map/ppermute | solution.py:161
  49.2 17.9 %collective-permute-start.7 = (f32[32,3072]{1,0:T(8,128)S(1)}, f32[32,3072]{1,0:T(8,128)S(1)}, u32[]{:S(2)}, u32[]{:S(2)}) collective-permute-start(f32[32,3072]{1,0:T(8,128)S(1)} %get-tuple-element.56), channel_id=1, source_target_pairs={{0,3},{1,2},{2,1},{3,0},{4,7},{5,6},{6,5},{7,4},{8,11},{9,10},{10,... | collective-permute-start | bytes 1179656 | tf_op jit(solution)/shard_map/ppermute | solution.py:179
  54.0 35.1 %collective-permute-start.26 = (f32[32,3072]{1,0:T(8,128)S(1)}, f32[32,3072]{1,0:T(8,128)S(1)}, u32[]{:S(2)}, u32[]{:S(2)}) collective-permute-start(f32[32,3072]{1,0:T(8,128)S(1)} %broadcast_select_fusion.1), channel_id=1, source_target_pairs={{4,12},{8,0},{5,13},{9,1},{6,14},{10,2},{7,15},{11,3},{20,28},{24,... | collective-permute-start | bytes 1179656 | tf_op jit(solution)/shard_map/ppermute | solution.py:164
  55.4 33.8 %collective-permute-start.24 = (f32[32,3072]{1,0:T(8,128)S(1)}, f32[32,3072]{1,0:T(8,128)S(1)}, u32[]{:S(2)}, u32[]{:S(2)}) collective-permute-start(f32[32,3072]{1,0:T(8,128)S(1)} %collective-permute-done.23), channel_id=1, source_target_pairs={{4,8},{8,12},{5,9},{9,13},{6,10},{10,14},{7,11},{11,15},{20,24},{2... | collective-permute-start | bytes 1179656 | tf_op jit(solution)/shard_map/ppermute | solution.py:162
  56.1 33.1 %collective-permute-start.25 = (f32[32,3072]{1,0:T(8,128)S(1)}, f32[32,3072]{1,0:T(8,128)S(1)}, u32[]{:S(2)}, u32[]{:S(2)}) collective-permute-start(f32[32,3072]{1,0:T(8,128)S(1)} %collective-permute-done.22), channel_id=1, source_target_pairs={{4,0},{8,4},{5,1},{9,5},{6,2},{10,6},{7,3},{11,7},{20,16},{24,20},... | collective-permute-start | bytes 1179656 | tf_op jit(solution)/shard_map/ppermute | solution.py:163
  92.8 18.2 %collective-permute-start.29 = (f32[32,3072]{1,0:T(8,128)}, f32[32,3072]{1,0:T(8,128)S(1)}, u32[]{:S(2)}, u32[]{:S(2)}) collective-permute-start(f32[32,3072]{1,0:T(8,128)} %get-tuple-element.60), channel_id=1, source_target_pairs={{0,3},{1,2},{2,1},{3,0},{4,7},{5,6},{6,5},{7,4},{8,11},{9,10},{10,... | collective-permute-start | bytes 1179656 | tf_op jit(solution)/shard_map/ppermute | solution.py:179
  94.0 38.5 %collective-permute-start.8 = (f32[32,3072]{1,0:T(8,128)}, f32[32,3072]{1,0:T(8,128)S(1)}, u32[]{:S(2)}, u32[]{:S(2)}) collective-permute-start(f32[32,3072]{1,0:T(8,128)} %copy-done.4), channel_id=1, source_target_pairs={{0,1},{1,0},{2,3},{3,2},{4,5},{5,4},{6,7},{7,6},{8,9},{9,8},{10,11... | collective-permute-start | bytes 1179656 | tf_op jit(solution)/shard_map/ppermute | solution.py:187
  95.6 36.9 %collective-permute-start.10 = (f32[32,3072]{1,0:T(8,128)S(1)}, f32[32,3072]{1,0:T(8,128)S(1)}, u32[]{:S(2)}, u32[]{:S(2)}) collective-permute-start(f32[32,3072]{1,0:T(8,128)S(1)} %add.19), channel_id=1, source_target_pairs={{0,2},{1,3},{2,0},{3,1},{4,6},{5,7},{6,4},{7,5},{8,10},{9,11},{10,... | collective-permute-start | bytes 1179656 | tf_op jit(solution)/shard_map/ppermute | solution.py:189
  131.7 15.2 %collective-permute-start.31 = (f32[32,3072]{1,0:T(8,128)S(1)}, f32[32,3072]{1,0:T(8,128)S(1)}, u32[]{:S(2)}, u32[]{:S(2)}) collective-permute-start(f32[32,3072]{1,0:T(8,128)S(1)} %get-tuple-element.43), channel_id=1, source_target_pairs={{0,1},{1,0},{2,3},{3,2},{4,5},{5,4},{6,7},{7,6},{8,9},{9,8},{10,11... | collective-permute-start | bytes 1179656 | tf_op jit(solution)/shard_map/ppermute | solution.py:188
  140.9 13.2 %collective-permute-start.11 = (f32[32,3072]{1,0:T(8,128)S(1)}, f32[32,3072]{1,0:T(8,128)S(1)}, u32[]{:S(2)}, u32[]{:S(2)}) collective-permute-start(f32[32,3072]{1,0:T(8,128)S(1)} %get-tuple-element.34), channel_id=1, source_target_pairs={{4,0},{8,4},{12,8},{5,1},{9,5},{13,9},{6,2},{10,6},{14,10},{7,3},{... | collective-permute-start | bytes 1179656 | tf_op jit(solution)/shard_map/ppermute | solution.py:161
  142.2 13.1 %collective-permute-start.12 = (f32[32,3072]{1,0:T(8,128)S(1)}, f32[32,3072]{1,0:T(8,128)S(1)}, u32[]{:S(2)}, u32[]{:S(2)}) collective-permute-start(f32[32,3072]{1,0:T(8,128)S(1)} %get-tuple-element.34), channel_id=1, source_target_pairs={{0,4},{4,8},{8,12},{1,5},{5,9},{9,13},{2,6},{6,10},{10,14},{3,7},{... | collective-permute-start | bytes 1179656 | tf_op jit(solution)/shard_map/ppermute | solution.py:160
  155.3 23.1 %collective-permute-start.15 = (f32[32,3072]{1,0:T(8,128)S(1)}, f32[32,3072]{1,0:T(8,128)S(1)}, u32[]{:S(2)}, u32[]{:S(2)}) collective-permute-start(f32[32,3072]{1,0:T(8,128)S(1)} %broadcast_select_fusion.2), channel_id=1, source_target_pairs={{4,12},{8,0},{5,13},{9,1},{6,14},{10,2},{7,15},{11,3},{20,28},{24,... | collective-permute-start | bytes 1179656 | tf_op jit(solution)/shard_map/ppermute | solution.py:164
  156.6 21.8 %collective-permute-start.13 = (f32[32,3072]{1,0:T(8,128)S(1)}, f32[32,3072]{1,0:T(8,128)S(1)}, u32[]{:S(2)}, u32[]{:S(2)}) collective-permute-start(f32[32,3072]{1,0:T(8,128)S(1)} %collective-permute-done.12), channel_id=1, source_target_pairs={{4,8},{8,12},{5,9},{9,13},{6,10},{10,14},{7,11},{11,15},{20,24},{2... | collective-permute-start | bytes 1179656 | tf_op jit(solution)/shard_map/ppermute | solution.py:162
  157.3 21.1 %collective-permute-start.14 = (f32[32,3072]{1,0:T(8,128)S(1)}, f32[32,3072]{1,0:T(8,128)S(1)}, u32[]{:S(2)}, u32[]{:S(2)}) collective-permute-start(f32[32,3072]{1,0:T(8,128)S(1)} %collective-permute-done.11), channel_id=1, source_target_pairs={{4,0},{8,4},{5,1},{9,5},{6,2},{10,6},{7,3},{11,7},{20,16},{24,20},... | collective-permute-start | bytes 1179656 | tf_op jit(solution)/shard_map/ppermute | solution.py:163
  167.1 18.4 %collective-permute-start.33 = (f32[32,3072]{1,0:T(8,128)S(1)}, f32[32,3072]{1,0:T(8,128)S(1)}, u32[]{:S(2)}, u32[]{:S(2)}) collective-permute-start(f32[32,3072]{1,0:T(8,128)S(1)} %get-tuple-element.46), channel_id=1, source_target_pairs={{4,0},{8,4},{12,8},{5,1},{9,5},{13,9},{6,2},{10,6},{14,10},{7,3},{... | collective-permute-start | bytes 1179656 | tf_op jit(solution)/shard_map/ppermute | solution.py:161
  168.4 17.1 %collective-permute-start.34 = (f32[32,3072]{1,0:T(8,128)S(1)}, f32[32,3072]{1,0:T(8,128)S(1)}, u32[]{:S(2)}, u32[]{:S(2)}) collective-permute-start(f32[32,3072]{1,0:T(8,128)S(1)} %get-tuple-element.46), channel_id=1, source_target_pairs={{0,4},{4,8},{8,12},{1,5},{5,9},{9,13},{2,6},{6,10},{10,14},{3,7},{... | collective-permute-start | bytes 1179656 | tf_op jit(solution)/shard_map/ppermute | solution.py:160
  185.5 15.0 %collective-permute-start.37 = (f32[32,3072]{1,0:T(8,128)S(1)}, f32[32,3072]{1,0:T(8,128)S(1)}, u32[]{:S(2)}, u32[]{:S(2)}) collective-permute-start(f32[32,3072]{1,0:T(8,128)S(1)} %broadcast_select_fusion), channel_id=1, source_target_pairs={{4,12},{8,0},{5,13},{9,1},{6,14},{10,2},{7,15},{11,3},{20,28},{24,... | collective-permute-start | bytes 1179656 | tf_op jit(solution)/shard_map/ppermute | solution.py:164
  186.8 13.7 %collective-permute-start.35 = (f32[32,3072]{1,0:T(8,128)S(1)}, f32[32,3072]{1,0:T(8,128)S(1)}, u32[]{:S(2)}, u32[]{:S(2)}) collective-permute-start(f32[32,3072]{1,0:T(8,128)S(1)} %collective-permute-done.34), channel_id=1, source_target_pairs={{4,8},{8,12},{5,9},{9,13},{6,10},{10,14},{7,11},{11,15},{20,24},{2... | collective-permute-start | bytes 1179656 | tf_op jit(solution)/shard_map/ppermute | solution.py:162
  187.5 19.4 %collective-permute-start.36 = (f32[32,3072]{1,0:T(8,128)S(1)}, f32[32,3072]{1,0:T(8,128)S(1)}, u32[]{:S(2)}, u32[]{:S(2)}) collective-permute-start(f32[32,3072]{1,0:T(8,128)S(1)} %collective-permute-done.33), channel_id=1, source_target_pairs={{4,0},{8,4},{5,1},{9,5},{6,2},{10,6},{7,3},{11,7},{20,16},{24,20},... | collective-permute-start | bytes 1179656 | tf_op jit(solution)/shard_map/ppermute | solution.py:163
  189.0 19.9 %collective-permute-start.16 = (f32[32,3072]{1,0:T(8,128)S(1)}, f32[32,3072]{1,0:T(8,128)S(1)}, u32[]{:S(2)}, u32[]{:S(2)}) collective-permute-start(f32[32,3072]{1,0:T(8,128)S(1)} %get-tuple-element.69), channel_id=1, source_target_pairs={{0,1},{1,0},{2,3},{3,2},{4,5},{5,4},{6,7},{7,6},{8,9},{9,8},{10,11... | collective-permute-start | bytes 1179656 | tf_op jit(solution)/shard_map/ppermute | solution.py:179
  189.1 20.1 %collective-permute-start.17 = (f32[32,3072]{1,0:T(8,128)S(1)}, f32[32,3072]{1,0:T(8,128)S(1)}, u32[]{:S(2)}, u32[]{:S(2)}) collective-permute-start(f32[32,3072]{1,0:T(8,128)S(1)} %get-tuple-element.68), channel_id=1, source_target_pairs={{0,2},{1,3},{2,0},{3,1},{4,6},{5,7},{6,4},{7,5},{8,10},{9,11},{10,... | collective-permute-start | bytes 1179656 | tf_op jit(solution)/shard_map/ppermute | solution.py:179
  207.2 25.5 %collective-permute-start.38 = (f32[32,3072]{1,0:T(8,128)S(1)}, f32[32,3072]{1,0:T(8,128)S(1)}, u32[]{:S(2)}, u32[]{:S(2)}) collective-permute-start(f32[32,3072]{1,0:T(8,128)S(1)} %get-tuple-element.72), channel_id=1, source_target_pairs={{0,1},{1,0},{2,3},{3,2},{4,5},{5,4},{6,7},{7,6},{8,9},{9,8},{10,11... | collective-permute-start | bytes 1179656 | tf_op jit(solution)/shard_map/ppermute | solution.py:179
  207.3 25.5 %collective-permute-start.39 = (f32[32,3072]{1,0:T(8,128)S(1)}, f32[32,3072]{1,0:T(8,128)S(1)}, u32[]{:S(2)}, u32[]{:S(2)}) collective-permute-start(f32[32,3072]{1,0:T(8,128)S(1)} %get-tuple-element.71), channel_id=1, source_target_pairs={{0,2},{1,3},{2,0},{3,1},{4,6},{5,7},{6,4},{7,5},{8,10},{9,11},{10,... | collective-permute-start | bytes 1179656 | tf_op jit(solution)/shard_map/ppermute | solution.py:179
  208.9 23.9 %collective-permute-start.40 = (f32[32,3072]{1,0:T(8,128)S(1)}, f32[32,3072]{1,0:T(8,128)S(1)}, u32[]{:S(2)}, u32[]{:S(2)}) collective-permute-start(f32[32,3072]{1,0:T(8,128)S(1)} %get-tuple-element.58), channel_id=1, source_target_pairs={{0,3},{1,2},{2,1},{3,0},{4,7},{5,6},{6,5},{7,4},{8,11},{9,10},{10,... | collective-permute-start | bytes 1179656 | tf_op jit(solution)/shard_map/ppermute | solution.py:179
  232.6 21.4 %collective-permute-start.20 = (f32[32,3072]{1,0:T(8,128)S(1)}, f32[32,3072]{1,0:T(8,128)S(1)}, u32[]{:S(2)}, u32[]{:S(2)}) collective-permute-start(f32[32,3072]{1,0:T(8,128)S(1)} %get-tuple-element.38), channel_id=1, source_target_pairs={{0,1},{1,0},{2,3},{3,2},{4,5},{5,4},{6,7},{7,6},{8,9},{9,8},{10,11... | collective-permute-start | bytes 1179656 | tf_op jit(solution)/shard_map/ppermute | solution.py:188
  254.7 18.2 %collective-permute-start.41 = (f32[32,3072]{1,0:T(8,128)S(1)}, f32[32,3072]{1,0:T(8,128)S(1)}, u32[]{:S(2)}, u32[]{:S(2)}) collective-permute-start(f32[32,3072]{1,0:T(8,128)S(1)} %get-tuple-element.48), channel_id=1, source_target_pairs={{0,1},{1,0},{2,3},{3,2},{4,5},{5,4},{6,7},{7,6},{8,9},{9,8},{10,11... | collective-permute-start | bytes 1179656 | tf_op jit(solution)/shard_map/ppermute | solution.py:187
  255.3 18.7 %collective-permute-start.43 = (f32[32,3072]{1,0:T(8,128)S(1)}, f32[32,3072]{1,0:T(8,128)S(1)}, u32[]{:S(2)}, u32[]{:S(2)}) collective-permute-start(f32[32,3072]{1,0:T(8,128)S(1)} %add.22), channel_id=1, source_target_pairs={{0,2},{1,3},{2,0},{3,1},{4,6},{5,7},{6,4},{7,5},{8,10},{9,11},{10,... | collective-permute-start | bytes 1179656 | tf_op jit(solution)/shard_map/ppermute | solution.py:189
  (26 other events, 544.9 us)

commit v2 on v0

v2 whole, which is shorter than its diff:
```python
import jax
import jax.numpy as jnp
from jax import lax
from jax.experimental import pallas as pl
from jax.experimental.pallas import tpu as pltpu
from jax.sharding import PartitionSpec as P

NEWTON = 4
LANES = 128
PARTS = 2

coupling = 0.3
step_size = 0.5

f32 = jnp.float32
bf16 = jnp.bfloat16
NT = (((1,), (1,)), ((), ()))
CORNER = pl.BlockSpec((8, LANES), lambda *_: (0, 0))


def newton(value, state, stress, friction, volume):
    grow = jnp.exp(state)
    for turn in range(NEWTON):
        expo = jnp.exp(value)
        slipx = expo * grow
        square = 1.0 + slipx * slipx
        inverse = lax.rsqrt(square)
        fault_f = jnp.log(slipx + square * inverse)
        fault_d = slipx * inverse
        creep = grow * jnp.exp(value * (1.0 / 3.0))
        part_f = friction * jnp.where(volume, creep, fault_f)
        part_d = friction * jnp.where(volume, creep * (1.0 / 3.0), fault_d)
        value = value - jnp.clip((part_f + expo - stress) / (part_d + expo), -1.0, 1.0)
    return value


def step_kernel(scale, last, part, parts, base, value, state, sums, first, friction, region, partner):
    high, wide = base.shape
    tiles = wide // LANES
    terms = [a for group in sums for a in group] + ([first] if last else [])
    n_sum = len(terms)
    n_value = len(value)
    span = wide // parts
    width = wide // len(sums)
    each = len(sums[0])

    def body(*refs):
        base_ref, state_ref, value_refs = refs[0], refs[1], refs[2 : 2 + n_value]
        sum_refs = refs[2 + n_value : 2 + n_value + n_sum]
        friction_ref, region_ref, partner_ref = refs[2 + n_value + n_sum : 5 + n_value + n_sum]
        outs = refs[5 + n_value + n_sum : -1]
        raw = refs[-1]
        for k in range(len(sums)):
            cols = pl.ds(k * width, width)
            total = sum_refs[k * each][...]
            for ref in sum_refs[k * each + 1 : (k + 1) * each]:
                total = total + ref[pl.ds(0, high), :]
            if last:
                total = sum_refs[-1][:, cols] + total
            elif part == 0:
                outs[2][:, cols] = total
            raw[:, cols] = base_ref[:, cols] + scale * total

        def tiles_of(value_ref, begin, count):
            def tile(j, _):
                there = pl.ds(pl.multiple_of(j * LANES, LANES), LANES)
                cols = pl.ds(pl.multiple_of(part * span + begin + j * LANES, LANES), LANES)
                into = pl.ds(pl.multiple_of(begin + j * LANES, LANES), LANES)
                where = jnp.broadcast_to(partner_ref[:, cols], (8, LANES))
                lane = where % LANES
                block = where // LANES
                groups = high // 8
                moved = [jnp.zeros((8, LANES), f32) for _ in range(groups)]
                for k in range(tiles):
                    here = block == k
                    for g in range(groups):
                        got = jnp.take_along_axis(
                            raw[pl.ds(g * 8, 8), pl.ds(k * LANES, LANES)], lane, axis=1, mode="promise_in_bounds"
                        )
                        moved[g] = jnp.where(here, got, moved[g])
                fric = jnp.broadcast_to(friction_ref[:, cols], (8, LANES))
                volume = jnp.broadcast_to(region_ref[:, cols], (8, LANES)) == 1
                for g in range(groups):
                    rows = pl.ds(g * 8, 8)
                    own = raw[rows, cols]
                    stress = own + coupling * (moved[g] - own)
                    new = newton(value_ref[rows, there], state_ref[rows, cols], stress, fric, volume)
                    outs[0][rows, into] = new
                    outs[1][rows, into] = stress if last else jnp.exp(new)
                return 0

            lax.fori_loop(0, count // LANES, tile, 0)

        for k in range(n_value):
            tiles_of(value_refs[k], k * (span // n_value), span // n_value)

    full = jax.ShapeDtypeStruct((high, wide), f32)
    some = jax.ShapeDtypeStruct((high, span), f32)
    out_shape = [some, some] + ([full] if part == 0 and not last else [])
    return pl.pallas_call(
        body,
        grid=(1,),
        in_specs=[whole(a.shape) for a in (base, state, *value, *terms, friction, region, partner)],
        out_specs=[whole(a.shape) for a in out_shape],
        out_shape=out_shape,
        scratch_shapes=[pltpu.VMEM((high, wide), f32)],
        compiler_params=pltpu.CompilerParams(vmem_limit_bytes=24 << 20),
        cost_estimate=pl.CostEstimate(flops=200 * high * span, bytes_accessed=28 * high * wide, transcendentals=20 * high * span),
    )(base, state, *value, *terms, friction, region, partner)


def whole(shape):
    return pl.BlockSpec(shape, lambda *_: (0, 0), pipeline_mode=pl.Buffered(1))


def rates_times(halves, choice, kernel, part, parts, deps, tile=256):
    high, depth = halves[0][0][0].shape
    much = 4 * high
    rows = kernel.shape[0] // parts
    tile = min(tile, rows)
    steps = rows // tile
    flat = [
        pltpu.with_memory_space_constraint(ref, pltpu.HBM) for pairs in halves for pair in pairs for ref in pair
    ]

    def body(choice_ref, *refs):
        ins, kernel_ref = refs[:16], refs[16]
        own, across, other, stacked, landed, sem = refs[17 + len(deps) :]

        @pl.when(pl.program_id(0) == 0)
        def _():
            def fetch(k, ref):
                return pltpu.make_async_copy(ref, landed.at[k], sem.at[k])

            for k in range(8):

                @pl.when(choice_ref[0] == 0)
                def _():
                    fetch(k, ins[2 * k]).start()

                @pl.when(choice_ref[0] != 0)
                def _():
                    fetch(k, ins[2 * k + 1]).start()

            for k in range(8):
                fetch(k, ins[2 * k]).wait()
                cols = pl.ds((k // 4) * depth, depth)
                row = (k % 4) * high
                rates = landed[k]
                rough = rates.astype(bf16)
                stacked[pl.ds(row, high), cols] = rough
                stacked[pl.ds(much + row, high), cols] = (rates - rough.astype(f32)).astype(bf16)

        block = kernel_ref[...]
        upper = block.astype(bf16)
        lower = (block - upper.astype(f32)).astype(bf16)
        both = lax.dot_general(stacked[...], upper, NT, preferred_element_type=f32)
        rest = lax.dot_general(stacked[pl.ds(0, much), :], lower, NT, preferred_element_type=f32)
        total = both[:much] + both[much:] + rest
        own[...] = total[:high]
        across[...] = total[2 * high : 3 * high]
        other[pl.ds(0, high), :] = total[high : 2 * high]
        other[pl.ds(high, high), :] = total[3 * high :]

    one = pl.BlockSpec((high, tile), lambda i: (0, i))
    two = pl.BlockSpec((2 * high, tile), lambda i: (0, i))
    return pl.pallas_call(
        body,
        grid=(steps,),
        in_specs=[pl.BlockSpec(memory_space=pltpu.SMEM)]
        + [pl.BlockSpec(memory_space=pltpu.HBM)] * 16
        + [pl.BlockSpec((tile, 2 * depth), lambda i: (part * steps + i, 0))]
        + [CORNER] * len(deps),
        out_specs=[one, one, two],
        out_shape=[
            jax.ShapeDtypeStruct((high, rows), f32),
            jax.ShapeDtypeStruct((high, rows), f32),
            jax.ShapeDtypeStruct((2 * high, rows), f32),
        ],
        scratch_shapes=[
            pltpu.VMEM((2 * much, 2 * depth), bf16),
            pltpu.VMEM((8, high, depth), f32),
            pltpu.SemaphoreType.DMA((8,)),
        ],
        compiler_params=pltpu.CompilerParams(vmem_limit_bytes=24 << 20),
        cost_estimate=pl.CostEstimate(
            flops=24 * much * rows * depth, bytes_accessed=8 * rows * depth, transcendentals=0
        ),
    )(choice, *flat, pltpu.with_memory_space_constraint(kernel, pltpu.HBM), *deps)


OUTER = [(0, 1), (1, 0), (2, 3), (3, 2)]
INNER = [(0, 0), (1, 2), (2, 1), (3, 3)]
PLANE = ("col", "sub")
CORE = [(i, i ^ 1) for i in range(4)]
ACROSS = [(i, i ^ 2) for i in range(4)]


def where_sent():
    row = lax.axis_index("row")
    return (row == 1) | (row == 2), lax.axis_index("col") == row // 2


def spread_one(rates):
    return [lax.ppermute(rates, "row", OUTER), lax.ppermute(rates, "row", INNER)]


def spread_two(near):
    return [lax.ppermute(near[1], "row", OUTER), lax.ppermute(near[0], "row", INNER)]


def spread_three(two):
    return lax.ppermute(two[1], "row", OUTER)


def shift(first, second):
    beside = where_sent()[1]
    mine = jnp.where(beside, first, second)
    sent = jnp.where(beside, second, first)
    got = lax.ppermute(sent, PLANE, ACROSS)
    return [mine, lax.ppermute(mine, PLANE, CORE), got, lax.ppermute(got, PLANE, CORE)]


def spread(rates):
    middle = where_sent()[0]
    near = spread_one(rates)
    two = spread_two(near)
    far = spread_three(two)
    one = shift(rates, jnp.where(middle, near[1], two[0]))
    return list(zip(one, shift(near[0], jnp.where(middle, two[1], far))))


def first_block():
    row = lax.axis_index("row")
    beside = lax.axis_index("col") == row // 2
    near = jnp.where(beside, row, jnp.where(row < 2, 2, 1))
    return (near % 2 != lax.axis_index("sub")).astype(jnp.int32)[None]


def once(array, guard):
    return jnp.where(guard == guard, array, 0.0)


def spread_any(rates):
    blocks = lax.all_gather(rates, "row", axis=0)
    pieces = lax.all_to_all(blocks, ("col", "sub"), 0, 0)
    return [pieces[p] for p in range(pieces.shape[0])]


def sums_any(pieces, kernel):
    rates = jnp.concatenate(pieces, axis=0)
    partial = lax.dot_general(rates, kernel, NT, precision=lax.Precision.HIGH, preferred_element_type=f32)
    return [[lax.psum_scatter(partial, ("col", "sub"), scatter_dimension=0, tiled=True)]]


def solution(mesh):
    small = mesh.shape["row"] == 4 and mesh.shape["col"] == 2 and mesh.shape["sub"] == 2

    def plain(kernel, log_rate, state, base_stress, labels):
        sums = sums_any(spread_any(jnp.exp(log_rate)), kernel)
        value, rates, first = step_kernel(step_size, False, 0, 1, base_stress, [log_rate], state, sums, None, *labels)
        sums = sums_any(spread_any(rates), kernel)
        return tuple(step_kernel(0.5 * step_size, True, 0, 1, base_stress, [value], state, sums, first, *labels))

    def chunked(kernel, log_rate, state, base_stress, labels):
        wide = kernel.shape[1]
        choice = first_block()
        cuts = [slice(k * wide // 2, (k + 1) * wide // 2) for k in range(2)]

        def product(halves):
            sums = []
            for part in range(PARTS):
                deps = [sums[0][0], before] if sums else []
                own, across, other = rates_times(halves, choice, kernel, part, PARTS, deps)
                if sums:
                    stacked = other.reshape(2, *own.shape)
                    other = once(stacked, sums[0][2][None]).reshape(other.shape)
                swapped = lax.ppermute(other, PLANE, CORE)
                before = across + swapped[own.shape[0] :]
                sums.append([own, swapped, lax.ppermute(before, PLANE, ACROSS)])
            return sums

        rates = jnp.exp(log_rate)
        ready = spread(rates[:, cuts[0]])
        sums = product([ready, spread(rates[:, cuts[1]])])
        value, rates, first = step_kernel(
            step_size, False, 0, 2, base_stress, [log_rate[:, cuts[0]]], state, sums, None, *labels
        )
        ready = spread(rates)
        other_value, rates = step_kernel(
            step_size, False, 1, 2, base_stress, [log_rate[:, cuts[1]]], state, sums, None, *labels
        )
        sums = product([ready, spread(rates)])
        return tuple(
            step_kernel(
                0.5 * step_size, True, 0, 1, base_stress, [value, other_value], state, sums, first, *labels
            )
        )

    def per_device(kernel, log_rate, state, base_stress, friction, region, adjacency):
        partner = (adjacency - lax.axis_index("row") * kernel.shape[0])[None, :]
        labels = (friction[None, :], region[None, :], partner)
        return (chunked if small else plain)(kernel, log_rate, state, base_stress, labels)

    in_specs = (
        P("row", ("col", "sub")),
        P(("member", "col", "sub"), "row"),
        P(("member", "col", "sub"), "row"),
        P(("member", "col", "sub"), "row"),
        P("row"),
        P("row"),
        P("row"),
    )
    out_specs = (P(("member", "col", "sub"), "row"), P(("member", "col", "sub"), "row"))
    return jax.shard_map(per_device, mesh=mesh, in_specs=in_specs, out_specs=out_specs, check_vma=False)
```

time: 510 us -> 268 us (0.53)
  waiting for transfers between devices: 376 us -> 113 us
  Pallas kernels: 0 us -> 77 us
  matrix products: 73.4 us -> 0 us
  starting transfers between devices: 0.43 us -> 64.3 us
  other arithmetic: 22.4 us -> 3.8 us
  local copies, waits for them, and re-layouts: 22.6 us -> 6.72 us
  between operations: 14.2 us -> 1.41 us
    psum x2 -> x0, waiting for transfers between devices: 242 us -> none  [from_root(): return lax.psum(jnp.where(mine, shard, jnp.zeros_like(shard)), axis)]
    ppermute x0 -> x52, waiting for transfers between devices: none -> 113 us  [the longest x8 27.2 us: shift(): got = lax.ppermute(sent, PLANE, ACROSS)]
    pallas_call x0 -> x7, Pallas kernels: none -> 77 us  [the longest x4 55.4 us: rates_times(): pl.pallas_call(body, grid=(steps,), in_specs=[pl.BlockSpec(memory_space=p...]
    reduce_scatter x2 -> x0, waiting for transfers between devices: 73.5 us -> none  [total(): lax.psum_scatter(rates_times(columns, kernel), ('col', 'sub'), scatter_di...]
    dot_general x2 -> x0, matrix products: 73.4 us -> none  [rates_times(): lax.dot_general(rates, kernel, (((1,), (1,)), ((), ())), precision=lax.Pr...]
    ppermute x0 -> x52, starting transfers between devices: none -> 64.3 us  [the longest x4 21.7 us: spread_two(): lax.ppermute(near[1], 'row', OUTER)]
    all_gather x2 -> x0, waiting for transfers between devices: 60.6 us -> none  [spread(): whole = lax.all_gather(rates, ('col', 'sub'), axis=0, tiled=True)]
    gather x4 -> x0, local copies, waits for them, and re-layouts: 17.1 us -> none  [couple(): return stress + coupling * (jnp.take(stress, partner, axis=1) - stress)]
  transfers between devices with their start and end apart: 6 -> 52, of which waited for: 6 -> 22; matrix products, arithmetic and copies ran while one was open for 0% -> 1% of each run, Pallas kernels for 0% -> 12%
where the time goes in v2:
time: 268 us; the launch traced here: 267 us
  waiting for transfers between devices  113 us (42%)
  Pallas kernels  77 us (29%)
  starting transfers between devices  64.3 us (24%)
  local copies, waits for them, and re-layouts  6.72 us (3%)
  other arithmetic  3.8 us (1%)
    pallas_call x4, Pallas kernels, rates_times(): pl.pallas_call(body, grid=(steps,), in_specs=[pl.BlockSpec(memory_space=p...  55.4 us
    ppermute x8, waiting for transfers between devices, shift(): got = lax.ppermute(sent, PLANE, ACROSS)  27.2 us
    ppermute x4, waiting for transfers between devices, spread_three(): return lax.ppermute(two[1], 'row', OUTER)  24.2 us
    ppermute x4, starting transfers between devices, spread_two(): lax.ppermute(near[1], 'row', OUTER)  21.7 us
    pallas_call x3, Pallas kernels, step_kernel(): pl.pallas_call(body, grid=(1,), in_specs=[whole(a.shape) for a in (base,...  21.6 us
    ppermute x4, waiting for transfers between devices, product(): sums.append([own, swapped, lax.ppermute(before, PLANE, ACROSS)])  19.1 us
    ppermute x4, waiting for transfers between devices, spread_two(): lax.ppermute(near[1], 'row', OUTER)  19 us
    ppermute x4, waiting for transfers between devices, spread_one(): lax.ppermute(rates, 'row', OUTER)  11.9 us
  transfers between devices with their start and end apart: 52, of which 22 were waited for; matrix products, arithmetic and copies ran while one was open for 1% of the time, Pallas kernels for 12%

profile of v2, /device:TPU:0, one launch (start us, length us, event | category | flops | bytes accessed | tf_op | source)
XLA Modules:
  0.0 266.7 jit_solution(11007865382808609718)
XLA Ops:
  2.6 5.9 %collective-permute-start.13 = (f32[64,1536]{1,0:T(8,128)S(1)}, f32[64,1536]{1,0:T(8,128)S(1)}, u32[]{:S(2)}, u32[]{:S(2)}) collective-permute-start(f32[64,1536]{1,0:T(8,128)S(1)} %slice.33), channel_id=1, source_target_pairs={{0,4},{4,0},{8,12},{12,8},{1,5},{5,1},{9,13},{13,9},{2,6},{6,2},{1... | collective-permute-start | bytes 1179656 | tf_op jit(solution)/shard_map/ppermute | solution.py:205
  8.5 9.2 %collective-permute-start.12 = (f32[64,1536]{1,0:T(8,128)S(1)}, f32[64,1536]{1,0:T(8,128)S(1)}, u32[]{:S(2)}, u32[]{:S(2)}) collective-permute-start(f32[64,1536]{1,0:T(8,128)S(1)} %collective-permute-done.11), channel_id=1, source_target_pairs={{0,4},{4,0},{8,12},{12,8},{1,5},{5,1},{9,13},{13,9},{2,6},{6,2},{1... | collective-permute-start | bytes 1179656 | tf_op jit(solution)/shard_map/ppermute | solution.py:209
  18.4 7.6 %collective-permute-done.12 = f32[64,1536]{1,0:T(8,128)S(1)} collective-permute-done((f32[64,1536]{1,0:T(8,128)S(1)}, f32[64,1536]{1,0:T(8,128)S(1)}, u32[]{:S(2)}, u32[]{:S(2)}) %collective-permute-start.12) | collective-permute-done | bytes 393248 | tf_op jit(solution)/shard_map/ppermute | solution.py:209
  28.6 3.1 %collective-permute-start.15 = (f32[64,1536]{1,0:T(8,128)S(1)}, f32[64,1536]{1,0:T(8,128)S(1)}, u32[]{:S(2)}, u32[]{:S(2)}) collective-permute-start(f32[64,1536]{1,0:T(8,128)S(1)} %collective-permute-done.14), channel_id=1, source_target_pairs={{0,4},{4,0},{8,12},{12,8},{1,5},{5,1},{9,13},{13,9},{2,6},{6,2},{1... | collective-permute-start | bytes 1179656 | tf_op jit(solution)/shard_map/ppermute | solution.py:213
  33.2 5.0 %collective-permute-done.2 = f32[64,1536]{1,0:T(8,128)S(1)} collective-permute-done((f32[64,1536]{1,0:T(8,128)S(1)}, f32[64,1536]{1,0:T(8,128)S(1)}, u32[]{:S(2)}, u32[]{:S(2)}) %collective-permute-start.2) | collective-permute-done | bytes 393248 | tf_op jit(solution)/shard_map/ppermute | solution.py:205
  38.9 4.6 %collective-permute-start.1 = (f32[64,1536]{1,0:T(8,128)S(1)}, f32[64,1536]{1,0:T(8,128)S(1)}, u32[]{:S(2)}, u32[]{:S(2)}) collective-permute-start(f32[64,1536]{1,0:T(8,128)S(1)} %collective-permute-done), channel_id=1, source_target_pairs={{0,4},{4,0},{8,12},{12,8},{1,5},{5,1},{9,13},{13,9},{2,6},{6,2},{1... | collective-permute-start | bytes 1179656 | tf_op jit(solution)/shard_map/ppermute | solution.py:209
  43.5 3.1 %collective-permute-done.15 = f32[64,1536]{1,0:T(8,128)S(1)} collective-permute-done((f32[64,1536]{1,0:T(8,128)S(1)}, f32[64,1536]{1,0:T(8,128)S(1)}, u32[]{:S(2)}, u32[]{:S(2)}) %collective-permute-start.15) | collective-permute-done | bytes 393248 | tf_op jit(solution)/shard_map/ppermute | solution.py:213
  48.8 3.6 %collective-permute-done.1 = f32[64,1536]{1,0:T(8,128)S(1)} collective-permute-done((f32[64,1536]{1,0:T(8,128)S(1)}, f32[64,1536]{1,0:T(8,128)S(1)}, u32[]{:S(2)}, u32[]{:S(2)}) %collective-permute-start.1) | collective-permute-done | bytes 393248 | tf_op jit(solution)/shard_map/ppermute | solution.py:209
  54.1 6.7 %collective-permute-done.4 = f32[64,1536]{1,0:T(8,128)S(1)} collective-permute-done((f32[64,1536]{1,0:T(8,128)S(1)}, f32[64,1536]{1,0:T(8,128)S(1)}, u32[]{:S(2)}, u32[]{:S(2)}) %collective-permute-start.4) | collective-permute-done | bytes 393248 | tf_op jit(solution)/shard_map/ppermute | solution.py:213
  63.6 8.9 %collective-permute-done.7.refs_4_ = f32[64,1536]{1,0:T(8,128)S(1)} collective-permute-done((f32[64,1536]{1,0:T(8,128)S(1)}, f32[64,1536]{1,0:T(8,128)S(1)}, u32[]{:S(2)}, u32[]{:S(2)}) %collective-permute-start.7) | collective-permute-done | bytes 393248 | tf_op jit(solution)/shard_map/ppermute | solution.py:220
  72.5 4.3 %collective-permute-done.8.refs_5_ = f32[64,1536]{1,0:T(8,128)} collective-permute-done((f32[64,1536]{1,0:T(8,128)S(1)}, f32[64,1536]{1,0:T(8,128)}, u32[]{:S(2)}, u32[]{:S(2)}) %collective-permute-start.8) | collective-permute-done | bytes 393248 | tf_op jit(solution)/shard_map/ppermute | solution.py:220
  78.9 13.9 %shard_map.86 = (f32[64,1536]{1,0:T(8,128)S(1)}, f32[64,1536]{1,0:T(8,128)S(1)}, f32[128,1536]{1,0:T(8,128)S(1)}) custom-call(s32[1]{0:T(128)} %bitcast.choice_ref, f32[64,1536]{1,0:T(8,128)} %copy-done.14, f32[64,1536]{1,0:T(8,128)} %copy-done.16, f32[64,1536]{1,0:T(8,128)} %collective-permute-done.5.refs_2_, f32[64,1536]{1,0:T(8,128)} %collective-permute-done.6.refs_3_, ...), custom_call_target="tpu_custom_call" | custom-call | flops 14495514624 | bytes 18874368 | tf_op jit(solution)/shard_map/pallas_call | solution.py:167
  96.8 13.8 %shard_map.87 = (f32[64,1536]{1,0:T(8,128)S(1)}, f32[64,1536]{1,0:T(8,128)S(1)}, f32[128,1536]{1,0:T(8,128)S(1)}) custom-call(s32[1]{0:T(128)} %bitcast.choice_ref, f32[64,1536]{1,0:T(8,128)} %copy-done.14, f32[64,1536]{1,0:T(8,128)} %copy-done.16, f32[64,1536]{1,0:T(8,128)} %collective-permute-done.5.refs_2_, f32[64,1536]{1,0:T(8,128)} %collective-permute-done.6.refs_3_, ...), custom_call_target="tpu_custom_call" | custom-call | flops 14495514624 | bytes 18874368 | tf_op jit(solution)/shard_map/pallas_call | solution.py:167
  117.1 9.4 %collective-permute-done.25.refs_8_ = f32[64,1536]{1,0:T(8,128)S(1)} collective-permute-done((f32[64,1536]{1,0:T(8,128)S(1)}, f32[64,1536]{1,0:T(8,128)S(1)}, u32[]{:S(2)}, u32[]{:S(2)}) %collective-permute-start.25) | collective-permute-done | bytes 393248 | tf_op jit(solution)/shard_map/ppermute | solution.py:280
  129.3 5.3 %shard_map.89 = (f32[64,1536]{1,0:T(8,128)S(1)}, f32[64,1536]{1,0:T(8,128)S(1)}) custom-call(f32[64,3072]{1,0:T(8,128)S(1)} %copy-done, f32[64,3072]{1,0:T(8,128)S(1)} %copy-done.1, f32[64,1536]{1,0:T(8,128)S(1)} %get-tuple-element.52.refs_2_, f32[64,1536]{1,0:T(8,128)S(1)} %copy-done.3, f32[128,1536]{1,0:T(8,128)S(1)} %collective-permute-done.22.refs_4_, ...), custom_call_target="tpu_custom_call" | custom-call | flops 19660800 | bytes 5505024 | tf_op jit(solution)/shard_map/pallas_call | solution.py:100
  135.3 4.1 %collective-permute-start.39 = (f32[64,1536]{1,0:T(8,128)S(1)}, f32[64,1536]{1,0:T(8,128)S(1)}, u32[]{:S(2)}, u32[]{:S(2)}) collective-permute-start(f32[64,1536]{1,0:T(8,128)S(1)} %get-tuple-element.28), channel_id=1, source_target_pairs={{0,4},{4,0},{8,12},{12,8},{1,5},{5,1},{9,13},{13,9},{2,6},{6,2},{1... | collective-permute-start | bytes 1179656 | tf_op jit(solution)/shard_map/ppermute | solution.py:205
  140.1 5.2 %shard_map.88 = (f32[64,1536]{1,0:T(8,128)S(1)}, f32[64,1536]{1,0:T(8,128)S(1)}, f32[64,3072]{1,0:T(8,128)S(1)}) custom-call(f32[64,3072]{1,0:T(8,128)S(1)} %copy-done, f32[64,3072]{1,0:T(8,128)S(1)} %copy-done.1, f32[64,1536]{1,0:T(8,128)S(1)} %get-tuple-element.53.refs_2_, f32[64,1536]{1,0:T(8,128)S(1)} %copy-done.3, ...), custom_call_target="tpu_custom_call" | custom-call | flops 19660800 | bytes 5505024 | tf_op jit(solution)/shard_map/pallas_call | solution.py:100
  146.1 3.7 %collective-permute-start.38 = (f32[64,1536]{1,0:T(8,128)S(1)}, f32[64,1536]{1,0:T(8,128)S(1)}, u32[]{:S(2)}, u32[]{:S(2)}) collective-permute-start(f32[64,1536]{1,0:T(8,128)S(1)} %collective-permute-done.37), channel_id=1, source_target_pairs={{0,4},{4,0},{8,12},{12,8},{1,5},{5,1},{9,13},{13,9},{2,6},{6,2},{1... | collective-permute-start | bytes 1179656 | tf_op jit(solution)/shard_map/ppermute | solution.py:209
  150.5 6.9 %collective-permute-done.28 = f32[64,1536]{1,0:T(8,128)S(1)} collective-permute-done((f32[64,1536]{1,0:T(8,128)S(1)}, f32[64,1536]{1,0:T(8,128)S(1)}, u32[]{:S(2)}, u32[]{:S(2)}) %collective-permute-start.28) | collective-permute-done | bytes 393248 | tf_op jit(solution)/shard_map/ppermute | solution.py:205
  158.3 4.2 %collective-permute-start.27 = (f32[64,1536]{1,0:T(8,128)S(1)}, f32[64,1536]{1,0:T(8,128)S(1)}, u32[]{:S(2)}, u32[]{:S(2)}) collective-permute-start(f32[64,1536]{1,0:T(8,128)S(1)} %collective-permute-done.26), channel_id=1, source_target_pairs={{0,4},{4,0},{8,12},{12,8},{1,5},{5,1},{9,13},{13,9},{2,6},{6,2},{1... | collective-permute-start | bytes 1179656 | tf_op jit(solution)/shard_map/ppermute | solution.py:209
  162.5 3.4 %collective-permute-done.38 = f32[64,1536]{1,0:T(8,128)S(1)} collective-permute-done((f32[64,1536]{1,0:T(8,128)S(1)}, f32[64,1536]{1,0:T(8,128)S(1)}, u32[]{:S(2)}, u32[]{:S(2)}) %collective-permute-start.38) | collective-permute-done | bytes 393248 | tf_op jit(solution)/shard_map/ppermute | solution.py:209
  166.6 3.2 %collective-permute-start.41 = (f32[64,1536]{1,0:T(8,128)S(1)}, f32[64,1536]{1,0:T(8,128)S(1)}, u32[]{:S(2)}, u32[]{:S(2)}) collective-permute-start(f32[64,1536]{1,0:T(8,128)S(1)} %collective-permute-done.40), channel_id=1, source_target_pairs={{0,4},{4,0},{8,12},{12,8},{1,5},{5,1},{9,13},{13,9},{2,6},{6,2},{1... | collective-permute-start | bytes 1179656 | tf_op jit(solution)/shard_map/ppermute | solution.py:213
  169.8 4.5 %collective-permute-done.27 = f32[64,1536]{1,0:T(8,128)S(1)} collective-permute-done((f32[64,1536]{1,0:T(8,128)S(1)}, f32[64,1536]{1,0:T(8,128)S(1)}, u32[]{:S(2)}, u32[]{:S(2)}) %collective-permute-start.27) | collective-permute-done | bytes 393248 | tf_op jit(solution)/shard_map/ppermute | solution.py:209
  175.0 6.4 %collective-permute-done.41 = f32[64,1536]{1,0:T(8,128)S(1)} collective-permute-done((f32[64,1536]{1,0:T(8,128)S(1)}, f32[64,1536]{1,0:T(8,128)S(1)}, u32[]{:S(2)}, u32[]{:S(2)}) %collective-permute-start.41) | collective-permute-done | bytes 393248 | tf_op jit(solution)/shard_map/ppermute | solution.py:213
  183.2 8.0 %collective-permute-done.30 = f32[64,1536]{1,0:T(8,128)S(1)} collective-permute-done((f32[64,1536]{1,0:T(8,128)S(1)}, f32[64,1536]{1,0:T(8,128)S(1)}, u32[]{:S(2)}, u32[]{:S(2)}) %collective-permute-start.30) | collective-permute-done | bytes 393248 | tf_op jit(solution)/shard_map/ppermute | solution.py:213
  194.0 9.2 %collective-permute-done.45.refs_13_ = f32[64,1536]{1,0:T(8,128)S(1)} collective-permute-done((f32[64,1536]{1,0:T(8,128)S(1)}, f32[64,1536]{1,0:T(8,128)S(1)}, u32[]{:S(2)}, u32[]{:S(2)}) %collective-permute-start.45) | collective-permute-done | bytes 393248 | tf_op jit(solution)/shard_map/ppermute | solution.py:220
  203.8 4.8 %collective-permute-done.34.refs_5_ = f32[64,1536]{1,0:T(8,128)S(1)} collective-permute-done((f32[64,1536]{1,0:T(8,128)S(1)}, f32[64,1536]{1,0:T(8,128)S(1)}, u32[]{:S(2)}, u32[]{:S(2)}) %collective-permute-start.34) | collective-permute-done | bytes 393248 | tf_op jit(solution)/shard_map/ppermute | solution.py:220
  211.1 13.8 %shard_map.90 = (f32[64,1536]{1,0:T(8,128)S(1)}, f32[64,1536]{1,0:T(8,128)S(1)}, f32[128,1536]{1,0:T(8,128)S(1)}) custom-call(s32[1]{0:T(128)} %bitcast.choice_ref, f32[64,1536]{1,0:T(8,128)} %copy-done.15, f32[64,1536]{1,0:T(8,128)} %copy-done.18, f32[64,1536]{1,0:T(8,128)} %copy-done.28, f32[64,1536]{1,0:T(8,128)} %copy-done.32, f32[64,1536]{1,0:T(8,128)} %copy-done.27, ...), custom_call_target="tpu_custom_call" | custom-call | flops 14495514624 | bytes 18874368 | tf_op jit(solution)/shard_map/pallas_call | solution.py:167
  228.0 13.8 %shard_map.91 = (f32[64,1536]{1,0:T(8,128)S(1)}, f32[64,1536]{1,0:T(8,128)S(1)}, f32[128,1536]{1,0:T(8,128)S(1)}) custom-call(s32[1]{0:T(128)} %bitcast.choice_ref, f32[64,1536]{1,0:T(8,128)} %copy-done.15, f32[64,1536]{1,0:T(8,128)} %copy-done.18, f32[64,1536]{1,0:T(8,128)} %copy-done.28, f32[64,1536]{1,0:T(8,128)} %copy-done.32, f32[64,1536]{1,0:T(8,128)} %copy-done.27, ...), custom_call_target="tpu_custom_call" | custom-call | flops 14495514624 | bytes 18874368 | tf_op jit(solution)/shard_map/pallas_call | solution.py:167
  242.1 2.3 collective-permute-done.50.refs_8_
  246.0 9.7 %collective-permute-done.51.refs_9_ = f32[64,1536]{1,0:T(8,128)S(1)} collective-permute-done((f32[64,1536]{1,0:T(8,128)S(1)}, f32[64,1536]{1,0:T(8,128)S(1)}, u32[]{:S(2)}, u32[]{:S(2)}) %collective-permute-start.51) | collective-permute-done | bytes 393248 | tf_op jit(solution)/shard_map/ppermute | solution.py:280
  255.6 11.1 %shard_map.92 = (f32[64,3072]{1,0:T(8,128)}, f32[64,3072]{1,0:T(8,128)}) custom-call(f32[64,3072]{1,0:T(8,128)S(1)} %copy-done, f32[64,3072]{1,0:T(8,128)S(1)} %copy-done.1, f32[64,1536]{1,0:T(8,128)S(1)} %get-tuple-element.25.refs_2_, f32[64,1536]{1,0:T(8,128)S(1)} %get-tuple-element.26.refs_3_, f32[64,1536]{1,0:T(8,128)S(1)} %get-tuple-element.29.refs_17_.refs_4_, ...), custom_call_target="tpu_custom_call" | custom-call | flops 39321600 | bytes 5505024 | tf_op jit(solution)/shard_map/pallas_call | solution.py:100
  (173 shorter events, 46.6 us)
Async XLA Ops:
  2.6 15.1 %collective-permute-start.13 = (f32[64,1536]{1,0:T(8,128)S(1)}, f32[64,1536]{1,0:T(8,128)S(1)}, u32[]{:S(2)}, u32[]{:S(2)}) collective-permute-start(f32[64,1536]{1,0:T(8,128)S(1)} %slice.33), channel_id=1, source_target_pairs={{0,4},{4,0},{8,12},{12,8},{1,5},{5,1},{9,13},{13,9},{2,6},{6,2},{1... | collective-permute-start | bytes 1179656 | tf_op jit(solution)/shard_map/ppermute | solution.py:205
  8.5 17.4 %collective-permute-start.12 = (f32[64,1536]{1,0:T(8,128)S(1)}, f32[64,1536]{1,0:T(8,128)S(1)}, u32[]{:S(2)}, u32[]{:S(2)}) collective-permute-start(f32[64,1536]{1,0:T(8,128)S(1)} %collective-permute-done.11), channel_id=1, source_target_pairs={{0,4},{4,0},{8,12},{12,8},{1,5},{5,1},{9,13},{13,9},{2,6},{6,2},{1... | collective-permute-start | bytes 1179656 | tf_op jit(solution)/shard_map/ppermute | solution.py:209
  26.1 12.1 %collective-permute-start.2 = (f32[64,1536]{1,0:T(8,128)S(1)}, f32[64,1536]{1,0:T(8,128)S(1)}, u32[]{:S(2)}, u32[]{:S(2)}) collective-permute-start(f32[64,1536]{1,0:T(8,128)S(1)} %get-tuple-element.54), channel_id=1, source_target_pairs={{0,4},{4,0},{8,12},{12,8},{1,5},{5,1},{9,13},{13,9},{2,6},{6,2},{1... | collective-permute-start | bytes 1179656 | tf_op jit(solution)/shard_map/ppermute | solution.py:205
  28.6 18.0 %collective-permute-start.15 = (f32[64,1536]{1,0:T(8,128)S(1)}, f32[64,1536]{1,0:T(8,128)S(1)}, u32[]{:S(2)}, u32[]{:S(2)}) collective-permute-start(f32[64,1536]{1,0:T(8,128)S(1)} %collective-permute-done.14), channel_id=1, source_target_pairs={{0,4},{4,0},{8,12},{12,8},{1,5},{5,1},{9,13},{13,9},{2,6},{6,2},{1... | collective-permute-start | bytes 1179656 | tf_op jit(solution)/shard_map/ppermute | solution.py:213
  31.7 16.5 %collective-permute-start.18 = (f32[64,1536]{1,0:T(8,128)S(1)}, f32[64,1536]{1,0:T(8,128)S(1)}, u32[]{:S(2)}, u32[]{:S(2)}) collective-permute-start(f32[64,1536]{1,0:T(8,128)S(1)} %get-tuple-element.36), channel_id=1, source_target_pairs={{0,2},{1,3},{2,0},{3,1},{4,6},{5,7},{6,4},{7,5},{8,10},{9,11},{10,... | collective-permute-start | bytes 1179656 | tf_op jit(solution)/shard_map/ppermute | solution.py:220
  33.2 29.1 %collective-permute-start.16 = (f32[64,1536]{1,0:T(8,128)S(1)}, f32[64,1536]{1,0:T(8,128)S(1)}, u32[]{:S(2)}, u32[]{:S(2)}) collective-permute-start(f32[64,1536]{1,0:T(8,128)S(1)} %get-tuple-element.37.refs_8_), channel_id=1, source_target_pairs={{0,1},{1,0},{2,3},{3,2},{4,5},{5,4},{6,7},{7,6},{8,9},{9,8},{10,11... | collective-permute-start | bytes 1179656 | tf_op jit(solution)/shard_map/ppermute | solution.py:221
  38.9 13.4 %collective-permute-start.1 = (f32[64,1536]{1,0:T(8,128)S(1)}, f32[64,1536]{1,0:T(8,128)S(1)}, u32[]{:S(2)}, u32[]{:S(2)}) collective-permute-start(f32[64,1536]{1,0:T(8,128)S(1)} %collective-permute-done), channel_id=1, source_target_pairs={{0,4},{4,0},{8,12},{12,8},{1,5},{5,1},{9,13},{13,9},{2,6},{6,2},{1... | collective-permute-start | bytes 1179656 | tf_op jit(solution)/shard_map/ppermute | solution.py:209
  46.7 16.3 %collective-permute-start.19 = (f32[64,1536]{1,0:T(8,128)S(1)}, f32[64,1536]{1,0:T(8,128)S(1)}, u32[]{:S(2)}, u32[]{:S(2)}) collective-permute-start(f32[64,1536]{1,0:T(8,128)S(1)} %get-tuple-element.48), channel_id=1, source_target_pairs={{0,2},{1,3},{2,0},{3,1},{4,6},{5,7},{6,4},{7,5},{8,10},{9,11},{10,... | collective-permute-start | bytes 1179656 | tf_op jit(solution)/shard_map/ppermute | solution.py:220
  48.2 14.7 %collective-permute-start.17 = (f32[64,1536]{1,0:T(8,128)S(1)}, f32[64,1536]{1,0:T(8,128)S(1)}, u32[]{:S(2)}, u32[]{:S(2)}) collective-permute-start(f32[64,1536]{1,0:T(8,128)S(1)} %get-tuple-element.49.refs_9_), channel_id=1, source_target_pairs={{0,1},{1,0},{2,3},{3,2},{4,5},{5,4},{6,7},{7,6},{8,9},{9,8},{10,11... | collective-permute-start | bytes 1179656 | tf_op jit(solution)/shard_map/ppermute | solution.py:221
  48.3 15.2 %collective-permute-start.20 = (f32[64,1536]{1,0:T(8,128)S(1)}, f32[64,1536]{1,0:T(8,128)S(1)}, u32[]{:S(2)}, u32[]{:S(2)}) collective-permute-start(f32[64,1536]{1,0:T(8,128)S(1)} %collective-permute-done.18.refs_12_), channel_id=1, source_target_pairs={{0,1},{1,0},{2,3},{3,2},{4,5},{5,4},{6,7},{7,6},{8,9},{9,8},{10,11... | collective-permute-start | bytes 1179656 | tf_op jit(solution)/shard_map/ppermute | solution.py:221
  62.3 14.4 %collective-permute-start.8 = (f32[64,1536]{1,0:T(8,128)S(1)}, f32[64,1536]{1,0:T(8,128)}, u32[]{:S(2)}, u32[]{:S(2)}) collective-permute-start(f32[64,1536]{1,0:T(8,128)S(1)} %get-tuple-element.50), channel_id=1, source_target_pairs={{0,2},{1,3},{2,0},{3,1},{4,6},{5,7},{6,4},{7,5},{8,10},{9,11},{10,... | collective-permute-start | bytes 1179656 | tf_op jit(solution)/shard_map/ppermute | solution.py:220
  62.9 13.8 %collective-permute-start.5 = (f32[64,1536]{1,0:T(8,128)S(1)}, f32[64,1536]{1,0:T(8,128)}, u32[]{:S(2)}, u32[]{:S(2)}) collective-permute-start(f32[64,1536]{1,0:T(8,128)S(1)} %get-tuple-element.39.refs_0_), channel_id=1, source_target_pairs={{0,1},{1,0},{2,3},{3,2},{4,5},{5,4},{6,7},{7,6},{8,9},{9,8},{10,11... | collective-permute-start | bytes 1179656 | tf_op jit(solution)/shard_map/ppermute | solution.py:221
  63.0 13.8 %collective-permute-start.21 = (f32[64,1536]{1,0:T(8,128)S(1)}, f32[64,1536]{1,0:T(8,128)}, u32[]{:S(2)}, u32[]{:S(2)}) collective-permute-start(f32[64,1536]{1,0:T(8,128)S(1)} %collective-permute-done.19.refs_13_), channel_id=1, source_target_pairs={{0,1},{1,0},{2,3},{3,2},{4,5},{5,4},{6,7},{7,6},{8,9},{9,8},{10,11... | collective-permute-start | bytes 1179656 | tf_op jit(solution)/shard_map/ppermute | solution.py:221
  63.5 13.3 %collective-permute-start.6 = (f32[64,1536]{1,0:T(8,128)S(1)}, f32[64,1536]{1,0:T(8,128)}, u32[]{:S(2)}, u32[]{:S(2)}) collective-permute-start(f32[64,1536]{1,0:T(8,128)S(1)} %get-tuple-element.51.refs_1_), channel_id=1, source_target_pairs={{0,1},{1,0},{2,3},{3,2},{4,5},{5,4},{6,7},{7,6},{8,9},{9,8},{10,11... | collective-permute-start | bytes 1179656 | tf_op jit(solution)/shard_map/ppermute | solution.py:221
  95.2 15.4 %collective-permute-start.23 = (f32[64,1536]{1,0:T(8,128)S(1)}, f32[64,1536]{1,0:T(8,128)S(1)}, u32[]{:S(2)}, u32[]{:S(2)}) collective-permute-start(f32[64,1536]{1,0:T(8,128)S(1)} %slice_add_fusion.3.refs_18_), channel_id=1, source_target_pairs={{0,2},{1,3},{2,0},{3,1},{4,6},{5,7},{6,4},{7,5},{8,10},{9,11},{10,... | collective-permute-start | bytes 1179656 | tf_op jit(solution)/shard_map/ppermute | solution.py:280
  135.3 14.6 %collective-permute-start.39 = (f32[64,1536]{1,0:T(8,128)S(1)}, f32[64,1536]{1,0:T(8,128)S(1)}, u32[]{:S(2)}, u32[]{:S(2)}) collective-permute-start(f32[64,1536]{1,0:T(8,128)S(1)} %get-tuple-element.28), channel_id=1, source_target_pairs={{0,4},{4,0},{8,12},{12,8},{1,5},{5,1},{9,13},{13,9},{2,6},{6,2},{1... | collective-permute-start | bytes 1179656 | tf_op jit(solution)/shard_map/ppermute | solution.py:205
  145.3 12.1 %collective-permute-start.28 = (f32[64,1536]{1,0:T(8,128)S(1)}, f32[64,1536]{1,0:T(8,128)S(1)}, u32[]{:S(2)}, u32[]{:S(2)}) collective-permute-start(f32[64,1536]{1,0:T(8,128)S(1)} %get-tuple-element.27), channel_id=1, source_target_pairs={{0,4},{4,0},{8,12},{12,8},{1,5},{5,1},{9,13},{13,9},{2,6},{6,2},{1... | collective-permute-start | bytes 1179656 | tf_op jit(solution)/shard_map/ppermute | solution.py:205
  145.4 12.9 %collective-permute-start.26 = (f32[64,1536]{1,0:T(8,128)S(1)}, f32[64,1536]{1,0:T(8,128)S(1)}, u32[]{:S(2)}, u32[]{:S(2)}) collective-permute-start(f32[64,1536]{1,0:T(8,128)S(1)} %get-tuple-element.27), channel_id=1, source_target_pairs={{0,0},{4,8},{8,4},{12,12},{1,1},{5,9},{9,5},{13,13},{2,2},{6,10},{... | collective-permute-start | bytes 1179656 | tf_op jit(solution)/shard_map/ppermute | solution.py:205
  146.1 19.8 %collective-permute-start.38 = (f32[64,1536]{1,0:T(8,128)S(1)}, f32[64,1536]{1,0:T(8,128)S(1)}, u32[]{:S(2)}, u32[]{:S(2)}) collective-permute-start(f32[64,1536]{1,0:T(8,128)S(1)} %collective-permute-done.37), channel_id=1, source_target_pairs={{0,4},{4,0},{8,12},{12,8},{1,5},{5,1},{9,13},{13,9},{2,6},{6,2},{1... | collective-permute-start | bytes 1179656 | tf_op jit(solution)/shard_map/ppermute | solution.py:209
  149.8 16.7 %collective-permute-start.40 = (f32[64,1536]{1,0:T(8,128)S(1)}, f32[64,1536]{1,0:T(8,128)S(1)}, u32[]{:S(2)}, u32[]{:S(2)}) collective-permute-start(f32[64,1536]{1,0:T(8,128)S(1)} %collective-permute-done.39), channel_id=1, source_target_pairs={{0,0},{4,8},{8,4},{12,12},{1,1},{5,9},{9,5},{13,13},{2,2},{6,10},{... | collective-permute-start | bytes 1179656 | tf_op jit(solution)/shard_map/ppermute | solution.py:209
  157.4 17.6 %collective-permute-start.29 = (f32[64,1536]{1,0:T(8,128)S(1)}, f32[64,1536]{1,0:T(8,128)S(1)}, u32[]{:S(2)}, u32[]{:S(2)}) collective-permute-start(f32[64,1536]{1,0:T(8,128)S(1)} %collective-permute-done.28), channel_id=1, source_target_pairs={{0,0},{4,8},{8,4},{12,12},{1,1},{5,9},{9,5},{13,13},{2,2},{6,10},{... | collective-permute-start | bytes 1179656 | tf_op jit(solution)/shard_map/ppermute | solution.py:209
  158.3 16.0 %collective-permute-start.27 = (f32[64,1536]{1,0:T(8,128)S(1)}, f32[64,1536]{1,0:T(8,128)S(1)}, u32[]{:S(2)}, u32[]{:S(2)}) collective-permute-start(f32[64,1536]{1,0:T(8,128)S(1)} %collective-permute-done.26), channel_id=1, source_target_pairs={{0,4},{4,0},{8,12},{12,8},{1,5},{5,1},{9,13},{13,9},{2,6},{6,2},{1... | collective-permute-start | bytes 1179656 | tf_op jit(solution)/shard_map/ppermute | solution.py:209
  166.0 25.9 %collective-permute-start.44 = (f32[64,1536]{1,0:T(8,128)S(1)}, f32[64,1536]{1,0:T(8,128)S(1)}, u32[]{:S(2)}, u32[]{:S(2)}) collective-permute-start(f32[64,1536]{1,0:T(8,128)S(1)} %get-tuple-element.42), channel_id=1, source_target_pairs={{0,2},{1,3},{2,0},{3,1},{4,6},{5,7},{6,4},{7,5},{8,10},{9,11},{10,... | collective-permute-start | bytes 1179656 | tf_op jit(solution)/shard_map/ppermute | solution.py:220
  166.5 25.4 %collective-permute-start.42 = (f32[64,1536]{1,0:T(8,128)S(1)}, f32[64,1536]{1,0:T(8,128)S(1)}, u32[]{:S(2)}, u32[]{:S(2)}) collective-permute-start(f32[64,1536]{1,0:T(8,128)S(1)} %get-tuple-element.43.refs_8_), channel_id=1, source_target_pairs={{0,1},{1,0},{2,3},{3,2},{4,5},{5,4},{6,7},{7,6},{8,9},{9,8},{10,11... | collective-permute-start | bytes 1179656 | tf_op jit(solution)/shard_map/ppermute | solution.py:221
  166.6 14.8 %collective-permute-start.41 = (f32[64,1536]{1,0:T(8,128)S(1)}, f32[64,1536]{1,0:T(8,128)S(1)}, u32[]{:S(2)}, u32[]{:S(2)}) collective-permute-start(f32[64,1536]{1,0:T(8,128)S(1)} %collective-permute-done.40), channel_id=1, source_target_pairs={{0,4},{4,0},{8,12},{12,8},{1,5},{5,1},{9,13},{13,9},{2,6},{6,2},{1... | collective-permute-start | bytes 1179656 | tf_op jit(solution)/shard_map/ppermute | solution.py:213
  174.4 19.1 %collective-permute-start.33 = (f32[64,1536]{1,0:T(8,128)S(1)}, f32[64,1536]{1,0:T(8,128)S(1)}, u32[]{:S(2)}, u32[]{:S(2)}) collective-permute-start(f32[64,1536]{1,0:T(8,128)S(1)} %get-tuple-element.46), channel_id=1, source_target_pairs={{0,2},{1,3},{2,0},{3,1},{4,6},{5,7},{6,4},{7,5},{8,10},{9,11},{10,... | collective-permute-start | bytes 1179656 | tf_op jit(solution)/shard_map/ppermute | solution.py:220
  175.0 18.7 %collective-permute-start.31 = (f32[64,1536]{1,0:T(8,128)S(1)}, f32[64,1536]{1,0:T(8,128)S(1)}, u32[]{:S(2)}, u32[]{:S(2)}) collective-permute-start(f32[64,1536]{1,0:T(8,128)S(1)} %get-tuple-element.47.refs_0_), channel_id=1, source_target_pairs={{0,1},{1,0},{2,3},{3,2},{4,5},{5,4},{6,7},{7,6},{8,9},{9,8},{10,11... | collective-permute-start | bytes 1179656 | tf_op jit(solution)/shard_map/ppermute | solution.py:221
  191.2 12.1 %collective-permute-start.45 = (f32[64,1536]{1,0:T(8,128)S(1)}, f32[64,1536]{1,0:T(8,128)S(1)}, u32[]{:S(2)}, u32[]{:S(2)}) collective-permute-start(f32[64,1536]{1,0:T(8,128)S(1)} %get-tuple-element.40), channel_id=1, source_target_pairs={{0,2},{1,3},{2,0},{3,1},{4,6},{5,7},{6,4},{7,5},{8,10},{9,11},{10,... | collective-permute-start | bytes 1179656 | tf_op jit(solution)/shard_map/ppermute | solution.py:220
  192.0 16.6 %collective-permute-start.34 = (f32[64,1536]{1,0:T(8,128)S(1)}, f32[64,1536]{1,0:T(8,128)S(1)}, u32[]{:S(2)}, u32[]{:S(2)}) collective-permute-start(f32[64,1536]{1,0:T(8,128)S(1)} %get-tuple-element.44), channel_id=1, source_target_pairs={{0,2},{1,3},{2,0},{3,1},{4,6},{5,7},{6,4},{7,5},{8,10},{9,11},{10,... | collective-permute-start | bytes 1179656 | tf_op jit(solution)/shard_map/ppermute | solution.py:220
  193.5 15.0 %collective-permute-start.32 = (f32[64,1536]{1,0:T(8,128)S(1)}, f32[64,1536]{1,0:T(8,128)S(1)}, u32[]{:S(2)}, u32[]{:S(2)}) collective-permute-start(f32[64,1536]{1,0:T(8,128)S(1)} %get-tuple-element.45.refs_1_), channel_id=1, source_target_pairs={{0,1},{1,0},{2,3},{3,2},{4,5},{5,4},{6,7},{7,6},{8,9},{9,8},{10,11... | collective-permute-start | bytes 1179656 | tf_op jit(solution)/shard_map/ppermute | solution.py:221
  193.7 14.9 %collective-permute-start.46 = (f32[64,1536]{1,0:T(8,128)S(1)}, f32[64,1536]{1,0:T(8,128)S(1)}, u32[]{:S(2)}, u32[]{:S(2)}) collective-permute-start(f32[64,1536]{1,0:T(8,128)S(1)} %collective-permute-done.44.refs_12_), channel_id=1, source_target_pairs={{0,1},{1,0},{2,3},{3,2},{4,5},{5,4},{6,7},{7,6},{8,9},{9,8},{10,11... | collective-permute-start | bytes 1179656 | tf_op jit(solution)/shard_map/ppermute | solution.py:221
  227.4 14.5 %collective-permute-start.49 = (f32[64,1536]{1,0:T(8,128)S(1)}, f32[64,1536]{1,0:T(8,128)S(1)}, u32[]{:S(2)}, u32[]{:S(2)}) collective-permute-start(f32[64,1536]{1,0:T(8,128)S(1)} %slice_add_fusion.1.refs_18_), channel_id=1, source_target_pairs={{0,2},{1,3},{2,0},{3,1},{4,6},{5,7},{6,4},{7,5},{8,10},{9,11},{10,... | collective-permute-start | bytes 1179656 | tf_op jit(solution)/shard_map/ppermute | solution.py:280
  (57 other events, 742.7 us)

commit v3 on v2

--- a/solution.py
+++ b/solution.py
@@ -61,23 +61,33 @@
                 outs[2][:, cols] = total
             raw[:, cols] = base_ref[:, cols] + scale * total
 
+        groups = high // 8
+
+        def gather(cols):
+            where = jnp.broadcast_to(partner_ref[:, cols], (8, LANES))
+            lane = where % LANES
+            block = where // LANES
+            moved = [jnp.zeros((8, LANES), f32) for _ in range(groups)]
+            for k in range(tiles):
+                here = block == k
+                for g in range(groups):
+                    got = jnp.take_along_axis(
+                        raw[pl.ds(g * 8, 8), pl.ds(k * LANES, LANES)], lane, axis=1, mode="promise_in_bounds"
+                    )
+                    moved[g] = jnp.where(here, got, moved[g])
+            return moved
+
         def tiles_of(value_ref, begin, count):
-            def tile(j, _):
+            steps = count // LANES
+
+            def place(j):
+                return pl.ds(pl.multiple_of(part * span + begin + j * LANES, LANES), LANES)
+
+            def tile(j, moved):
+                cols = place(j)
                 there = pl.ds(pl.multiple_of(j * LANES, LANES), LANES)
-                cols = pl.ds(pl.multiple_of(part * span + begin + j * LANES, LANES), LANES)
                 into = pl.ds(pl.multiple_of(begin + j * LANES, LANES), LANES)
-                where = jnp.broadcast_to(partner_ref[:, cols], (8, LANES))
-                lane = where % LANES
-                block = where // LANES
-                groups = high // 8
-                moved = [jnp.zeros((8, LANES), f32) for _ in range(groups)]
-                for k in range(tiles):
-                    here = block == k
-                    for g in range(groups):
-                        got = jnp.take_along_axis(
-                            raw[pl.ds(g * 8, 8), pl.ds(k * LANES, LANES)], lane, axis=1, mode="promise_in_bounds"
-                        )
-                        moved[g] = jnp.where(here, got, moved[g])
+                later = gather(place(jnp.minimum(j + 1, steps - 1)))
                 fric = jnp.broadcast_to(friction_ref[:, cols], (8, LANES))
                 volume = jnp.broadcast_to(region_ref[:, cols], (8, LANES)) == 1
                 for g in range(groups):
@@ -87,9 +97,9 @@
                     new = newton(value_ref[rows, there], state_ref[rows, cols], stress, fric, volume)
                     outs[0][rows, into] = new
                     outs[1][rows, into] = stress if last else jnp.exp(new)
-                return 0
-
-            lax.fori_loop(0, count // LANES, tile, 0)
+                return later
+
+            lax.fori_loop(0, steps, tile, gather(place(0)))
 
         for k in range(n_value):
             tiles_of(value_refs[k], k * (span // n_value), span // n_value)

time: 268 us -> 263 us (0.981)
  Pallas kernels: 77 us -> 71.8 us
  waiting for transfers between devices: 113 us -> 116 us
    pallas_call x3, Pallas kernels: 21.6 us -> 16.4 us  [step_kernel(): pl.pallas_call(body, grid=(1,), in_specs=[whole(a.shape) for a in (base,...]
  transfers between devices with their start and end apart: 52 -> 52, of which waited for: 22 -> 23; matrix products, arithmetic and copies ran while one was open for 1% -> 1% of each run, Pallas kernels for 12% -> 12%
where the time goes in v3:
time: 263 us; the launch traced here: 262 us
  waiting for transfers between devices  116 us (44%)
  Pallas kernels  71.8 us (27%)
  starting transfers between devices  62.6 us (24%)
  local copies, waits for them, and re-layouts  6.72 us (3%)
  other arithmetic  3.8 us (1%)
    pallas_call x4, Pallas kernels, rates_times(): pl.pallas_call(body, grid=(steps,), in_specs=[pl.BlockSpec(memory_space=p...  55.4 us
    ppermute x8, waiting for transfers between devices, shift(): got = lax.ppermute(sent, PLANE, ACROSS)  26.8 us
    ppermute x4, waiting for transfers between devices, spread_three(): return lax.ppermute(two[1], 'row', OUTER)  23.5 us
    ppermute x4, starting transfers between devices, spread_two(): lax.ppermute(near[1], 'row', OUTER)  21.3 us
    ppermute x4, waiting for transfers between devices, spread_two(): lax.ppermute(near[1], 'row', OUTER)  20.6 us
    ppermute x4, waiting for transfers between devices, product(): sums.append([own, swapped, lax.ppermute(before, PLANE, ACROSS)])  19.4 us
    pallas_call x3, Pallas kernels, step_kernel(): pl.pallas_call(body, grid=(1,), in_specs=[whole(a.shape) for a in (base,...  16.4 us
    ppermute x4, waiting for transfers between devices, spread_one(): lax.ppermute(rates, 'row', OUTER)  13.6 us
  transfers between devices with their start and end apart: 52, of which 23 were waited for; matrix products, arithmetic and copies ran while one was open for 1% of the time, Pallas kernels for 12%

profile of v3, /device:TPU:0, one launch (start us, length us, event | category | flops | bytes accessed | tf_op | source)
XLA Modules:
  0.0 262.3 jit_solution(16741941239302117443)
XLA Ops:
  2.6 5.9 %collective-permute-start.13 = (f32[64,1536]{1,0:T(8,128)S(1)}, f32[64,1536]{1,0:T(8,128)S(1)}, u32[]{:S(2)}, u32[]{:S(2)}) collective-permute-start(f32[64,1536]{1,0:T(8,128)S(1)} %slice.33), channel_id=1, source_target_pairs={{0,4},{4,0},{8,12},{12,8},{1,5},{5,1},{9,13},{13,9},{2,6},{6,2},{1... | collective-permute-start | bytes 1179656 | tf_op jit(solution)/shard_map/ppermute | solution.py:215
  8.5 9.2 %collective-permute-start.12 = (f32[64,1536]{1,0:T(8,128)S(1)}, f32[64,1536]{1,0:T(8,128)S(1)}, u32[]{:S(2)}, u32[]{:S(2)}) collective-permute-start(f32[64,1536]{1,0:T(8,128)S(1)} %collective-permute-done.11), channel_id=1, source_target_pairs={{0,4},{4,0},{8,12},{12,8},{1,5},{5,1},{9,13},{13,9},{2,6},{6,2},{1... | collective-permute-start | bytes 1179656 | tf_op jit(solution)/shard_map/ppermute | solution.py:219
  18.4 7.6 %collective-permute-done.12 = f32[64,1536]{1,0:T(8,128)S(1)} collective-permute-done((f32[64,1536]{1,0:T(8,128)S(1)}, f32[64,1536]{1,0:T(8,128)S(1)}, u32[]{:S(2)}, u32[]{:S(2)}) %collective-permute-start.12) | collective-permute-done | bytes 393248 | tf_op jit(solution)/shard_map/ppermute | solution.py:219
  28.6 3.1 %collective-permute-start.15 = (f32[64,1536]{1,0:T(8,128)S(1)}, f32[64,1536]{1,0:T(8,128)S(1)}, u32[]{:S(2)}, u32[]{:S(2)}) collective-permute-start(f32[64,1536]{1,0:T(8,128)S(1)} %collective-permute-done.14), channel_id=1, source_target_pairs={{0,4},{4,0},{8,12},{12,8},{1,5},{5,1},{9,13},{13,9},{2,6},{6,2},{1... | collective-permute-start | bytes 1179656 | tf_op jit(solution)/shard_map/ppermute | solution.py:223
  33.2 5.0 %collective-permute-done.2 = f32[64,1536]{1,0:T(8,128)S(1)} collective-permute-done((f32[64,1536]{1,0:T(8,128)S(1)}, f32[64,1536]{1,0:T(8,128)S(1)}, u32[]{:S(2)}, u32[]{:S(2)}) %collective-permute-start.2) | collective-permute-done | bytes 393248 | tf_op jit(solution)/shard_map/ppermute | solution.py:215
  38.9 4.6 %collective-permute-start.1 = (f32[64,1536]{1,0:T(8,128)S(1)}, f32[64,1536]{1,0:T(8,128)S(1)}, u32[]{:S(2)}, u32[]{:S(2)}) collective-permute-start(f32[64,1536]{1,0:T(8,128)S(1)} %collective-permute-done), channel_id=1, source_target_pairs={{0,4},{4,0},{8,12},{12,8},{1,5},{5,1},{9,13},{13,9},{2,6},{6,2},{1... | collective-permute-start | bytes 1179656 | tf_op jit(solution)/shard_map/ppermute | solution.py:219
  43.5 3.1 %collective-permute-done.15 = f32[64,1536]{1,0:T(8,128)S(1)} collective-permute-done((f32[64,1536]{1,0:T(8,128)S(1)}, f32[64,1536]{1,0:T(8,128)S(1)}, u32[]{:S(2)}, u32[]{:S(2)}) %collective-permute-start.15) | collective-permute-done | bytes 393248 | tf_op jit(solution)/shard_map/ppermute | solution.py:223
  48.8 3.6 %collective-permute-done.1 = f32[64,1536]{1,0:T(8,128)S(1)} collective-permute-done((f32[64,1536]{1,0:T(8,128)S(1)}, f32[64,1536]{1,0:T(8,128)S(1)}, u32[]{:S(2)}, u32[]{:S(2)}) %collective-permute-start.1) | collective-permute-done | bytes 393248 | tf_op jit(solution)/shard_map/ppermute | solution.py:219
  54.1 6.7 %collective-permute-done.4 = f32[64,1536]{1,0:T(8,128)S(1)} collective-permute-done((f32[64,1536]{1,0:T(8,128)S(1)}, f32[64,1536]{1,0:T(8,128)S(1)}, u32[]{:S(2)}, u32[]{:S(2)}) %collective-permute-start.4) | collective-permute-done | bytes 393248 | tf_op jit(solution)/shard_map/ppermute | solution.py:223
  63.6 8.9 %collective-permute-done.7.refs_4_ = f32[64,1536]{1,0:T(8,128)S(1)} collective-permute-done((f32[64,1536]{1,0:T(8,128)S(1)}, f32[64,1536]{1,0:T(8,128)S(1)}, u32[]{:S(2)}, u32[]{:S(2)}) %collective-permute-start.7) | collective-permute-done | bytes 393248 | tf_op jit(solution)/shard_map/ppermute | solution.py:230
  72.5 4.3 %collective-permute-done.8.refs_5_ = f32[64,1536]{1,0:T(8,128)} collective-permute-done((f32[64,1536]{1,0:T(8,128)S(1)}, f32[64,1536]{1,0:T(8,128)}, u32[]{:S(2)}, u32[]{:S(2)}) %collective-permute-start.8) | collective-permute-done | bytes 393248 | tf_op jit(solution)/shard_map/ppermute | solution.py:230
  78.9 13.9 %shard_map.86 = (f32[64,1536]{1,0:T(8,128)S(1)}, f32[64,1536]{1,0:T(8,128)S(1)}, f32[128,1536]{1,0:T(8,128)S(1)}) custom-call(s32[1]{0:T(128)} %bitcast.choice_ref, f32[64,1536]{1,0:T(8,128)} %copy-done.14, f32[64,1536]{1,0:T(8,128)} %copy-done.16, f32[64,1536]{1,0:T(8,128)} %collective-permute-done.5.refs_2_, f32[64,1536]{1,0:T(8,128)} %collective-permute-done.6.refs_3_, ...), custom_call_target="tpu_custom_call" | custom-call | flops 14495514624 | bytes 18874368 | tf_op jit(solution)/shard_map/pallas_call | solution.py:177
  93.0 2.2 collective-permute-done.22.refs_4_
  96.8 13.8 %shard_map.87 = (f32[64,1536]{1,0:T(8,128)S(1)}, f32[64,1536]{1,0:T(8,128)S(1)}, f32[128,1536]{1,0:T(8,128)S(1)}) custom-call(s32[1]{0:T(128)} %bitcast.choice_ref, f32[64,1536]{1,0:T(8,128)} %copy-done.14, f32[64,1536]{1,0:T(8,128)} %copy-done.16, f32[64,1536]{1,0:T(8,128)} %collective-permute-done.5.refs_2_, f32[64,1536]{1,0:T(8,128)} %collective-permute-done.6.refs_3_, ...), custom_call_target="tpu_custom_call" | custom-call | flops 14495514624 | bytes 18874368 | tf_op jit(solution)/shard_map/pallas_call | solution.py:177
  117.1 9.4 %collective-permute-done.25.refs_8_ = f32[64,1536]{1,0:T(8,128)S(1)} collective-permute-done((f32[64,1536]{1,0:T(8,128)S(1)}, f32[64,1536]{1,0:T(8,128)S(1)}, u32[]{:S(2)}, u32[]{:S(2)}) %collective-permute-start.25) | collective-permute-done | bytes 393248 | tf_op jit(solution)/shard_map/ppermute | solution.py:290
  129.3 3.9 %shard_map.89 = (f32[64,1536]{1,0:T(8,128)S(1)}, f32[64,1536]{1,0:T(8,128)S(1)}) custom-call(f32[64,3072]{1,0:T(8,128)S(1)} %copy-done, f32[64,3072]{1,0:T(8,128)S(1)} %copy-done.1, f32[64,1536]{1,0:T(8,128)S(1)} %get-tuple-element.52.refs_2_, f32[64,1536]{1,0:T(8,128)S(1)} %copy-done.3, f32[128,1536]{1,0:T(8,128)S(1)} %collective-permute-done.22.refs_4_, ...), custom_call_target="tpu_custom_call" | custom-call | flops 19660800 | bytes 5505024 | tf_op jit(solution)/shard_map/pallas_call | solution.py:110
  133.9 4.1 %collective-permute-start.39 = (f32[64,1536]{1,0:T(8,128)S(1)}, f32[64,1536]{1,0:T(8,128)S(1)}, u32[]{:S(2)}, u32[]{:S(2)}) collective-permute-start(f32[64,1536]{1,0:T(8,128)S(1)} %get-tuple-element.28), channel_id=1, source_target_pairs={{0,4},{4,0},{8,12},{12,8},{1,5},{5,1},{9,13},{13,9},{2,6},{6,2},{1... | collective-permute-start | bytes 1179656 | tf_op jit(solution)/shard_map/ppermute | solution.py:215
  138.7 3.9 %shard_map.88 = (f32[64,1536]{1,0:T(8,128)S(1)}, f32[64,1536]{1,0:T(8,128)S(1)}, f32[64,3072]{1,0:T(8,128)S(1)}) custom-call(f32[64,3072]{1,0:T(8,128)S(1)} %copy-done, f32[64,3072]{1,0:T(8,128)S(1)} %copy-done.1, f32[64,1536]{1,0:T(8,128)S(1)} %get-tuple-element.53.refs_2_, f32[64,1536]{1,0:T(8,128)S(1)} %copy-done.3, ...), custom_call_target="tpu_custom_call" | custom-call | flops 19660800 | bytes 5505024 | tf_op jit(solution)/shard_map/pallas_call | solution.py:110
  143.4 3.7 %collective-permute-start.38 = (f32[64,1536]{1,0:T(8,128)S(1)}, f32[64,1536]{1,0:T(8,128)S(1)}, u32[]{:S(2)}, u32[]{:S(2)}) collective-permute-start(f32[64,1536]{1,0:T(8,128)S(1)} %collective-permute-done.37), channel_id=1, source_target_pairs={{0,4},{4,0},{8,12},{12,8},{1,5},{5,1},{9,13},{13,9},{2,6},{6,2},{1... | collective-permute-start | bytes 1179656 | tf_op jit(solution)/shard_map/ppermute | solution.py:219
  148.7 7.7 %collective-permute-done.28 = f32[64,1536]{1,0:T(8,128)S(1)} collective-permute-done((f32[64,1536]{1,0:T(8,128)S(1)}, f32[64,1536]{1,0:T(8,128)S(1)}, u32[]{:S(2)}, u32[]{:S(2)}) %collective-permute-start.28) | collective-permute-done | bytes 393248 | tf_op jit(solution)/shard_map/ppermute | solution.py:215
  157.3 3.8 %collective-permute-start.27 = (f32[64,1536]{1,0:T(8,128)S(1)}, f32[64,1536]{1,0:T(8,128)S(1)}, u32[]{:S(2)}, u32[]{:S(2)}) collective-permute-start(f32[64,1536]{1,0:T(8,128)S(1)} %collective-permute-done.26), channel_id=1, source_target_pairs={{0,4},{4,0},{8,12},{12,8},{1,5},{5,1},{9,13},{13,9},{2,6},{6,2},{1... | collective-permute-start | bytes 1179656 | tf_op jit(solution)/shard_map/ppermute | solution.py:219
  161.1 3.8 %collective-permute-done.38 = f32[64,1536]{1,0:T(8,128)S(1)} collective-permute-done((f32[64,1536]{1,0:T(8,128)S(1)}, f32[64,1536]{1,0:T(8,128)S(1)}, u32[]{:S(2)}, u32[]{:S(2)}) %collective-permute-start.38) | collective-permute-done | bytes 393248 | tf_op jit(solution)/shard_map/ppermute | solution.py:219
  167.6 5.7 %collective-permute-done.27 = f32[64,1536]{1,0:T(8,128)S(1)} collective-permute-done((f32[64,1536]{1,0:T(8,128)S(1)}, f32[64,1536]{1,0:T(8,128)S(1)}, u32[]{:S(2)}, u32[]{:S(2)}) %collective-permute-start.27) | collective-permute-done | bytes 393248 | tf_op jit(solution)/shard_map/ppermute | solution.py:219
  173.9 6.1 %collective-permute-done.41 = f32[64,1536]{1,0:T(8,128)S(1)} collective-permute-done((f32[64,1536]{1,0:T(8,128)S(1)}, f32[64,1536]{1,0:T(8,128)S(1)}, u32[]{:S(2)}, u32[]{:S(2)}) %collective-permute-start.41) | collective-permute-done | bytes 393248 | tf_op jit(solution)/shard_map/ppermute | solution.py:223
  181.8 7.6 %collective-permute-done.30 = f32[64,1536]{1,0:T(8,128)S(1)} collective-permute-done((f32[64,1536]{1,0:T(8,128)S(1)}, f32[64,1536]{1,0:T(8,128)S(1)}, u32[]{:S(2)}, u32[]{:S(2)}) %collective-permute-start.30) | collective-permute-done | bytes 393248 | tf_op jit(solution)/shard_map/ppermute | solution.py:223
  192.2 9.2 %collective-permute-done.45.refs_13_ = f32[64,1536]{1,0:T(8,128)S(1)} collective-permute-done((f32[64,1536]{1,0:T(8,128)S(1)}, f32[64,1536]{1,0:T(8,128)S(1)}, u32[]{:S(2)}, u32[]{:S(2)}) %collective-permute-start.45) | collective-permute-done | bytes 393248 | tf_op jit(solution)/shard_map/ppermute | solution.py:230
  202.0 4.3 %collective-permute-done.34.refs_5_ = f32[64,1536]{1,0:T(8,128)S(1)} collective-permute-done((f32[64,1536]{1,0:T(8,128)S(1)}, f32[64,1536]{1,0:T(8,128)S(1)}, u32[]{:S(2)}, u32[]{:S(2)}) %collective-permute-start.34) | collective-permute-done | bytes 393248 | tf_op jit(solution)/shard_map/ppermute | solution.py:230
  208.9 13.8 %shard_map.90 = (f32[64,1536]{1,0:T(8,128)S(1)}, f32[64,1536]{1,0:T(8,128)S(1)}, f32[128,1536]{1,0:T(8,128)S(1)}) custom-call(s32[1]{0:T(128)} %bitcast.choice_ref, f32[64,1536]{1,0:T(8,128)} %copy-done.15, f32[64,1536]{1,0:T(8,128)} %copy-done.18, f32[64,1536]{1,0:T(8,128)} %copy-done.28, f32[64,1536]{1,0:T(8,128)} %copy-done.32, f32[64,1536]{1,0:T(8,128)} %copy-done.27, ...), custom_call_target="tpu_custom_call" | custom-call | flops 14495514624 | bytes 18874368 | tf_op jit(solution)/shard_map/pallas_call | solution.py:177
  226.0 13.8 %shard_map.91 = (f32[64,1536]{1,0:T(8,128)S(1)}, f32[64,1536]{1,0:T(8,128)S(1)}, f32[128,1536]{1,0:T(8,128)S(1)}) custom-call(s32[1]{0:T(128)} %bitcast.choice_ref, f32[64,1536]{1,0:T(8,128)} %copy-done.15, f32[64,1536]{1,0:T(8,128)} %copy-done.18, f32[64,1536]{1,0:T(8,128)} %copy-done.28, f32[64,1536]{1,0:T(8,128)} %copy-done.32, f32[64,1536]{1,0:T(8,128)} %copy-done.27, ...), custom_call_target="tpu_custom_call" | custom-call | flops 14495514624 | bytes 18874368 | tf_op jit(solution)/shard_map/pallas_call | solution.py:177
  240.1 2.3 collective-permute-done.50.refs_8_
  243.8 9.9 %collective-permute-done.51.refs_9_ = f32[64,1536]{1,0:T(8,128)S(1)} collective-permute-done((f32[64,1536]{1,0:T(8,128)S(1)}, f32[64,1536]{1,0:T(8,128)S(1)}, u32[]{:S(2)}, u32[]{:S(2)}) %collective-permute-start.51) | collective-permute-done | bytes 393248 | tf_op jit(solution)/shard_map/ppermute | solution.py:290
  253.7 8.7 %shard_map.92 = (f32[64,3072]{1,0:T(8,128)}, f32[64,3072]{1,0:T(8,128)}) custom-call(f32[64,3072]{1,0:T(8,128)S(1)} %copy-done, f32[64,3072]{1,0:T(8,128)S(1)} %copy-done.1, f32[64,1536]{1,0:T(8,128)S(1)} %get-tuple-element.25.refs_2_, f32[64,1536]{1,0:T(8,128)S(1)} %get-tuple-element.26.refs_3_, f32[64,1536]{1,0:T(8,128)S(1)} %get-tuple-element.29.refs_17_.refs_4_, ...), custom_call_target="tpu_custom_call" | custom-call | flops 39321600 | bytes 5505024 | tf_op jit(solution)/shard_map/pallas_call | solution.py:110
  (173 shorter events, 47.3 us)
Async XLA Ops:
  2.6 15.1 %collective-permute-start.13 = (f32[64,1536]{1,0:T(8,128)S(1)}, f32[64,1536]{1,0:T(8,128)S(1)}, u32[]{:S(2)}, u32[]{:S(2)}) collective-permute-start(f32[64,1536]{1,0:T(8,128)S(1)} %slice.33), channel_id=1, source_target_pairs={{0,4},{4,0},{8,12},{12,8},{1,5},{5,1},{9,13},{13,9},{2,6},{6,2},{1... | collective-permute-start | bytes 1179656 | tf_op jit(solution)/shard_map/ppermute | solution.py:215
  8.5 17.4 %collective-permute-start.12 = (f32[64,1536]{1,0:T(8,128)S(1)}, f32[64,1536]{1,0:T(8,128)S(1)}, u32[]{:S(2)}, u32[]{:S(2)}) collective-permute-start(f32[64,1536]{1,0:T(8,128)S(1)} %collective-permute-done.11), channel_id=1, source_target_pairs={{0,4},{4,0},{8,12},{12,8},{1,5},{5,1},{9,13},{13,9},{2,6},{6,2},{1... | collective-permute-start | bytes 1179656 | tf_op jit(solution)/shard_map/ppermute | solution.py:219
  26.1 12.1 %collective-permute-start.2 = (f32[64,1536]{1,0:T(8,128)S(1)}, f32[64,1536]{1,0:T(8,128)S(1)}, u32[]{:S(2)}, u32[]{:S(2)}) collective-permute-start(f32[64,1536]{1,0:T(8,128)S(1)} %get-tuple-element.54), channel_id=1, source_target_pairs={{0,4},{4,0},{8,12},{12,8},{1,5},{5,1},{9,13},{13,9},{2,6},{6,2},{1... | collective-permute-start | bytes 1179656 | tf_op jit(solution)/shard_map/ppermute | solution.py:215
  28.6 18.0 %collective-permute-start.15 = (f32[64,1536]{1,0:T(8,128)S(1)}, f32[64,1536]{1,0:T(8,128)S(1)}, u32[]{:S(2)}, u32[]{:S(2)}) collective-permute-start(f32[64,1536]{1,0:T(8,128)S(1)} %collective-permute-done.14), channel_id=1, source_target_pairs={{0,4},{4,0},{8,12},{12,8},{1,5},{5,1},{9,13},{13,9},{2,6},{6,2},{1... | collective-permute-start | bytes 1179656 | tf_op jit(solution)/shard_map/ppermute | solution.py:223
  31.7 16.5 %collective-permute-start.18 = (f32[64,1536]{1,0:T(8,128)S(1)}, f32[64,1536]{1,0:T(8,128)S(1)}, u32[]{:S(2)}, u32[]{:S(2)}) collective-permute-start(f32[64,1536]{1,0:T(8,128)S(1)} %get-tuple-element.36), channel_id=1, source_target_pairs={{0,2},{1,3},{2,0},{3,1},{4,6},{5,7},{6,4},{7,5},{8,10},{9,11},{10,... | collective-permute-start | bytes 1179656 | tf_op jit(solution)/shard_map/ppermute | solution.py:230
  33.2 29.1 %collective-permute-start.16 = (f32[64,1536]{1,0:T(8,128)S(1)}, f32[64,1536]{1,0:T(8,128)S(1)}, u32[]{:S(2)}, u32[]{:S(2)}) collective-permute-start(f32[64,1536]{1,0:T(8,128)S(1)} %get-tuple-element.37.refs_8_), channel_id=1, source_target_pairs={{0,1},{1,0},{2,3},{3,2},{4,5},{5,4},{6,7},{7,6},{8,9},{9,8},{10,11... | collective-permute-start | bytes 1179656 | tf_op jit(solution)/shard_map/ppermute | solution.py:231
  38.9 13.4 %collective-permute-start.1 = (f32[64,1536]{1,0:T(8,128)S(1)}, f32[64,1536]{1,0:T(8,128)S(1)}, u32[]{:S(2)}, u32[]{:S(2)}) collective-permute-start(f32[64,1536]{1,0:T(8,128)S(1)} %collective-permute-done), channel_id=1, source_target_pairs={{0,4},{4,0},{8,12},{12,8},{1,5},{5,1},{9,13},{13,9},{2,6},{6,2},{1... | collective-permute-start | bytes 1179656 | tf_op jit(solution)/shard_map/ppermute | solution.py:219
  46.7 16.3 %collective-permute-start.19 = (f32[64,1536]{1,0:T(8,128)S(1)}, f32[64,1536]{1,0:T(8,128)S(1)}, u32[]{:S(2)}, u32[]{:S(2)}) collective-permute-start(f32[64,1536]{1,0:T(8,128)S(1)} %get-tuple-element.48), channel_id=1, source_target_pairs={{0,2},{1,3},{2,0},{3,1},{4,6},{5,7},{6,4},{7,5},{8,10},{9,11},{10,... | collective-permute-start | bytes 1179656 | tf_op jit(solution)/shard_map/ppermute | solution.py:230
  48.2 14.7 %collective-permute-start.17 = (f32[64,1536]{1,0:T(8,128)S(1)}, f32[64,1536]{1,0:T(8,128)S(1)}, u32[]{:S(2)}, u32[]{:S(2)}) collective-permute-start(f32[64,1536]{1,0:T(8,128)S(1)} %get-tuple-element.49.refs_9_), channel_id=1, source_target_pairs={{0,1},{1,0},{2,3},{3,2},{4,5},{5,4},{6,7},{7,6},{8,9},{9,8},{10,11... | collective-permute-start | bytes 1179656 | tf_op jit(solution)/shard_map/ppermute | solution.py:231
  48.3 15.2 %collective-permute-start.20 = (f32[64,1536]{1,0:T(8,128)S(1)}, f32[64,1536]{1,0:T(8,128)S(1)}, u32[]{:S(2)}, u32[]{:S(2)}) collective-permute-start(f32[64,1536]{1,0:T(8,128)S(1)} %collective-permute-done.18.refs_12_), channel_id=1, source_target_pairs={{0,1},{1,0},{2,3},{3,2},{4,5},{5,4},{6,7},{7,6},{8,9},{9,8},{10,11... | collective-permute-start | bytes 1179656 | tf_op jit(solution)/shard_map/ppermute | solution.py:231
  62.3 14.4 %collective-permute-start.8 = (f32[64,1536]{1,0:T(8,128)S(1)}, f32[64,1536]{1,0:T(8,128)}, u32[]{:S(2)}, u32[]{:S(2)}) collective-permute-start(f32[64,1536]{1,0:T(8,128)S(1)} %get-tuple-element.50), channel_id=1, source_target_pairs={{0,2},{1,3},{2,0},{3,1},{4,6},{5,7},{6,4},{7,5},{8,10},{9,11},{10,... | collective-permute-start | bytes 1179656 | tf_op jit(solution)/shard_map/ppermute | solution.py:230
  62.9 13.8 %collective-permute-start.5 = (f32[64,1536]{1,0:T(8,128)S(1)}, f32[64,1536]{1,0:T(8,128)}, u32[]{:S(2)}, u32[]{:S(2)}) collective-permute-start(f32[64,1536]{1,0:T(8,128)S(1)} %get-tuple-element.39.refs_0_), channel_id=1, source_target_pairs={{0,1},{1,0},{2,3},{3,2},{4,5},{5,4},{6,7},{7,6},{8,9},{9,8},{10,11... | collective-permute-start | bytes 1179656 | tf_op jit(solution)/shard_map/ppermute | solution.py:231
  63.0 13.8 %collective-permute-start.21 = (f32[64,1536]{1,0:T(8,128)S(1)}, f32[64,1536]{1,0:T(8,128)}, u32[]{:S(2)}, u32[]{:S(2)}) collective-permute-start(f32[64,1536]{1,0:T(8,128)S(1)} %collective-permute-done.19.refs_13_), channel_id=1, source_target_pairs={{0,1},{1,0},{2,3},{3,2},{4,5},{5,4},{6,7},{7,6},{8,9},{9,8},{10,11... | collective-permute-start | bytes 1179656 | tf_op jit(solution)/shard_map/ppermute | solution.py:231
  63.5 13.3 %collective-permute-start.6 = (f32[64,1536]{1,0:T(8,128)S(1)}, f32[64,1536]{1,0:T(8,128)}, u32[]{:S(2)}, u32[]{:S(2)}) collective-permute-start(f32[64,1536]{1,0:T(8,128)S(1)} %get-tuple-element.51.refs_1_), channel_id=1, source_target_pairs={{0,1},{1,0},{2,3},{3,2},{4,5},{5,4},{6,7},{7,6},{8,9},{9,8},{10,11... | collective-permute-start | bytes 1179656 | tf_op jit(solution)/shard_map/ppermute | solution.py:231
  95.2 15.4 %collective-permute-start.23 = (f32[64,1536]{1,0:T(8,128)S(1)}, f32[64,1536]{1,0:T(8,128)S(1)}, u32[]{:S(2)}, u32[]{:S(2)}) collective-permute-start(f32[64,1536]{1,0:T(8,128)S(1)} %slice_add_fusion.3.refs_18_), channel_id=1, source_target_pairs={{0,2},{1,3},{2,0},{3,1},{4,6},{5,7},{6,4},{7,5},{8,10},{9,11},{10,... | collective-permute-start | bytes 1179656 | tf_op jit(solution)/shard_map/ppermute | solution.py:290
  133.9 14.1 %collective-permute-start.39 = (f32[64,1536]{1,0:T(8,128)S(1)}, f32[64,1536]{1,0:T(8,128)S(1)}, u32[]{:S(2)}, u32[]{:S(2)}) collective-permute-start(f32[64,1536]{1,0:T(8,128)S(1)} %get-tuple-element.28), channel_id=1, source_target_pairs={{0,4},{4,0},{8,12},{12,8},{1,5},{5,1},{9,13},{13,9},{2,6},{6,2},{1... | collective-permute-start | bytes 1179656 | tf_op jit(solution)/shard_map/ppermute | solution.py:215
  142.6 13.9 %collective-permute-start.28 = (f32[64,1536]{1,0:T(8,128)S(1)}, f32[64,1536]{1,0:T(8,128)S(1)}, u32[]{:S(2)}, u32[]{:S(2)}) collective-permute-start(f32[64,1536]{1,0:T(8,128)S(1)} %get-tuple-element.27), channel_id=1, source_target_pairs={{0,4},{4,0},{8,12},{12,8},{1,5},{5,1},{9,13},{13,9},{2,6},{6,2},{1... | collective-permute-start | bytes 1179656 | tf_op jit(solution)/shard_map/ppermute | solution.py:215
  142.7 14.7 %collective-permute-start.26 = (f32[64,1536]{1,0:T(8,128)S(1)}, f32[64,1536]{1,0:T(8,128)S(1)}, u32[]{:S(2)}, u32[]{:S(2)}) collective-permute-start(f32[64,1536]{1,0:T(8,128)S(1)} %get-tuple-element.27), channel_id=1, source_target_pairs={{0,0},{4,8},{8,4},{12,12},{1,1},{5,9},{9,5},{13,13},{2,2},{6,10},{... | collective-permute-start | bytes 1179656 | tf_op jit(solution)/shard_map/ppermute | solution.py:215
  143.4 21.5 %collective-permute-start.38 = (f32[64,1536]{1,0:T(8,128)S(1)}, f32[64,1536]{1,0:T(8,128)S(1)}, u32[]{:S(2)}, u32[]{:S(2)}) collective-permute-start(f32[64,1536]{1,0:T(8,128)S(1)} %collective-permute-done.37), channel_id=1, source_target_pairs={{0,4},{4,0},{8,12},{12,8},{1,5},{5,1},{9,13},{13,9},{2,6},{6,2},{1... | collective-permute-start | bytes 1179656 | tf_op jit(solution)/shard_map/ppermute | solution.py:219
  148.0 17.6 %collective-permute-start.40 = (f32[64,1536]{1,0:T(8,128)S(1)}, f32[64,1536]{1,0:T(8,128)S(1)}, u32[]{:S(2)}, u32[]{:S(2)}) collective-permute-start(f32[64,1536]{1,0:T(8,128)S(1)} %collective-permute-done.39), channel_id=1, source_target_pairs={{0,0},{4,8},{8,4},{12,12},{1,1},{5,9},{9,5},{13,13},{2,2},{6,10},{... | collective-permute-start | bytes 1179656 | tf_op jit(solution)/shard_map/ppermute | solution.py:219
  156.4 17.4 %collective-permute-start.29 = (f32[64,1536]{1,0:T(8,128)S(1)}, f32[64,1536]{1,0:T(8,128)S(1)}, u32[]{:S(2)}, u32[]{:S(2)}) collective-permute-start(f32[64,1536]{1,0:T(8,128)S(1)} %collective-permute-done.28), channel_id=1, source_target_pairs={{0,0},{4,8},{8,4},{12,12},{1,1},{5,9},{9,5},{13,13},{2,2},{6,10},{... | collective-permute-start | bytes 1179656 | tf_op jit(solution)/shard_map/ppermute | solution.py:219
  157.3 16.0 %collective-permute-start.27 = (f32[64,1536]{1,0:T(8,128)S(1)}, f32[64,1536]{1,0:T(8,128)S(1)}, u32[]{:S(2)}, u32[]{:S(2)}) collective-permute-start(f32[64,1536]{1,0:T(8,128)S(1)} %collective-permute-done.26), channel_id=1, source_target_pairs={{0,4},{4,0},{8,12},{12,8},{1,5},{5,1},{9,13},{13,9},{2,6},{6,2},{1... | collective-permute-start | bytes 1179656 | tf_op jit(solution)/shard_map/ppermute | solution.py:219
  165.0 25.2 %collective-permute-start.44 = (f32[64,1536]{1,0:T(8,128)S(1)}, f32[64,1536]{1,0:T(8,128)S(1)}, u32[]{:S(2)}, u32[]{:S(2)}) collective-permute-start(f32[64,1536]{1,0:T(8,128)S(1)} %get-tuple-element.42), channel_id=1, source_target_pairs={{0,2},{1,3},{2,0},{3,1},{4,6},{5,7},{6,4},{7,5},{8,10},{9,11},{10,... | collective-permute-start | bytes 1179656 | tf_op jit(solution)/shard_map/ppermute | solution.py:230
  165.6 24.7 %collective-permute-start.42 = (f32[64,1536]{1,0:T(8,128)S(1)}, f32[64,1536]{1,0:T(8,128)S(1)}, u32[]{:S(2)}, u32[]{:S(2)}) collective-permute-start(f32[64,1536]{1,0:T(8,128)S(1)} %get-tuple-element.43.refs_8_), channel_id=1, source_target_pairs={{0,1},{1,0},{2,3},{3,2},{4,5},{5,4},{6,7},{7,6},{8,9},{9,8},{10,11... | collective-permute-start | bytes 1179656 | tf_op jit(solution)/shard_map/ppermute | solution.py:231
  165.6 14.4 %collective-permute-start.41 = (f32[64,1536]{1,0:T(8,128)S(1)}, f32[64,1536]{1,0:T(8,128)S(1)}, u32[]{:S(2)}, u32[]{:S(2)}) collective-permute-start(f32[64,1536]{1,0:T(8,128)S(1)} %collective-permute-done.40), channel_id=1, source_target_pairs={{0,4},{4,0},{8,12},{12,8},{1,5},{5,1},{9,13},{13,9},{2,6},{6,2},{1... | collective-permute-start | bytes 1179656 | tf_op jit(solution)/shard_map/ppermute | solution.py:223
  173.4 18.3 %collective-permute-start.33 = (f32[64,1536]{1,0:T(8,128)S(1)}, f32[64,1536]{1,0:T(8,128)S(1)}, u32[]{:S(2)}, u32[]{:S(2)}) collective-permute-start(f32[64,1536]{1,0:T(8,128)S(1)} %get-tuple-element.46), channel_id=1, source_target_pairs={{0,2},{1,3},{2,0},{3,1},{4,6},{5,7},{6,4},{7,5},{8,10},{9,11},{10,... | collective-permute-start | bytes 1179656 | tf_op jit(solution)/shard_map/ppermute | solution.py:230
  173.9 18.0 %collective-permute-start.31 = (f32[64,1536]{1,0:T(8,128)S(1)}, f32[64,1536]{1,0:T(8,128)S(1)}, u32[]{:S(2)}, u32[]{:S(2)}) collective-permute-start(f32[64,1536]{1,0:T(8,128)S(1)} %get-tuple-element.47.refs_0_), channel_id=1, source_target_pairs={{0,1},{1,0},{2,3},{3,2},{4,5},{5,4},{6,7},{7,6},{8,9},{9,8},{10,11... | collective-permute-start | bytes 1179656 | tf_op jit(solution)/shard_map/ppermute | solution.py:231
  189.4 12.1 %collective-permute-start.45 = (f32[64,1536]{1,0:T(8,128)S(1)}, f32[64,1536]{1,0:T(8,128)S(1)}, u32[]{:S(2)}, u32[]{:S(2)}) collective-permute-start(f32[64,1536]{1,0:T(8,128)S(1)} %get-tuple-element.40), channel_id=1, source_target_pairs={{0,2},{1,3},{2,0},{3,1},{4,6},{5,7},{6,4},{7,5},{8,10},{9,11},{10,... | collective-permute-start | bytes 1179656 | tf_op jit(solution)/shard_map/ppermute | solution.py:230
  190.3 16.0 %collective-permute-start.34 = (f32[64,1536]{1,0:T(8,128)S(1)}, f32[64,1536]{1,0:T(8,128)S(1)}, u32[]{:S(2)}, u32[]{:S(2)}) collective-permute-start(f32[64,1536]{1,0:T(8,128)S(1)} %get-tuple-element.44), channel_id=1, source_target_pairs={{0,2},{1,3},{2,0},{3,1},{4,6},{5,7},{6,4},{7,5},{8,10},{9,11},{10,... | collective-permute-start | bytes 1179656 | tf_op jit(solution)/shard_map/ppermute | solution.py:230
  191.7 14.6 %collective-permute-start.32 = (f32[64,1536]{1,0:T(8,128)S(1)}, f32[64,1536]{1,0:T(8,128)S(1)}, u32[]{:S(2)}, u32[]{:S(2)}) collective-permute-start(f32[64,1536]{1,0:T(8,128)S(1)} %get-tuple-element.45.refs_1_), channel_id=1, source_target_pairs={{0,1},{1,0},{2,3},{3,2},{4,5},{5,4},{6,7},{7,6},{8,9},{9,8},{10,11... | collective-permute-start | bytes 1179656 | tf_op jit(solution)/shard_map/ppermute | solution.py:231
  191.9 14.5 %collective-permute-start.46 = (f32[64,1536]{1,0:T(8,128)S(1)}, f32[64,1536]{1,0:T(8,128)S(1)}, u32[]{:S(2)}, u32[]{:S(2)}) collective-permute-start(f32[64,1536]{1,0:T(8,128)S(1)} %collective-permute-done.44.refs_12_), channel_id=1, source_target_pairs={{0,1},{1,0},{2,3},{3,2},{4,5},{5,4},{6,7},{7,6},{8,9},{9,8},{10,11... | collective-permute-start | bytes 1179656 | tf_op jit(solution)/shard_map/ppermute | solution.py:231
  225.2 14.7 %collective-permute-start.49 = (f32[64,1536]{1,0:T(8,128)S(1)}, f32[64,1536]{1,0:T(8,128)S(1)}, u32[]{:S(2)}, u32[]{:S(2)}) collective-permute-start(f32[64,1536]{1,0:T(8,128)S(1)} %slice_add_fusion.1.refs_18_), channel_id=1, source_target_pairs={{0,2},{1,3},{2,0},{3,1},{4,6},{5,7},{6,4},{7,5},{8,10},{9,11},{10,... | collective-permute-start | bytes 1179656 | tf_op jit(solution)/shard_map/ppermute | solution.py:290
  (57 other events, 733.7 us)

commit v4 on v3

--- a/solution.py
+++ b/solution.py
@@ -116,7 +116,7 @@
         scratch_shapes=[pltpu.VMEM((high, wide), f32)],
         compiler_params=pltpu.CompilerParams(vmem_limit_bytes=24 << 20),
         cost_estimate=pl.CostEstimate(flops=200 * high * span, bytes_accessed=28 * high * wide, transcendentals=20 * high * span),
-    )(base, state, *value, *terms, friction, region, partner)
+    )(*(a if last else pltpu.with_memory_space_constraint(a, pltpu.HBM) for a in (base, state, *value)), *terms, friction, region, partner)
 
 
 def whole(shape):
@@ -223,21 +223,34 @@
     return lax.ppermute(two[1], "row", OUTER)
 
 
-def shift(first, second):
+def shift(first, second, guard=None):
     beside = where_sent()[1]
     mine = jnp.where(beside, first, second)
     sent = jnp.where(beside, second, first)
+    if guard is not None:
+        sent = once(sent, guard)
     got = lax.ppermute(sent, PLANE, ACROSS)
     return [mine, lax.ppermute(mine, PLANE, CORE), got, lax.ppermute(got, PLANE, CORE)]
 
 
-def spread(rates):
-    middle = where_sent()[0]
+def along(rates, guard=None):
     near = spread_one(rates)
     two = spread_two(near)
-    far = spread_three(two)
-    one = shift(rates, jnp.where(middle, near[1], two[0]))
-    return list(zip(one, shift(near[0], jnp.where(middle, two[1], far))))
+    if guard is not None:
+        return rates, near, two, spread_three([two[0], once(two[1], guard)])
+    return rates, near, two, spread_three(two)
+
+
+def spread(halves, ordered):
+    middle = where_sent()[0]
+    one = [shift(rates, jnp.where(middle, near[1], two[0])) for rates, near, two, far in halves]
+    guard = one[1][2] if ordered else None
+    pairs = []
+    for k, (rates, near, two, far) in enumerate(halves):
+        last = shift(near[0], jnp.where(middle, two[1], far), guard)
+        pairs.append(list(zip(one[k], last)))
+        guard = last[2] if ordered else None
+    return pairs
 
 
 def first_block():
@@ -291,16 +304,15 @@
             return sums
 
         rates = jnp.exp(log_rate)
-        ready = spread(rates[:, cuts[0]])
-        sums = product([ready, spread(rates[:, cuts[1]])])
+        sums = product(spread([along(rates[:, cut]) for cut in cuts], False))
         value, rates, first = step_kernel(
             step_size, False, 0, 2, base_stress, [log_rate[:, cuts[0]]], state, sums, None, *labels
         )
-        ready = spread(rates)
+        ready = along(rates)
         other_value, rates = step_kernel(
             step_size, False, 1, 2, base_stress, [log_rate[:, cuts[1]]], state, sums, None, *labels
         )
-        sums = product([ready, spread(rates)])
+        sums = product(spread([ready, along(rates)], False))
         return tuple(
             step_kernel(
                 0.5 * step_size, True, 0, 1, base_stress, [value, other_value], state, sums, first, *labels

time: 263 us -> 261 us (level)
  Pallas kernels: 71.8 us -> 74.6 us
    unnamed x74 -> x64, local copies, waits for them, and re-layouts: 4.28 us -> 0.88 us
    pallas_call x3, Pallas kernels: 16.4 us -> 19.2 us  [step_kernel(): pl.pallas_call(body, grid=(1,), in_specs=[whole(a.shape) for a in (base,...]
  transfers between devices with their start and end apart: 52 -> 52, of which waited for: 23 -> 22; matrix products, arithmetic and copies ran while one was open for 1% -> 1% of each run, Pallas kernels for 12% -> 13%
where the time goes in v4:
time: 261 us; the launch traced here: 260 us
  waiting for transfers between devices  114 us (44%)
  Pallas kernels  74.6 us (29%)
  starting transfers between devices  63.4 us (24%)
  local copies, waits for them, and re-layouts  4.2 us (2%)
    pallas_call x4, Pallas kernels, rates_times(): pl.pallas_call(body, grid=(steps,), in_specs=[pl.BlockSpec(memory_space=p...  55.4 us
    ppermute x8, waiting for transfers between devices, shift(): got = lax.ppermute(sent, PLANE, ACROSS)  26.9 us
    ppermute x4, waiting for transfers between devices, spread_three(): return lax.ppermute(two[1], 'row', OUTER)  23.8 us
    ppermute x4, starting transfers between devices, spread_two(): lax.ppermute(near[1], 'row', OUTER)  21.5 us
    ppermute x4, waiting for transfers between devices, spread_two(): lax.ppermute(near[1], 'row', OUTER)  20 us
    pallas_call x3, Pallas kernels, step_kernel(): pl.pallas_call(body, grid=(1,), in_specs=[whole(a.shape) for a in (base,...  19.2 us
    ppermute x4, waiting for transfers between devices, product(): sums.append([own, swapped, lax.ppermute(before, PLANE, ACROSS)])  18.3 us
    ppermute x4, waiting for transfers between devices, spread_one(): lax.ppermute(rates, 'row', OUTER)  12.7 us
  transfers between devices with their start and end apart: 52, of which 22 were waited for; matrix products, arithmetic and copies ran while one was open for 1% of the time, Pallas kernels for 13%

profile of v4, /device:TPU:0, one launch (start us, length us, event | category | flops | bytes accessed | tf_op | source)
XLA Modules:
  0.0 259.8 jit_solution(12629740440938884386)
XLA Ops:
  2.6 5.9 %collective-permute-start.13 = (f32[64,1536]{1,0:T(8,128)S(1)}, f32[64,1536]{1,0:T(8,128)S(1)}, u32[]{:S(2)}, u32[]{:S(2)}) collective-permute-start(f32[64,1536]{1,0:T(8,128)S(1)} %slice.33), channel_id=1, source_target_pairs={{0,4},{4,0},{8,12},{12,8},{1,5},{5,1},{9,13},{13,9},{2,6},{6,2},{1... | collective-permute-start | bytes 1179656 | tf_op jit(solution)/shard_map/ppermute | solution.py:215
  8.5 9.2 %collective-permute-start.12 = (f32[64,1536]{1,0:T(8,128)S(1)}, f32[64,1536]{1,0:T(8,128)S(1)}, u32[]{:S(2)}, u32[]{:S(2)}) collective-permute-start(f32[64,1536]{1,0:T(8,128)S(1)} %collective-permute-done.11), channel_id=1, source_target_pairs={{0,4},{4,0},{8,12},{12,8},{1,5},{5,1},{9,13},{13,9},{2,6},{6,2},{1... | collective-permute-start | bytes 1179656 | tf_op jit(solution)/shard_map/ppermute | solution.py:219
  18.4 7.6 %collective-permute-done.12 = f32[64,1536]{1,0:T(8,128)S(1)} collective-permute-done((f32[64,1536]{1,0:T(8,128)S(1)}, f32[64,1536]{1,0:T(8,128)S(1)}, u32[]{:S(2)}, u32[]{:S(2)}) %collective-permute-start.12) | collective-permute-done | bytes 393248 | tf_op jit(solution)/shard_map/ppermute | solution.py:219
  28.6 3.1 %collective-permute-start.15 = (f32[64,1536]{1,0:T(8,128)S(1)}, f32[64,1536]{1,0:T(8,128)S(1)}, u32[]{:S(2)}, u32[]{:S(2)}) collective-permute-start(f32[64,1536]{1,0:T(8,128)S(1)} %collective-permute-done.14), channel_id=1, source_target_pairs={{0,4},{4,0},{8,12},{12,8},{1,5},{5,1},{9,13},{13,9},{2,6},{6,2},{1... | collective-permute-start | bytes 1179656 | tf_op jit(solution)/shard_map/ppermute | solution.py:223
  33.2 5.0 %collective-permute-done.2 = f32[64,1536]{1,0:T(8,128)S(1)} collective-permute-done((f32[64,1536]{1,0:T(8,128)S(1)}, f32[64,1536]{1,0:T(8,128)S(1)}, u32[]{:S(2)}, u32[]{:S(2)}) %collective-permute-start.2) | collective-permute-done | bytes 393248 | tf_op jit(solution)/shard_map/ppermute | solution.py:215
  38.9 4.6 %collective-permute-start.1 = (f32[64,1536]{1,0:T(8,128)S(1)}, f32[64,1536]{1,0:T(8,128)S(1)}, u32[]{:S(2)}, u32[]{:S(2)}) collective-permute-start(f32[64,1536]{1,0:T(8,128)S(1)} %collective-permute-done), channel_id=1, source_target_pairs={{0,4},{4,0},{8,12},{12,8},{1,5},{5,1},{9,13},{13,9},{2,6},{6,2},{1... | collective-permute-start | bytes 1179656 | tf_op jit(solution)/shard_map/ppermute | solution.py:219
  43.5 3.1 %collective-permute-done.15 = f32[64,1536]{1,0:T(8,128)S(1)} collective-permute-done((f32[64,1536]{1,0:T(8,128)S(1)}, f32[64,1536]{1,0:T(8,128)S(1)}, u32[]{:S(2)}, u32[]{:S(2)}) %collective-permute-start.15) | collective-permute-done | bytes 393248 | tf_op jit(solution)/shard_map/ppermute | solution.py:223
  48.8 3.6 %collective-permute-done.1 = f32[64,1536]{1,0:T(8,128)S(1)} collective-permute-done((f32[64,1536]{1,0:T(8,128)S(1)}, f32[64,1536]{1,0:T(8,128)S(1)}, u32[]{:S(2)}, u32[]{:S(2)}) %collective-permute-start.1) | collective-permute-done | bytes 393248 | tf_op jit(solution)/shard_map/ppermute | solution.py:219
  54.1 6.7 %collective-permute-done.4 = f32[64,1536]{1,0:T(8,128)S(1)} collective-permute-done((f32[64,1536]{1,0:T(8,128)S(1)}, f32[64,1536]{1,0:T(8,128)S(1)}, u32[]{:S(2)}, u32[]{:S(2)}) %collective-permute-start.4) | collective-permute-done | bytes 393248 | tf_op jit(solution)/shard_map/ppermute | solution.py:223
  63.6 8.9 %collective-permute-done.7.refs_4_ = f32[64,1536]{1,0:T(8,128)S(1)} collective-permute-done((f32[64,1536]{1,0:T(8,128)S(1)}, f32[64,1536]{1,0:T(8,128)S(1)}, u32[]{:S(2)}, u32[]{:S(2)}) %collective-permute-start.7) | collective-permute-done | bytes 393248 | tf_op jit(solution)/shard_map/ppermute | solution.py:232
  72.5 4.2 %collective-permute-done.8.refs_5_ = f32[64,1536]{1,0:T(8,128)S(1)} collective-permute-done((f32[64,1536]{1,0:T(8,128)S(1)}, f32[64,1536]{1,0:T(8,128)S(1)}, u32[]{:S(2)}, u32[]{:S(2)}) %collective-permute-start.8) | collective-permute-done | bytes 393248 | tf_op jit(solution)/shard_map/ppermute | solution.py:232
  78.7 13.9 %shard_map.86 = (f32[64,1536]{1,0:T(8,128)S(1)}, f32[64,1536]{1,0:T(8,128)S(1)}, f32[128,1536]{1,0:T(8,128)S(1)}) custom-call(s32[1]{0:T(128)} %bitcast.choice_ref, f32[64,1536]{1,0:T(8,128)} %copy-done.7, f32[64,1536]{1,0:T(8,128)} %copy-done.9, f32[64,1536]{1,0:T(8,128)} %collective-permute-done.5.refs_2_, f32[64,1536]{1,0:T(8,128)} %collective-permute-done.6.refs_3_, ...), custom_call_target="tpu_custom_call" | custom-call | flops 14495514624 | bytes 18874368 | tf_op jit(solution)/shard_map/pallas_call | solution.py:177
  96.5 13.8 %shard_map.87 = (f32[64,1536]{1,0:T(8,128)S(1)}, f32[64,1536]{1,0:T(8,128)S(1)}, f32[128,1536]{1,0:T(8,128)S(1)}) custom-call(s32[1]{0:T(128)} %bitcast.choice_ref, f32[64,1536]{1,0:T(8,128)} %copy-done.7, f32[64,1536]{1,0:T(8,128)} %copy-done.9, f32[64,1536]{1,0:T(8,128)} %collective-permute-done.5.refs_2_, f32[64,1536]{1,0:T(8,128)} %collective-permute-done.6.refs_3_, ...), custom_call_target="tpu_custom_call" | custom-call | flops 14495514624 | bytes 18874368 | tf_op jit(solution)/shard_map/pallas_call | solution.py:177
  111.4 2.5 collective-permute-done.24.refs_7_
  116.6 8.6 %collective-permute-done.25.refs_8_ = f32[64,1536]{1,0:T(8,128)S(1)} collective-permute-done((f32[64,1536]{1,0:T(8,128)S(1)}, f32[64,1536]{1,0:T(8,128)S(1)}, u32[]{:S(2)}, u32[]{:S(2)}) %collective-permute-start.25) | collective-permute-done | bytes 393248 | tf_op jit(solution)/shard_map/ppermute | solution.py:303
  125.2 5.3 %shard_map.89 = (f32[64,1536]{1,0:T(8,128)S(1)}, f32[64,1536]{1,0:T(8,128)S(1)}) custom-call(f32[64,3072]{1,0:T(8,128)} %refs_0_.5, f32[64,3072]{1,0:T(8,128)} %refs_1_.5, f32[64,1536]{1,0:T(8,128)} %get-tuple-element.52.refs_2_, f32[64,1536]{1,0:T(8,128)S(1)} %get-tuple-element.19.refs_17_.refs_3_, f32[128,1536]{1,0:T(8,128)S(1)} %collective-permute-done.22.refs_4_, ...), custom_call_target="tpu_custom_call" | custom-call | flops 19660800 | bytes 5505024 | tf_op jit(solution)/shard_map/pallas_call | solution.py:110
  131.2 4.1 %collective-permute-start.39 = (f32[64,1536]{1,0:T(8,128)S(1)}, f32[64,1536]{1,0:T(8,128)S(1)}, u32[]{:S(2)}, u32[]{:S(2)}) collective-permute-start(f32[64,1536]{1,0:T(8,128)S(1)} %get-tuple-element.28), channel_id=1, source_target_pairs={{0,4},{4,0},{8,12},{12,8},{1,5},{5,1},{9,13},{13,9},{2,6},{6,2},{1... | collective-permute-start | bytes 1179656 | tf_op jit(solution)/shard_map/ppermute | solution.py:215
  135.3 5.3 %shard_map.88 = (f32[64,1536]{1,0:T(8,128)S(1)}, f32[64,1536]{1,0:T(8,128)S(1)}, f32[64,3072]{1,0:T(8,128)S(1)}) custom-call(f32[64,3072]{1,0:T(8,128)} %refs_0_.5, f32[64,3072]{1,0:T(8,128)} %refs_1_.5, f32[64,1536]{1,0:T(8,128)} %get-tuple-element.53.refs_2_, f32[64,1536]{1,0:T(8,128)S(1)} %get-tuple-element.19.refs_17_.refs_3_, ...), custom_call_target="tpu_custom_call" | custom-call | flops 19660800 | bytes 5505024 | tf_op jit(solution)/shard_map/pallas_call | solution.py:110
  141.4 3.7 %collective-permute-start.38 = (f32[64,1536]{1,0:T(8,128)S(1)}, f32[64,1536]{1,0:T(8,128)S(1)}, u32[]{:S(2)}, u32[]{:S(2)}) collective-permute-start(f32[64,1536]{1,0:T(8,128)S(1)} %collective-permute-done.37), channel_id=1, source_target_pairs={{0,4},{4,0},{8,12},{12,8},{1,5},{5,1},{9,13},{13,9},{2,6},{6,2},{1... | collective-permute-start | bytes 1179656 | tf_op jit(solution)/shard_map/ppermute | solution.py:219
  145.9 7.7 %collective-permute-done.28 = f32[64,1536]{1,0:T(8,128)S(1)} collective-permute-done((f32[64,1536]{1,0:T(8,128)S(1)}, f32[64,1536]{1,0:T(8,128)S(1)}, u32[]{:S(2)}, u32[]{:S(2)}) %collective-permute-start.28) | collective-permute-done | bytes 393248 | tf_op jit(solution)/shard_map/ppermute | solution.py:215
  154.5 4.0 %collective-permute-start.27 = (f32[64,1536]{1,0:T(8,128)S(1)}, f32[64,1536]{1,0:T(8,128)S(1)}, u32[]{:S(2)}, u32[]{:S(2)}) collective-permute-start(f32[64,1536]{1,0:T(8,128)S(1)} %collective-permute-done.26), channel_id=1, source_target_pairs={{0,4},{4,0},{8,12},{12,8},{1,5},{5,1},{9,13},{13,9},{2,6},{6,2},{1... | collective-permute-start | bytes 1179656 | tf_op jit(solution)/shard_map/ppermute | solution.py:219
  158.4 3.6 %collective-permute-done.38 = f32[64,1536]{1,0:T(8,128)S(1)} collective-permute-done((f32[64,1536]{1,0:T(8,128)S(1)}, f32[64,1536]{1,0:T(8,128)S(1)}, u32[]{:S(2)}, u32[]{:S(2)}) %collective-permute-start.38) | collective-permute-done | bytes 393248 | tf_op jit(solution)/shard_map/ppermute | solution.py:219
  162.7 2.4 collective-permute-start.41
  165.1 5.3 %collective-permute-done.27 = f32[64,1536]{1,0:T(8,128)S(1)} collective-permute-done((f32[64,1536]{1,0:T(8,128)S(1)}, f32[64,1536]{1,0:T(8,128)S(1)}, u32[]{:S(2)}, u32[]{:S(2)}) %collective-permute-start.27) | collective-permute-done | bytes 393248 | tf_op jit(solution)/shard_map/ppermute | solution.py:219
  171.1 6.2 %collective-permute-done.41 = f32[64,1536]{1,0:T(8,128)S(1)} collective-permute-done((f32[64,1536]{1,0:T(8,128)S(1)}, f32[64,1536]{1,0:T(8,128)S(1)}, u32[]{:S(2)}, u32[]{:S(2)}) %collective-permute-start.41) | collective-permute-done | bytes 393248 | tf_op jit(solution)/shard_map/ppermute | solution.py:223
  179.2 7.8 %collective-permute-done.30 = f32[64,1536]{1,0:T(8,128)S(1)} collective-permute-done((f32[64,1536]{1,0:T(8,128)S(1)}, f32[64,1536]{1,0:T(8,128)S(1)}, u32[]{:S(2)}, u32[]{:S(2)}) %collective-permute-start.30) | collective-permute-done | bytes 393248 | tf_op jit(solution)/shard_map/ppermute | solution.py:223
  189.8 9.2 %collective-permute-done.45.refs_13_ = f32[64,1536]{1,0:T(8,128)S(1)} collective-permute-done((f32[64,1536]{1,0:T(8,128)S(1)}, f32[64,1536]{1,0:T(8,128)S(1)}, u32[]{:S(2)}, u32[]{:S(2)}) %collective-permute-start.45) | collective-permute-done | bytes 393248 | tf_op jit(solution)/shard_map/ppermute | solution.py:232
  199.5 4.5 %collective-permute-done.34.refs_5_ = f32[64,1536]{1,0:T(8,128)S(1)} collective-permute-done((f32[64,1536]{1,0:T(8,128)S(1)}, f32[64,1536]{1,0:T(8,128)S(1)}, u32[]{:S(2)}, u32[]{:S(2)}) %collective-permute-start.34) | collective-permute-done | bytes 393248 | tf_op jit(solution)/shard_map/ppermute | solution.py:232
  206.7 13.8 %shard_map.90 = (f32[64,1536]{1,0:T(8,128)S(1)}, f32[64,1536]{1,0:T(8,128)S(1)}, f32[128,1536]{1,0:T(8,128)S(1)}) custom-call(s32[1]{0:T(128)} %bitcast.choice_ref, f32[64,1536]{1,0:T(8,128)} %copy-done.8, f32[64,1536]{1,0:T(8,128)} %copy-done.11, f32[64,1536]{1,0:T(8,128)} %copy-done.23, f32[64,1536]{1,0:T(8,128)} %copy-done.27, f32[64,1536]{1,0:T(8,128)} %copy-done.21, ...), custom_call_target="tpu_custom_call" | custom-call | flops 14495514624 | bytes 18874368 | tf_op jit(solution)/shard_map/pallas_call | solution.py:177
  223.6 13.8 %shard_map.91 = (f32[64,1536]{1,0:T(8,128)S(1)}, f32[64,1536]{1,0:T(8,128)S(1)}, f32[128,1536]{1,0:T(8,128)S(1)}) custom-call(s32[1]{0:T(128)} %bitcast.choice_ref, f32[64,1536]{1,0:T(8,128)} %copy-done.8, f32[64,1536]{1,0:T(8,128)} %copy-done.11, f32[64,1536]{1,0:T(8,128)} %copy-done.23, f32[64,1536]{1,0:T(8,128)} %copy-done.27, f32[64,1536]{1,0:T(8,128)} %copy-done.21, ...), custom_call_target="tpu_custom_call" | custom-call | flops 14495514624 | bytes 18874368 | tf_op jit(solution)/shard_map/pallas_call | solution.py:177
  241.5 9.7 %collective-permute-done.51.refs_9_ = f32[64,1536]{1,0:T(8,128)S(1)} collective-permute-done((f32[64,1536]{1,0:T(8,128)S(1)}, f32[64,1536]{1,0:T(8,128)S(1)}, u32[]{:S(2)}, u32[]{:S(2)}) %collective-permute-start.51) | collective-permute-done | bytes 393248 | tf_op jit(solution)/shard_map/ppermute | solution.py:303
  251.2 8.6 %shard_map.92 = (f32[64,3072]{1,0:T(8,128)}, f32[64,3072]{1,0:T(8,128)}) custom-call(f32[64,3072]{1,0:T(8,128)S(1)} %copy-done, f32[64,3072]{1,0:T(8,128)S(1)} %copy-done.1, f32[64,1536]{1,0:T(8,128)S(1)} %get-tuple-element.25.refs_2_, f32[64,1536]{1,0:T(8,128)S(1)} %get-tuple-element.26.refs_3_, f32[64,1536]{1,0:T(8,128)S(1)} %get-tuple-element.29.refs_17_.refs_4_, ...), custom_call_target="tpu_custom_call" | custom-call | flops 39321600 | bytes 5505024 | tf_op jit(solution)/shard_map/pallas_call | solution.py:110
  (163 shorter events, 42.6 us)
Async XLA Ops:
  2.6 15.1 %collective-permute-start.13 = (f32[64,1536]{1,0:T(8,128)S(1)}, f32[64,1536]{1,0:T(8,128)S(1)}, u32[]{:S(2)}, u32[]{:S(2)}) collective-permute-start(f32[64,1536]{1,0:T(8,128)S(1)} %slice.33), channel_id=1, source_target_pairs={{0,4},{4,0},{8,12},{12,8},{1,5},{5,1},{9,13},{13,9},{2,6},{6,2},{1... | collective-permute-start | bytes 1179656 | tf_op jit(solution)/shard_map/ppermute | solution.py:215
  8.5 17.4 %collective-permute-start.12 = (f32[64,1536]{1,0:T(8,128)S(1)}, f32[64,1536]{1,0:T(8,128)S(1)}, u32[]{:S(2)}, u32[]{:S(2)}) collective-permute-start(f32[64,1536]{1,0:T(8,128)S(1)} %collective-permute-done.11), channel_id=1, source_target_pairs={{0,4},{4,0},{8,12},{12,8},{1,5},{5,1},{9,13},{13,9},{2,6},{6,2},{1... | collective-permute-start | bytes 1179656 | tf_op jit(solution)/shard_map/ppermute | solution.py:219
  26.1 12.1 %collective-permute-start.2 = (f32[64,1536]{1,0:T(8,128)S(1)}, f32[64,1536]{1,0:T(8,128)S(1)}, u32[]{:S(2)}, u32[]{:S(2)}) collective-permute-start(f32[64,1536]{1,0:T(8,128)S(1)} %get-tuple-element.54), channel_id=1, source_target_pairs={{0,4},{4,0},{8,12},{12,8},{1,5},{5,1},{9,13},{13,9},{2,6},{6,2},{1... | collective-permute-start | bytes 1179656 | tf_op jit(solution)/shard_map/ppermute | solution.py:215
  28.6 18.0 %collective-permute-start.15 = (f32[64,1536]{1,0:T(8,128)S(1)}, f32[64,1536]{1,0:T(8,128)S(1)}, u32[]{:S(2)}, u32[]{:S(2)}) collective-permute-start(f32[64,1536]{1,0:T(8,128)S(1)} %collective-permute-done.14), channel_id=1, source_target_pairs={{0,4},{4,0},{8,12},{12,8},{1,5},{5,1},{9,13},{13,9},{2,6},{6,2},{1... | collective-permute-start | bytes 1179656 | tf_op jit(solution)/shard_map/ppermute | solution.py:223
  31.7 16.5 %collective-permute-start.18 = (f32[64,1536]{1,0:T(8,128)S(1)}, f32[64,1536]{1,0:T(8,128)S(1)}, u32[]{:S(2)}, u32[]{:S(2)}) collective-permute-start(f32[64,1536]{1,0:T(8,128)S(1)} %get-tuple-element.36), channel_id=1, source_target_pairs={{0,2},{1,3},{2,0},{3,1},{4,6},{5,7},{6,4},{7,5},{8,10},{9,11},{10,... | collective-permute-start | bytes 1179656 | tf_op jit(solution)/shard_map/ppermute | solution.py:232
  33.2 29.1 %collective-permute-start.16 = (f32[64,1536]{1,0:T(8,128)S(1)}, f32[64,1536]{1,0:T(8,128)S(1)}, u32[]{:S(2)}, u32[]{:S(2)}) collective-permute-start(f32[64,1536]{1,0:T(8,128)S(1)} %get-tuple-element.37.refs_8_), channel_id=1, source_target_pairs={{0,1},{1,0},{2,3},{3,2},{4,5},{5,4},{6,7},{7,6},{8,9},{9,8},{10,11... | collective-permute-start | bytes 1179656 | tf_op jit(solution)/shard_map/ppermute | solution.py:233
  38.9 13.4 %collective-permute-start.1 = (f32[64,1536]{1,0:T(8,128)S(1)}, f32[64,1536]{1,0:T(8,128)S(1)}, u32[]{:S(2)}, u32[]{:S(2)}) collective-permute-start(f32[64,1536]{1,0:T(8,128)S(1)} %collective-permute-done), channel_id=1, source_target_pairs={{0,4},{4,0},{8,12},{12,8},{1,5},{5,1},{9,13},{13,9},{2,6},{6,2},{1... | collective-permute-start | bytes 1179656 | tf_op jit(solution)/shard_map/ppermute | solution.py:219
  46.7 16.3 %collective-permute-start.19 = (f32[64,1536]{1,0:T(8,128)S(1)}, f32[64,1536]{1,0:T(8,128)S(1)}, u32[]{:S(2)}, u32[]{:S(2)}) collective-permute-start(f32[64,1536]{1,0:T(8,128)S(1)} %get-tuple-element.48), channel_id=1, source_target_pairs={{0,2},{1,3},{2,0},{3,1},{4,6},{5,7},{6,4},{7,5},{8,10},{9,11},{10,... | collective-permute-start | bytes 1179656 | tf_op jit(solution)/shard_map/ppermute | solution.py:232
  48.2 14.7 %collective-permute-start.17 = (f32[64,1536]{1,0:T(8,128)S(1)}, f32[64,1536]{1,0:T(8,128)S(1)}, u32[]{:S(2)}, u32[]{:S(2)}) collective-permute-start(f32[64,1536]{1,0:T(8,128)S(1)} %get-tuple-element.49.refs_9_), channel_id=1, source_target_pairs={{0,1},{1,0},{2,3},{3,2},{4,5},{5,4},{6,7},{7,6},{8,9},{9,8},{10,11... | collective-permute-start | bytes 1179656 | tf_op jit(solution)/shard_map/ppermute | solution.py:233
  48.3 15.2 %collective-permute-start.20 = (f32[64,1536]{1,0:T(8,128)S(1)}, f32[64,1536]{1,0:T(8,128)S(1)}, u32[]{:S(2)}, u32[]{:S(2)}) collective-permute-start(f32[64,1536]{1,0:T(8,128)S(1)} %collective-permute-done.18.refs_12_), channel_id=1, source_target_pairs={{0,1},{1,0},{2,3},{3,2},{4,5},{5,4},{6,7},{7,6},{8,9},{9,8},{10,11... | collective-permute-start | bytes 1179656 | tf_op jit(solution)/shard_map/ppermute | solution.py:233
  62.3 14.3 %collective-permute-start.8 = (f32[64,1536]{1,0:T(8,128)S(1)}, f32[64,1536]{1,0:T(8,128)S(1)}, u32[]{:S(2)}, u32[]{:S(2)}) collective-permute-start(f32[64,1536]{1,0:T(8,128)S(1)} %get-tuple-element.50), channel_id=1, source_target_pairs={{0,2},{1,3},{2,0},{3,1},{4,6},{5,7},{6,4},{7,5},{8,10},{9,11},{10,... | collective-permute-start | bytes 1179656 | tf_op jit(solution)/shard_map/ppermute | solution.py:232
  62.9 13.8 %collective-permute-start.5 = (f32[64,1536]{1,0:T(8,128)S(1)}, f32[64,1536]{1,0:T(8,128)}, u32[]{:S(2)}, u32[]{:S(2)}) collective-permute-start(f32[64,1536]{1,0:T(8,128)S(1)} %get-tuple-element.39.refs_0_), channel_id=1, source_target_pairs={{0,1},{1,0},{2,3},{3,2},{4,5},{5,4},{6,7},{7,6},{8,9},{9,8},{10,11... | collective-permute-start | bytes 1179656 | tf_op jit(solution)/shard_map/ppermute | solution.py:233
  63.0 13.8 %collective-permute-start.21 = (f32[64,1536]{1,0:T(8,128)S(1)}, f32[64,1536]{1,0:T(8,128)}, u32[]{:S(2)}, u32[]{:S(2)}) collective-permute-start(f32[64,1536]{1,0:T(8,128)S(1)} %collective-permute-done.19.refs_13_), channel_id=1, source_target_pairs={{0,1},{1,0},{2,3},{3,2},{4,5},{5,4},{6,7},{7,6},{8,9},{9,8},{10,11... | collective-permute-start | bytes 1179656 | tf_op jit(solution)/shard_map/ppermute | solution.py:233
  63.5 13.3 %collective-permute-start.6 = (f32[64,1536]{1,0:T(8,128)S(1)}, f32[64,1536]{1,0:T(8,128)}, u32[]{:S(2)}, u32[]{:S(2)}) collective-permute-start(f32[64,1536]{1,0:T(8,128)S(1)} %get-tuple-element.51.refs_1_), channel_id=1, source_target_pairs={{0,1},{1,0},{2,3},{3,2},{4,5},{5,4},{6,7},{7,6},{8,9},{9,8},{10,11... | collective-permute-start | bytes 1179656 | tf_op jit(solution)/shard_map/ppermute | solution.py:233
  95.0 15.4 %collective-permute-start.23 = (f32[64,1536]{1,0:T(8,128)S(1)}, f32[64,1536]{1,0:T(8,128)S(1)}, u32[]{:S(2)}, u32[]{:S(2)}) collective-permute-start(f32[64,1536]{1,0:T(8,128)S(1)} %slice_add_fusion.3.refs_18_), channel_id=1, source_target_pairs={{0,2},{1,3},{2,0},{3,1},{4,6},{5,7},{6,4},{7,5},{8,10},{9,11},{10,... | collective-permute-start | bytes 1179656 | tf_op jit(solution)/shard_map/ppermute | solution.py:303
  131.2 13.9 %collective-permute-start.39 = (f32[64,1536]{1,0:T(8,128)S(1)}, f32[64,1536]{1,0:T(8,128)S(1)}, u32[]{:S(2)}, u32[]{:S(2)}) collective-permute-start(f32[64,1536]{1,0:T(8,128)S(1)} %get-tuple-element.28), channel_id=1, source_target_pairs={{0,4},{4,0},{8,12},{12,8},{1,5},{5,1},{9,13},{13,9},{2,6},{6,2},{1... | collective-permute-start | bytes 1179656 | tf_op jit(solution)/shard_map/ppermute | solution.py:215
  140.7 12.9 %collective-permute-start.28 = (f32[64,1536]{1,0:T(8,128)S(1)}, f32[64,1536]{1,0:T(8,128)S(1)}, u32[]{:S(2)}, u32[]{:S(2)}) collective-permute-start(f32[64,1536]{1,0:T(8,128)S(1)} %get-tuple-element.27), channel_id=1, source_target_pairs={{0,4},{4,0},{8,12},{12,8},{1,5},{5,1},{9,13},{13,9},{2,6},{6,2},{1... | collective-permute-start | bytes 1179656 | tf_op jit(solution)/shard_map/ppermute | solution.py:215
  140.7 13.7 %collective-permute-start.26 = (f32[64,1536]{1,0:T(8,128)S(1)}, f32[64,1536]{1,0:T(8,128)S(1)}, u32[]{:S(2)}, u32[]{:S(2)}) collective-permute-start(f32[64,1536]{1,0:T(8,128)S(1)} %get-tuple-element.27), channel_id=1, source_target_pairs={{0,0},{4,8},{8,4},{12,12},{1,1},{5,9},{9,5},{13,13},{2,2},{6,10},{... | collective-permute-start | bytes 1179656 | tf_op jit(solution)/shard_map/ppermute | solution.py:215
  141.4 20.6 %collective-permute-start.38 = (f32[64,1536]{1,0:T(8,128)S(1)}, f32[64,1536]{1,0:T(8,128)S(1)}, u32[]{:S(2)}, u32[]{:S(2)}) collective-permute-start(f32[64,1536]{1,0:T(8,128)S(1)} %collective-permute-done.37), channel_id=1, source_target_pairs={{0,4},{4,0},{8,12},{12,8},{1,5},{5,1},{9,13},{13,9},{2,6},{6,2},{1... | collective-permute-start | bytes 1179656 | tf_op jit(solution)/shard_map/ppermute | solution.py:219
  145.2 17.5 %collective-permute-start.40 = (f32[64,1536]{1,0:T(8,128)S(1)}, f32[64,1536]{1,0:T(8,128)S(1)}, u32[]{:S(2)}, u32[]{:S(2)}) collective-permute-start(f32[64,1536]{1,0:T(8,128)S(1)} %collective-permute-done.39), channel_id=1, source_target_pairs={{0,0},{4,8},{8,4},{12,12},{1,1},{5,9},{9,5},{13,13},{2,2},{6,10},{... | collective-permute-start | bytes 1179656 | tf_op jit(solution)/shard_map/ppermute | solution.py:219
  153.6 17.5 %collective-permute-start.29 = (f32[64,1536]{1,0:T(8,128)S(1)}, f32[64,1536]{1,0:T(8,128)S(1)}, u32[]{:S(2)}, u32[]{:S(2)}) collective-permute-start(f32[64,1536]{1,0:T(8,128)S(1)} %collective-permute-done.28), channel_id=1, source_target_pairs={{0,0},{4,8},{8,4},{12,12},{1,1},{5,9},{9,5},{13,13},{2,2},{6,10},{... | collective-permute-start | bytes 1179656 | tf_op jit(solution)/shard_map/ppermute | solution.py:219
  154.5 16.0 %collective-permute-start.27 = (f32[64,1536]{1,0:T(8,128)S(1)}, f32[64,1536]{1,0:T(8,128)S(1)}, u32[]{:S(2)}, u32[]{:S(2)}) collective-permute-start(f32[64,1536]{1,0:T(8,128)S(1)} %collective-permute-done.26), channel_id=1, source_target_pairs={{0,4},{4,0},{8,12},{12,8},{1,5},{5,1},{9,13},{13,9},{2,6},{6,2},{1... | collective-permute-start | bytes 1179656 | tf_op jit(solution)/shard_map/ppermute | solution.py:219
  162.1 25.5 %collective-permute-start.44 = (f32[64,1536]{1,0:T(8,128)S(1)}, f32[64,1536]{1,0:T(8,128)S(1)}, u32[]{:S(2)}, u32[]{:S(2)}) collective-permute-start(f32[64,1536]{1,0:T(8,128)S(1)} %get-tuple-element.42), channel_id=1, source_target_pairs={{0,2},{1,3},{2,0},{3,1},{4,6},{5,7},{6,4},{7,5},{8,10},{9,11},{10,... | collective-permute-start | bytes 1179656 | tf_op jit(solution)/shard_map/ppermute | solution.py:232
  162.7 25.0 %collective-permute-start.42 = (f32[64,1536]{1,0:T(8,128)S(1)}, f32[64,1536]{1,0:T(8,128)S(1)}, u32[]{:S(2)}, u32[]{:S(2)}) collective-permute-start(f32[64,1536]{1,0:T(8,128)S(1)} %get-tuple-element.43.refs_8_), channel_id=1, source_target_pairs={{0,1},{1,0},{2,3},{3,2},{4,5},{5,4},{6,7},{7,6},{8,9},{9,8},{10,11... | collective-permute-start | bytes 1179656 | tf_op jit(solution)/shard_map/ppermute | solution.py:233
  162.7 14.6 %collective-permute-start.41 = (f32[64,1536]{1,0:T(8,128)S(1)}, f32[64,1536]{1,0:T(8,128)S(1)}, u32[]{:S(2)}, u32[]{:S(2)}) collective-permute-start(f32[64,1536]{1,0:T(8,128)S(1)} %collective-permute-done.40), channel_id=1, source_target_pairs={{0,4},{4,0},{8,12},{12,8},{1,5},{5,1},{9,13},{13,9},{2,6},{6,2},{1... | collective-permute-start | bytes 1179656 | tf_op jit(solution)/shard_map/ppermute | solution.py:223
  170.5 18.7 %collective-permute-start.33 = (f32[64,1536]{1,0:T(8,128)S(1)}, f32[64,1536]{1,0:T(8,128)S(1)}, u32[]{:S(2)}, u32[]{:S(2)}) collective-permute-start(f32[64,1536]{1,0:T(8,128)S(1)} %get-tuple-element.46), channel_id=1, source_target_pairs={{0,2},{1,3},{2,0},{3,1},{4,6},{5,7},{6,4},{7,5},{8,10},{9,11},{10,... | collective-permute-start | bytes 1179656 | tf_op jit(solution)/shard_map/ppermute | solution.py:232
  171.1 18.3 %collective-permute-start.31 = (f32[64,1536]{1,0:T(8,128)S(1)}, f32[64,1536]{1,0:T(8,128)S(1)}, u32[]{:S(2)}, u32[]{:S(2)}) collective-permute-start(f32[64,1536]{1,0:T(8,128)S(1)} %get-tuple-element.47.refs_0_), channel_id=1, source_target_pairs={{0,1},{1,0},{2,3},{3,2},{4,5},{5,4},{6,7},{7,6},{8,9},{9,8},{10,11... | collective-permute-start | bytes 1179656 | tf_op jit(solution)/shard_map/ppermute | solution.py:233
  187.0 12.1 %collective-permute-start.45 = (f32[64,1536]{1,0:T(8,128)S(1)}, f32[64,1536]{1,0:T(8,128)S(1)}, u32[]{:S(2)}, u32[]{:S(2)}) collective-permute-start(f32[64,1536]{1,0:T(8,128)S(1)} %get-tuple-element.40), channel_id=1, source_target_pairs={{0,2},{1,3},{2,0},{3,1},{4,6},{5,7},{6,4},{7,5},{8,10},{9,11},{10,... | collective-permute-start | bytes 1179656 | tf_op jit(solution)/shard_map/ppermute | solution.py:232
  187.7 16.4 %collective-permute-start.34 = (f32[64,1536]{1,0:T(8,128)S(1)}, f32[64,1536]{1,0:T(8,128)S(1)}, u32[]{:S(2)}, u32[]{:S(2)}) collective-permute-start(f32[64,1536]{1,0:T(8,128)S(1)} %get-tuple-element.44), channel_id=1, source_target_pairs={{0,2},{1,3},{2,0},{3,1},{4,6},{5,7},{6,4},{7,5},{8,10},{9,11},{10,... | collective-permute-start | bytes 1179656 | tf_op jit(solution)/shard_map/ppermute | solution.py:232
  189.3 14.8 %collective-permute-start.32 = (f32[64,1536]{1,0:T(8,128)S(1)}, f32[64,1536]{1,0:T(8,128)S(1)}, u32[]{:S(2)}, u32[]{:S(2)}) collective-permute-start(f32[64,1536]{1,0:T(8,128)S(1)} %get-tuple-element.45.refs_1_), channel_id=1, source_target_pairs={{0,1},{1,0},{2,3},{3,2},{4,5},{5,4},{6,7},{7,6},{8,9},{9,8},{10,11... | collective-permute-start | bytes 1179656 | tf_op jit(solution)/shard_map/ppermute | solution.py:233
  189.4 14.7 %collective-permute-start.46 = (f32[64,1536]{1,0:T(8,128)S(1)}, f32[64,1536]{1,0:T(8,128)S(1)}, u32[]{:S(2)}, u32[]{:S(2)}) collective-permute-start(f32[64,1536]{1,0:T(8,128)S(1)} %collective-permute-done.44.refs_12_), channel_id=1, source_target_pairs={{0,1},{1,0},{2,3},{3,2},{4,5},{5,4},{6,7},{7,6},{8,9},{9,8},{10,11... | collective-permute-start | bytes 1179656 | tf_op jit(solution)/shard_map/ppermute | solution.py:233
  223.0 14.5 %collective-permute-start.49 = (f32[64,1536]{1,0:T(8,128)S(1)}, f32[64,1536]{1,0:T(8,128)S(1)}, u32[]{:S(2)}, u32[]{:S(2)}) collective-permute-start(f32[64,1536]{1,0:T(8,128)S(1)} %slice_add_fusion.1.refs_18_), channel_id=1, source_target_pairs={{0,2},{1,3},{2,0},{3,1},{4,6},{5,7},{6,4},{7,5},{8,10},{9,11},{10,... | collective-permute-start | bytes 1179656 | tf_op jit(solution)/shard_map/ppermute | solution.py:303
  (52 other events, 725.8 us)

commit v5 on v4

--- a/solution.py
+++ b/solution.py
@@ -94,7 +94,7 @@
                     rows = pl.ds(g * 8, 8)
                     own = raw[rows, cols]
                     stress = own + coupling * (moved[g] - own)
-                    new = newton(value_ref[rows, there], state_ref[rows, cols], stress, fric, volume)
+                    new = newton(value_ref[rows, there], state_ref[rows, into], stress, fric, volume)
                     outs[0][rows, into] = new
                     outs[1][rows, into] = stress if last else jnp.exp(new)
                 return later
@@ -110,7 +110,12 @@
     return pl.pallas_call(
         body,
         grid=(1,),
-        in_specs=[whole(a.shape) for a in (base, state, *value, *terms, friction, region, partner)],
+        in_specs=[
+            whole(base.shape),
+            pl.BlockSpec((high, span), lambda *_: (0, part), pipeline_mode=pl.Buffered(1)),
+            *(whole((high, a.shape[1])) for a in (*value, *terms)),
+            *(whole(a.shape) for a in (friction, region, partner)),
+        ],
         out_specs=[whole(a.shape) for a in out_shape],
         out_shape=out_shape,
         scratch_shapes=[pltpu.VMEM((high, wide), f32)],

time: 261 us -> 260 us (level)
  transfers between devices with their start and end apart: 52 -> 52, of which waited for: 22 -> 23; matrix products, arithmetic and copies ran while one was open for 1% -> 1% of each run, Pallas kernels for 13% -> 13%
where the time goes in v5:
time: 260 us; the launch traced here: 259 us
  waiting for transfers between devices  114 us (44%)
  Pallas kernels  74.4 us (29%)
  starting transfers between devices  63.1 us (24%)
  local copies, waits for them, and re-layouts  4.2 us (2%)
    pallas_call x4, Pallas kernels, rates_times(): pl.pallas_call(body, grid=(steps,), in_specs=[pl.BlockSpec(memory_space=p...  55.4 us
    ppermute x8, waiting for transfers between devices, shift(): got = lax.ppermute(sent, PLANE, ACROSS)  26.8 us
    ppermute x4, waiting for transfers between devices, spread_three(): return lax.ppermute(two[1], 'row', OUTER)  23.6 us
    ppermute x4, starting transfers between devices, spread_two(): lax.ppermute(near[1], 'row', OUTER)  21.4 us
    ppermute x4, waiting for transfers between devices, spread_two(): lax.ppermute(near[1], 'row', OUTER)  20.4 us
    pallas_call x3, Pallas kernels, step_kernel(): pl.pallas_call(body, grid=(1,), in_specs=[whole(base.shape), pl.BlockSpec...  19 us
    ppermute x4, waiting for transfers between devices, product(): sums.append([own, swapped, lax.ppermute(before, PLANE, ACROSS)])  18.3 us
    ppermute x4, waiting for transfers between devices, spread_one(): lax.ppermute(rates, 'row', OUTER)  12.9 us
  transfers between devices with their start and end apart: 52, of which 23 were waited for; matrix products, arithmetic and copies ran while one was open for 1% of the time, Pallas kernels for 13%

profile of v5, /device:TPU:0, one launch (start us, length us, event | category | flops | bytes accessed | tf_op | source)
XLA Modules:
  0.0 259.5 jit_solution(142915277436498282)
XLA Ops:
  2.6 5.9 %collective-permute-start.13 = (f32[64,1536]{1,0:T(8,128)S(1)}, f32[64,1536]{1,0:T(8,128)S(1)}, u32[]{:S(2)}, u32[]{:S(2)}) collective-permute-start(f32[64,1536]{1,0:T(8,128)S(1)} %slice.33), channel_id=1, source_target_pairs={{0,4},{4,0},{8,12},{12,8},{1,5},{5,1},{9,13},{13,9},{2,6},{6,2},{1... | collective-permute-start | bytes 1179656 | tf_op jit(solution)/shard_map/ppermute | solution.py:220
  8.5 9.2 %collective-permute-start.12 = (f32[64,1536]{1,0:T(8,128)S(1)}, f32[64,1536]{1,0:T(8,128)S(1)}, u32[]{:S(2)}, u32[]{:S(2)}) collective-permute-start(f32[64,1536]{1,0:T(8,128)S(1)} %collective-permute-done.11), channel_id=1, source_target_pairs={{0,4},{4,0},{8,12},{12,8},{1,5},{5,1},{9,13},{13,9},{2,6},{6,2},{1... | collective-permute-start | bytes 1179656 | tf_op jit(solution)/shard_map/ppermute | solution.py:224
  18.4 7.6 %collective-permute-done.12 = f32[64,1536]{1,0:T(8,128)S(1)} collective-permute-done((f32[64,1536]{1,0:T(8,128)S(1)}, f32[64,1536]{1,0:T(8,128)S(1)}, u32[]{:S(2)}, u32[]{:S(2)}) %collective-permute-start.12) | collective-permute-done | bytes 393248 | tf_op jit(solution)/shard_map/ppermute | solution.py:224
  28.6 3.1 %collective-permute-start.15 = (f32[64,1536]{1,0:T(8,128)S(1)}, f32[64,1536]{1,0:T(8,128)S(1)}, u32[]{:S(2)}, u32[]{:S(2)}) collective-permute-start(f32[64,1536]{1,0:T(8,128)S(1)} %collective-permute-done.14), channel_id=1, source_target_pairs={{0,4},{4,0},{8,12},{12,8},{1,5},{5,1},{9,13},{13,9},{2,6},{6,2},{1... | collective-permute-start | bytes 1179656 | tf_op jit(solution)/shard_map/ppermute | solution.py:228
  33.2 5.0 %collective-permute-done.2 = f32[64,1536]{1,0:T(8,128)S(1)} collective-permute-done((f32[64,1536]{1,0:T(8,128)S(1)}, f32[64,1536]{1,0:T(8,128)S(1)}, u32[]{:S(2)}, u32[]{:S(2)}) %collective-permute-start.2) | collective-permute-done | bytes 393248 | tf_op jit(solution)/shard_map/ppermute | solution.py:220
  38.9 4.6 %collective-permute-start.1 = (f32[64,1536]{1,0:T(8,128)S(1)}, f32[64,1536]{1,0:T(8,128)S(1)}, u32[]{:S(2)}, u32[]{:S(2)}) collective-permute-start(f32[64,1536]{1,0:T(8,128)S(1)} %collective-permute-done), channel_id=1, source_target_pairs={{0,4},{4,0},{8,12},{12,8},{1,5},{5,1},{9,13},{13,9},{2,6},{6,2},{1... | collective-permute-start | bytes 1179656 | tf_op jit(solution)/shard_map/ppermute | solution.py:224
  43.5 3.1 %collective-permute-done.15 = f32[64,1536]{1,0:T(8,128)S(1)} collective-permute-done((f32[64,1536]{1,0:T(8,128)S(1)}, f32[64,1536]{1,0:T(8,128)S(1)}, u32[]{:S(2)}, u32[]{:S(2)}) %collective-permute-start.15) | collective-permute-done | bytes 393248 | tf_op jit(solution)/shard_map/ppermute | solution.py:228
  48.8 3.6 %collective-permute-done.1 = f32[64,1536]{1,0:T(8,128)S(1)} collective-permute-done((f32[64,1536]{1,0:T(8,128)S(1)}, f32[64,1536]{1,0:T(8,128)S(1)}, u32[]{:S(2)}, u32[]{:S(2)}) %collective-permute-start.1) | collective-permute-done | bytes 393248 | tf_op jit(solution)/shard_map/ppermute | solution.py:224
  54.1 6.7 %collective-permute-done.4 = f32[64,1536]{1,0:T(8,128)S(1)} collective-permute-done((f32[64,1536]{1,0:T(8,128)S(1)}, f32[64,1536]{1,0:T(8,128)S(1)}, u32[]{:S(2)}, u32[]{:S(2)}) %collective-permute-start.4) | collective-permute-done | bytes 393248 | tf_op jit(solution)/shard_map/ppermute | solution.py:228
  63.6 8.9 %collective-permute-done.7.refs_4_ = f32[64,1536]{1,0:T(8,128)S(1)} collective-permute-done((f32[64,1536]{1,0:T(8,128)S(1)}, f32[64,1536]{1,0:T(8,128)S(1)}, u32[]{:S(2)}, u32[]{:S(2)}) %collective-permute-start.7) | collective-permute-done | bytes 393248 | tf_op jit(solution)/shard_map/ppermute | solution.py:237
  72.5 4.2 %collective-permute-done.8.refs_5_ = f32[64,1536]{1,0:T(8,128)S(1)} collective-permute-done((f32[64,1536]{1,0:T(8,128)S(1)}, f32[64,1536]{1,0:T(8,128)S(1)}, u32[]{:S(2)}, u32[]{:S(2)}) %collective-permute-start.8) | collective-permute-done | bytes 393248 | tf_op jit(solution)/shard_map/ppermute | solution.py:237
  78.7 13.9 %shard_map.86 = (f32[64,1536]{1,0:T(8,128)S(1)}, f32[64,1536]{1,0:T(8,128)S(1)}, f32[128,1536]{1,0:T(8,128)S(1)}) custom-call(s32[1]{0:T(128)} %bitcast.choice_ref, f32[64,1536]{1,0:T(8,128)} %copy-done.7, f32[64,1536]{1,0:T(8,128)} %copy-done.9, f32[64,1536]{1,0:T(8,128)} %collective-permute-done.5.refs_2_, f32[64,1536]{1,0:T(8,128)} %collective-permute-done.6.refs_3_, ...), custom_call_target="tpu_custom_call" | custom-call | flops 14495514624 | bytes 18874368 | tf_op jit(solution)/shard_map/pallas_call | solution.py:182
  96.5 13.8 %shard_map.87 = (f32[64,1536]{1,0:T(8,128)S(1)}, f32[64,1536]{1,0:T(8,128)S(1)}, f32[128,1536]{1,0:T(8,128)S(1)}) custom-call(s32[1]{0:T(128)} %bitcast.choice_ref, f32[64,1536]{1,0:T(8,128)} %copy-done.7, f32[64,1536]{1,0:T(8,128)} %copy-done.9, f32[64,1536]{1,0:T(8,128)} %collective-permute-done.5.refs_2_, f32[64,1536]{1,0:T(8,128)} %collective-permute-done.6.refs_3_, ...), custom_call_target="tpu_custom_call" | custom-call | flops 14495514624 | bytes 18874368 | tf_op jit(solution)/shard_map/pallas_call | solution.py:182
  111.4 2.5 collective-permute-done.24.refs_7_
  116.6 8.6 %collective-permute-done.25.refs_8_ = f32[64,1536]{1,0:T(8,128)S(1)} collective-permute-done((f32[64,1536]{1,0:T(8,128)S(1)}, f32[64,1536]{1,0:T(8,128)S(1)}, u32[]{:S(2)}, u32[]{:S(2)}) %collective-permute-start.25) | collective-permute-done | bytes 393248 | tf_op jit(solution)/shard_map/ppermute | solution.py:308
  125.2 5.2 %shard_map.89 = (f32[64,1536]{1,0:T(8,128)S(1)}, f32[64,1536]{1,0:T(8,128)S(1)}) custom-call(f32[64,3072]{1,0:T(8,128)} %refs_0_.5, f32[64,3072]{1,0:T(8,128)} %refs_1_.5, f32[64,1536]{1,0:T(8,128)} %get-tuple-element.52.refs_2_, f32[64,1536]{1,0:T(8,128)S(1)} %get-tuple-element.19.refs_17_.refs_3_, f32[128,1536]{1,0:T(8,128)S(1)} %collective-permute-done.22.refs_4_, ...), custom_call_target="tpu_custom_call" | custom-call | flops 19660800 | bytes 5505024 | tf_op jit(solution)/shard_map/pallas_call | solution.py:110
  131.1 4.1 %collective-permute-start.39 = (f32[64,1536]{1,0:T(8,128)S(1)}, f32[64,1536]{1,0:T(8,128)S(1)}, u32[]{:S(2)}, u32[]{:S(2)}) collective-permute-start(f32[64,1536]{1,0:T(8,128)S(1)} %get-tuple-element.28), channel_id=1, source_target_pairs={{0,4},{4,0},{8,12},{12,8},{1,5},{5,1},{9,13},{13,9},{2,6},{6,2},{1... | collective-permute-start | bytes 1179656 | tf_op jit(solution)/shard_map/ppermute | solution.py:220
  135.2 5.2 %shard_map.88 = (f32[64,1536]{1,0:T(8,128)S(1)}, f32[64,1536]{1,0:T(8,128)S(1)}, f32[64,3072]{1,0:T(8,128)S(1)}) custom-call(f32[64,3072]{1,0:T(8,128)} %refs_0_.5, f32[64,3072]{1,0:T(8,128)} %refs_1_.5, f32[64,1536]{1,0:T(8,128)} %get-tuple-element.53.refs_2_, f32[64,1536]{1,0:T(8,128)S(1)} %get-tuple-element.19.refs_17_.refs_3_, ...), custom_call_target="tpu_custom_call" | custom-call | flops 19660800 | bytes 5505024 | tf_op jit(solution)/shard_map/pallas_call | solution.py:110
  141.2 3.7 %collective-permute-start.38 = (f32[64,1536]{1,0:T(8,128)S(1)}, f32[64,1536]{1,0:T(8,128)S(1)}, u32[]{:S(2)}, u32[]{:S(2)}) collective-permute-start(f32[64,1536]{1,0:T(8,128)S(1)} %collective-permute-done.37), channel_id=1, source_target_pairs={{0,4},{4,0},{8,12},{12,8},{1,5},{5,1},{9,13},{13,9},{2,6},{6,2},{1... | collective-permute-start | bytes 1179656 | tf_op jit(solution)/shard_map/ppermute | solution.py:224
  145.8 7.7 %collective-permute-done.28 = f32[64,1536]{1,0:T(8,128)S(1)} collective-permute-done((f32[64,1536]{1,0:T(8,128)S(1)}, f32[64,1536]{1,0:T(8,128)S(1)}, u32[]{:S(2)}, u32[]{:S(2)}) %collective-permute-start.28) | collective-permute-done | bytes 393248 | tf_op jit(solution)/shard_map/ppermute | solution.py:220
  154.4 3.8 %collective-permute-start.27 = (f32[64,1536]{1,0:T(8,128)S(1)}, f32[64,1536]{1,0:T(8,128)S(1)}, u32[]{:S(2)}, u32[]{:S(2)}) collective-permute-start(f32[64,1536]{1,0:T(8,128)S(1)} %collective-permute-done.26), channel_id=1, source_target_pairs={{0,4},{4,0},{8,12},{12,8},{1,5},{5,1},{9,13},{13,9},{2,6},{6,2},{1... | collective-permute-start | bytes 1179656 | tf_op jit(solution)/shard_map/ppermute | solution.py:224
  158.3 3.7 %collective-permute-done.38 = f32[64,1536]{1,0:T(8,128)S(1)} collective-permute-done((f32[64,1536]{1,0:T(8,128)S(1)}, f32[64,1536]{1,0:T(8,128)S(1)}, u32[]{:S(2)}, u32[]{:S(2)}) %collective-permute-start.38) | collective-permute-done | bytes 393248 | tf_op jit(solution)/shard_map/ppermute | solution.py:224
  164.9 5.6 %collective-permute-done.27 = f32[64,1536]{1,0:T(8,128)S(1)} collective-permute-done((f32[64,1536]{1,0:T(8,128)S(1)}, f32[64,1536]{1,0:T(8,128)S(1)}, u32[]{:S(2)}, u32[]{:S(2)}) %collective-permute-start.27) | collective-permute-done | bytes 393248 | tf_op jit(solution)/shard_map/ppermute | solution.py:224
  171.1 6.1 %collective-permute-done.41 = f32[64,1536]{1,0:T(8,128)S(1)} collective-permute-done((f32[64,1536]{1,0:T(8,128)S(1)}, f32[64,1536]{1,0:T(8,128)S(1)}, u32[]{:S(2)}, u32[]{:S(2)}) %collective-permute-start.41) | collective-permute-done | bytes 393248 | tf_op jit(solution)/shard_map/ppermute | solution.py:228
  179.1 7.7 %collective-permute-done.30 = f32[64,1536]{1,0:T(8,128)S(1)} collective-permute-done((f32[64,1536]{1,0:T(8,128)S(1)}, f32[64,1536]{1,0:T(8,128)S(1)}, u32[]{:S(2)}, u32[]{:S(2)}) %collective-permute-start.30) | collective-permute-done | bytes 393248 | tf_op jit(solution)/shard_map/ppermute | solution.py:228
  189.6 9.2 %collective-permute-done.45.refs_13_ = f32[64,1536]{1,0:T(8,128)S(1)} collective-permute-done((f32[64,1536]{1,0:T(8,128)S(1)}, f32[64,1536]{1,0:T(8,128)S(1)}, u32[]{:S(2)}, u32[]{:S(2)}) %collective-permute-start.45) | collective-permute-done | bytes 393248 | tf_op jit(solution)/shard_map/ppermute | solution.py:237
  199.3 4.4 %collective-permute-done.34.refs_5_ = f32[64,1536]{1,0:T(8,128)S(1)} collective-permute-done((f32[64,1536]{1,0:T(8,128)S(1)}, f32[64,1536]{1,0:T(8,128)S(1)}, u32[]{:S(2)}, u32[]{:S(2)}) %collective-permute-start.34) | collective-permute-done | bytes 393248 | tf_op jit(solution)/shard_map/ppermute | solution.py:237
  206.3 13.8 %shard_map.90 = (f32[64,1536]{1,0:T(8,128)S(1)}, f32[64,1536]{1,0:T(8,128)S(1)}, f32[128,1536]{1,0:T(8,128)S(1)}) custom-call(s32[1]{0:T(128)} %bitcast.choice_ref, f32[64,1536]{1,0:T(8,128)} %copy-done.8, f32[64,1536]{1,0:T(8,128)} %copy-done.11, f32[64,1536]{1,0:T(8,128)} %copy-done.23, f32[64,1536]{1,0:T(8,128)} %copy-done.27, f32[64,1536]{1,0:T(8,128)} %copy-done.21, ...), custom_call_target="tpu_custom_call" | custom-call | flops 14495514624 | bytes 18874368 | tf_op jit(solution)/shard_map/pallas_call | solution.py:182
  223.2 13.8 %shard_map.91 = (f32[64,1536]{1,0:T(8,128)S(1)}, f32[64,1536]{1,0:T(8,128)S(1)}, f32[128,1536]{1,0:T(8,128)S(1)}) custom-call(s32[1]{0:T(128)} %bitcast.choice_ref, f32[64,1536]{1,0:T(8,128)} %copy-done.8, f32[64,1536]{1,0:T(8,128)} %copy-done.11, f32[64,1536]{1,0:T(8,128)} %copy-done.23, f32[64,1536]{1,0:T(8,128)} %copy-done.27, f32[64,1536]{1,0:T(8,128)} %copy-done.21, ...), custom_call_target="tpu_custom_call" | custom-call | flops 14495514624 | bytes 18874368 | tf_op jit(solution)/shard_map/pallas_call | solution.py:182
  237.3 2.3 collective-permute-done.50.refs_8_
  241.2 9.7 %collective-permute-done.51.refs_9_ = f32[64,1536]{1,0:T(8,128)S(1)} collective-permute-done((f32[64,1536]{1,0:T(8,128)S(1)}, f32[64,1536]{1,0:T(8,128)S(1)}, u32[]{:S(2)}, u32[]{:S(2)}) %collective-permute-start.51) | collective-permute-done | bytes 393248 | tf_op jit(solution)/shard_map/ppermute | solution.py:308
  250.9 8.6 %shard_map.92 = (f32[64,3072]{1,0:T(8,128)}, f32[64,3072]{1,0:T(8,128)}) custom-call(f32[64,3072]{1,0:T(8,128)S(1)} %copy-done, f32[64,3072]{1,0:T(8,128)S(1)} %copy-done.1, f32[64,1536]{1,0:T(8,128)S(1)} %get-tuple-element.25.refs_2_, f32[64,1536]{1,0:T(8,128)S(1)} %get-tuple-element.26.refs_3_, f32[64,1536]{1,0:T(8,128)S(1)} %get-tuple-element.29.refs_17_.refs_4_, ...), custom_call_target="tpu_custom_call" | custom-call | flops 39321600 | bytes 5505024 | tf_op jit(solution)/shard_map/pallas_call | solution.py:110
  (163 shorter events, 42.7 us)
Async XLA Ops:
  2.6 15.1 %collective-permute-start.13 = (f32[64,1536]{1,0:T(8,128)S(1)}, f32[64,1536]{1,0:T(8,128)S(1)}, u32[]{:S(2)}, u32[]{:S(2)}) collective-permute-start(f32[64,1536]{1,0:T(8,128)S(1)} %slice.33), channel_id=1, source_target_pairs={{0,4},{4,0},{8,12},{12,8},{1,5},{5,1},{9,13},{13,9},{2,6},{6,2},{1... | collective-permute-start | bytes 1179656 | tf_op jit(solution)/shard_map/ppermute | solution.py:220
  8.5 17.4 %collective-permute-start.12 = (f32[64,1536]{1,0:T(8,128)S(1)}, f32[64,1536]{1,0:T(8,128)S(1)}, u32[]{:S(2)}, u32[]{:S(2)}) collective-permute-start(f32[64,1536]{1,0:T(8,128)S(1)} %collective-permute-done.11), channel_id=1, source_target_pairs={{0,4},{4,0},{8,12},{12,8},{1,5},{5,1},{9,13},{13,9},{2,6},{6,2},{1... | collective-permute-start | bytes 1179656 | tf_op jit(solution)/shard_map/ppermute | solution.py:224
  26.1 12.1 %collective-permute-start.2 = (f32[64,1536]{1,0:T(8,128)S(1)}, f32[64,1536]{1,0:T(8,128)S(1)}, u32[]{:S(2)}, u32[]{:S(2)}) collective-permute-start(f32[64,1536]{1,0:T(8,128)S(1)} %get-tuple-element.54), channel_id=1, source_target_pairs={{0,4},{4,0},{8,12},{12,8},{1,5},{5,1},{9,13},{13,9},{2,6},{6,2},{1... | collective-permute-start | bytes 1179656 | tf_op jit(solution)/shard_map/ppermute | solution.py:220
  28.6 18.0 %collective-permute-start.15 = (f32[64,1536]{1,0:T(8,128)S(1)}, f32[64,1536]{1,0:T(8,128)S(1)}, u32[]{:S(2)}, u32[]{:S(2)}) collective-permute-start(f32[64,1536]{1,0:T(8,128)S(1)} %collective-permute-done.14), channel_id=1, source_target_pairs={{0,4},{4,0},{8,12},{12,8},{1,5},{5,1},{9,13},{13,9},{2,6},{6,2},{1... | collective-permute-start | bytes 1179656 | tf_op jit(solution)/shard_map/ppermute | solution.py:228
  31.7 16.5 %collective-permute-start.18 = (f32[64,1536]{1,0:T(8,128)S(1)}, f32[64,1536]{1,0:T(8,128)S(1)}, u32[]{:S(2)}, u32[]{:S(2)}) collective-permute-start(f32[64,1536]{1,0:T(8,128)S(1)} %get-tuple-element.36), channel_id=1, source_target_pairs={{0,2},{1,3},{2,0},{3,1},{4,6},{5,7},{6,4},{7,5},{8,10},{9,11},{10,... | collective-permute-start | bytes 1179656 | tf_op jit(solution)/shard_map/ppermute | solution.py:237
  33.2 29.1 %collective-permute-start.16 = (f32[64,1536]{1,0:T(8,128)S(1)}, f32[64,1536]{1,0:T(8,128)S(1)}, u32[]{:S(2)}, u32[]{:S(2)}) collective-permute-start(f32[64,1536]{1,0:T(8,128)S(1)} %get-tuple-element.37.refs_8_), channel_id=1, source_target_pairs={{0,1},{1,0},{2,3},{3,2},{4,5},{5,4},{6,7},{7,6},{8,9},{9,8},{10,11... | collective-permute-start | bytes 1179656 | tf_op jit(solution)/shard_map/ppermute | solution.py:238
  38.9 13.4 %collective-permute-start.1 = (f32[64,1536]{1,0:T(8,128)S(1)}, f32[64,1536]{1,0:T(8,128)S(1)}, u32[]{:S(2)}, u32[]{:S(2)}) collective-permute-start(f32[64,1536]{1,0:T(8,128)S(1)} %collective-permute-done), channel_id=1, source_target_pairs={{0,4},{4,0},{8,12},{12,8},{1,5},{5,1},{9,13},{13,9},{2,6},{6,2},{1... | collective-permute-start | bytes 1179656 | tf_op jit(solution)/shard_map/ppermute | solution.py:224
  46.7 16.3 %collective-permute-start.19 = (f32[64,1536]{1,0:T(8,128)S(1)}, f32[64,1536]{1,0:T(8,128)S(1)}, u32[]{:S(2)}, u32[]{:S(2)}) collective-permute-start(f32[64,1536]{1,0:T(8,128)S(1)} %get-tuple-element.48), channel_id=1, source_target_pairs={{0,2},{1,3},{2,0},{3,1},{4,6},{5,7},{6,4},{7,5},{8,10},{9,11},{10,... | collective-permute-start | bytes 1179656 | tf_op jit(solution)/shard_map/ppermute | solution.py:237
  48.2 14.7 %collective-permute-start.17 = (f32[64,1536]{1,0:T(8,128)S(1)}, f32[64,1536]{1,0:T(8,128)S(1)}, u32[]{:S(2)}, u32[]{:S(2)}) collective-permute-start(f32[64,1536]{1,0:T(8,128)S(1)} %get-tuple-element.49.refs_9_), channel_id=1, source_target_pairs={{0,1},{1,0},{2,3},{3,2},{4,5},{5,4},{6,7},{7,6},{8,9},{9,8},{10,11... | collective-permute-start | bytes 1179656 | tf_op jit(solution)/shard_map/ppermute | solution.py:238
  48.3 15.2 %collective-permute-start.20 = (f32[64,1536]{1,0:T(8,128)S(1)}, f32[64,1536]{1,0:T(8,128)S(1)}, u32[]{:S(2)}, u32[]{:S(2)}) collective-permute-start(f32[64,1536]{1,0:T(8,128)S(1)} %collective-permute-done.18.refs_12_), channel_id=1, source_target_pairs={{0,1},{1,0},{2,3},{3,2},{4,5},{5,4},{6,7},{7,6},{8,9},{9,8},{10,11... | collective-permute-start | bytes 1179656 | tf_op jit(solution)/shard_map/ppermute | solution.py:238
  62.3 14.3 %collective-permute-start.8 = (f32[64,1536]{1,0:T(8,128)S(1)}, f32[64,1536]{1,0:T(8,128)S(1)}, u32[]{:S(2)}, u32[]{:S(2)}) collective-permute-start(f32[64,1536]{1,0:T(8,128)S(1)} %get-tuple-element.50), channel_id=1, source_target_pairs={{0,2},{1,3},{2,0},{3,1},{4,6},{5,7},{6,4},{7,5},{8,10},{9,11},{10,... | collective-permute-start | bytes 1179656 | tf_op jit(solution)/shard_map/ppermute | solution.py:237
  62.9 13.8 %collective-permute-start.5 = (f32[64,1536]{1,0:T(8,128)S(1)}, f32[64,1536]{1,0:T(8,128)}, u32[]{:S(2)}, u32[]{:S(2)}) collective-permute-start(f32[64,1536]{1,0:T(8,128)S(1)} %get-tuple-element.39.refs_0_), channel_id=1, source_target_pairs={{0,1},{1,0},{2,3},{3,2},{4,5},{5,4},{6,7},{7,6},{8,9},{9,8},{10,11... | collective-permute-start | bytes 1179656 | tf_op jit(solution)/shard_map/ppermute | solution.py:238
  63.0 13.8 %collective-permute-start.21 = (f32[64,1536]{1,0:T(8,128)S(1)}, f32[64,1536]{1,0:T(8,128)}, u32[]{:S(2)}, u32[]{:S(2)}) collective-permute-start(f32[64,1536]{1,0:T(8,128)S(1)} %collective-permute-done.19.refs_13_), channel_id=1, source_target_pairs={{0,1},{1,0},{2,3},{3,2},{4,5},{5,4},{6,7},{7,6},{8,9},{9,8},{10,11... | collective-permute-start | bytes 1179656 | tf_op jit(solution)/shard_map/ppermute | solution.py:238
  63.5 13.3 %collective-permute-start.6 = (f32[64,1536]{1,0:T(8,128)S(1)}, f32[64,1536]{1,0:T(8,128)}, u32[]{:S(2)}, u32[]{:S(2)}) collective-permute-start(f32[64,1536]{1,0:T(8,128)S(1)} %get-tuple-element.51.refs_1_), channel_id=1, source_target_pairs={{0,1},{1,0},{2,3},{3,2},{4,5},{5,4},{6,7},{7,6},{8,9},{9,8},{10,11... | collective-permute-start | bytes 1179656 | tf_op jit(solution)/shard_map/ppermute | solution.py:238
  95.0 15.4 %collective-permute-start.23 = (f32[64,1536]{1,0:T(8,128)S(1)}, f32[64,1536]{1,0:T(8,128)S(1)}, u32[]{:S(2)}, u32[]{:S(2)}) collective-permute-start(f32[64,1536]{1,0:T(8,128)S(1)} %slice_add_fusion.3.refs_18_), channel_id=1, source_target_pairs={{0,2},{1,3},{2,0},{3,1},{4,6},{5,7},{6,4},{7,5},{8,10},{9,11},{10,... | collective-permute-start | bytes 1179656 | tf_op jit(solution)/shard_map/ppermute | solution.py:308
  131.1 14.0 %collective-permute-start.39 = (f32[64,1536]{1,0:T(8,128)S(1)}, f32[64,1536]{1,0:T(8,128)S(1)}, u32[]{:S(2)}, u32[]{:S(2)}) collective-permute-start(f32[64,1536]{1,0:T(8,128)S(1)} %get-tuple-element.28), channel_id=1, source_target_pairs={{0,4},{4,0},{8,12},{12,8},{1,5},{5,1},{9,13},{13,9},{2,6},{6,2},{1... | collective-permute-start | bytes 1179656 | tf_op jit(solution)/shard_map/ppermute | solution.py:220
  140.4 13.2 %collective-permute-start.28 = (f32[64,1536]{1,0:T(8,128)S(1)}, f32[64,1536]{1,0:T(8,128)S(1)}, u32[]{:S(2)}, u32[]{:S(2)}) collective-permute-start(f32[64,1536]{1,0:T(8,128)S(1)} %get-tuple-element.27), channel_id=1, source_target_pairs={{0,4},{4,0},{8,12},{12,8},{1,5},{5,1},{9,13},{13,9},{2,6},{6,2},{1... | collective-permute-start | bytes 1179656 | tf_op jit(solution)/shard_map/ppermute | solution.py:220
  140.5 13.9 %collective-permute-start.26 = (f32[64,1536]{1,0:T(8,128)S(1)}, f32[64,1536]{1,0:T(8,128)S(1)}, u32[]{:S(2)}, u32[]{:S(2)}) collective-permute-start(f32[64,1536]{1,0:T(8,128)S(1)} %get-tuple-element.27), channel_id=1, source_target_pairs={{0,0},{4,8},{8,4},{12,12},{1,1},{5,9},{9,5},{13,13},{2,2},{6,10},{... | collective-permute-start | bytes 1179656 | tf_op jit(solution)/shard_map/ppermute | solution.py:220
  141.2 20.8 %collective-permute-start.38 = (f32[64,1536]{1,0:T(8,128)S(1)}, f32[64,1536]{1,0:T(8,128)S(1)}, u32[]{:S(2)}, u32[]{:S(2)}) collective-permute-start(f32[64,1536]{1,0:T(8,128)S(1)} %collective-permute-done.37), channel_id=1, source_target_pairs={{0,4},{4,0},{8,12},{12,8},{1,5},{5,1},{9,13},{13,9},{2,6},{6,2},{1... | collective-permute-start | bytes 1179656 | tf_op jit(solution)/shard_map/ppermute | solution.py:224
  145.2 17.5 %collective-permute-start.40 = (f32[64,1536]{1,0:T(8,128)S(1)}, f32[64,1536]{1,0:T(8,128)S(1)}, u32[]{:S(2)}, u32[]{:S(2)}) collective-permute-start(f32[64,1536]{1,0:T(8,128)S(1)} %collective-permute-done.39), channel_id=1, source_target_pairs={{0,0},{4,8},{8,4},{12,12},{1,1},{5,9},{9,5},{13,13},{2,2},{6,10},{... | collective-permute-start | bytes 1179656 | tf_op jit(solution)/shard_map/ppermute | solution.py:224
  153.6 17.5 %collective-permute-start.29 = (f32[64,1536]{1,0:T(8,128)S(1)}, f32[64,1536]{1,0:T(8,128)S(1)}, u32[]{:S(2)}, u32[]{:S(2)}) collective-permute-start(f32[64,1536]{1,0:T(8,128)S(1)} %collective-permute-done.28), channel_id=1, source_target_pairs={{0,0},{4,8},{8,4},{12,12},{1,1},{5,9},{9,5},{13,13},{2,2},{6,10},{... | collective-permute-start | bytes 1179656 | tf_op jit(solution)/shard_map/ppermute | solution.py:224
  154.4 16.0 %collective-permute-start.27 = (f32[64,1536]{1,0:T(8,128)S(1)}, f32[64,1536]{1,0:T(8,128)S(1)}, u32[]{:S(2)}, u32[]{:S(2)}) collective-permute-start(f32[64,1536]{1,0:T(8,128)S(1)} %collective-permute-done.26), channel_id=1, source_target_pairs={{0,4},{4,0},{8,12},{12,8},{1,5},{5,1},{9,13},{13,9},{2,6},{6,2},{1... | collective-permute-start | bytes 1179656 | tf_op jit(solution)/shard_map/ppermute | solution.py:224
  162.1 25.3 %collective-permute-start.44 = (f32[64,1536]{1,0:T(8,128)S(1)}, f32[64,1536]{1,0:T(8,128)S(1)}, u32[]{:S(2)}, u32[]{:S(2)}) collective-permute-start(f32[64,1536]{1,0:T(8,128)S(1)} %get-tuple-element.42), channel_id=1, source_target_pairs={{0,2},{1,3},{2,0},{3,1},{4,6},{5,7},{6,4},{7,5},{8,10},{9,11},{10,... | collective-permute-start | bytes 1179656 | tf_op jit(solution)/shard_map/ppermute | solution.py:237
  162.7 24.8 %collective-permute-start.42 = (f32[64,1536]{1,0:T(8,128)S(1)}, f32[64,1536]{1,0:T(8,128)S(1)}, u32[]{:S(2)}, u32[]{:S(2)}) collective-permute-start(f32[64,1536]{1,0:T(8,128)S(1)} %get-tuple-element.43.refs_8_), channel_id=1, source_target_pairs={{0,1},{1,0},{2,3},{3,2},{4,5},{5,4},{6,7},{7,6},{8,9},{9,8},{10,11... | collective-permute-start | bytes 1179656 | tf_op jit(solution)/shard_map/ppermute | solution.py:238
  162.7 14.5 %collective-permute-start.41 = (f32[64,1536]{1,0:T(8,128)S(1)}, f32[64,1536]{1,0:T(8,128)S(1)}, u32[]{:S(2)}, u32[]{:S(2)}) collective-permute-start(f32[64,1536]{1,0:T(8,128)S(1)} %collective-permute-done.40), channel_id=1, source_target_pairs={{0,4},{4,0},{8,12},{12,8},{1,5},{5,1},{9,13},{13,9},{2,6},{6,2},{1... | collective-permute-start | bytes 1179656 | tf_op jit(solution)/shard_map/ppermute | solution.py:228
  170.5 18.5 %collective-permute-start.33 = (f32[64,1536]{1,0:T(8,128)S(1)}, f32[64,1536]{1,0:T(8,128)S(1)}, u32[]{:S(2)}, u32[]{:S(2)}) collective-permute-start(f32[64,1536]{1,0:T(8,128)S(1)} %get-tuple-element.46), channel_id=1, source_target_pairs={{0,2},{1,3},{2,0},{3,1},{4,6},{5,7},{6,4},{7,5},{8,10},{9,11},{10,... | collective-permute-start | bytes 1179656 | tf_op jit(solution)/shard_map/ppermute | solution.py:237
  171.1 18.1 %collective-permute-start.31 = (f32[64,1536]{1,0:T(8,128)S(1)}, f32[64,1536]{1,0:T(8,128)S(1)}, u32[]{:S(2)}, u32[]{:S(2)}) collective-permute-start(f32[64,1536]{1,0:T(8,128)S(1)} %get-tuple-element.47.refs_0_), channel_id=1, source_target_pairs={{0,1},{1,0},{2,3},{3,2},{4,5},{5,4},{6,7},{7,6},{8,9},{9,8},{10,11... | collective-permute-start | bytes 1179656 | tf_op jit(solution)/shard_map/ppermute | solution.py:238
  186.7 12.1 %collective-permute-start.45 = (f32[64,1536]{1,0:T(8,128)S(1)}, f32[64,1536]{1,0:T(8,128)S(1)}, u32[]{:S(2)}, u32[]{:S(2)}) collective-permute-start(f32[64,1536]{1,0:T(8,128)S(1)} %get-tuple-element.40), channel_id=1, source_target_pairs={{0,2},{1,3},{2,0},{3,1},{4,6},{5,7},{6,4},{7,5},{8,10},{9,11},{10,... | collective-permute-start | bytes 1179656 | tf_op jit(solution)/shard_map/ppermute | solution.py:237
  187.5 16.2 %collective-permute-start.34 = (f32[64,1536]{1,0:T(8,128)S(1)}, f32[64,1536]{1,0:T(8,128)S(1)}, u32[]{:S(2)}, u32[]{:S(2)}) collective-permute-start(f32[64,1536]{1,0:T(8,128)S(1)} %get-tuple-element.44), channel_id=1, source_target_pairs={{0,2},{1,3},{2,0},{3,1},{4,6},{5,7},{6,4},{7,5},{8,10},{9,11},{10,... | collective-permute-start | bytes 1179656 | tf_op jit(solution)/shard_map/ppermute | solution.py:237
  189.0 14.7 %collective-permute-start.32 = (f32[64,1536]{1,0:T(8,128)S(1)}, f32[64,1536]{1,0:T(8,128)S(1)}, u32[]{:S(2)}, u32[]{:S(2)}) collective-permute-start(f32[64,1536]{1,0:T(8,128)S(1)} %get-tuple-element.45.refs_1_), channel_id=1, source_target_pairs={{0,1},{1,0},{2,3},{3,2},{4,5},{5,4},{6,7},{7,6},{8,9},{9,8},{10,11... | collective-permute-start | bytes 1179656 | tf_op jit(solution)/shard_map/ppermute | solution.py:238
  189.2 14.6 %collective-permute-start.46 = (f32[64,1536]{1,0:T(8,128)S(1)}, f32[64,1536]{1,0:T(8,128)S(1)}, u32[]{:S(2)}, u32[]{:S(2)}) collective-permute-start(f32[64,1536]{1,0:T(8,128)S(1)} %collective-permute-done.44.refs_12_), channel_id=1, source_target_pairs={{0,1},{1,0},{2,3},{3,2},{4,5},{5,4},{6,7},{7,6},{8,9},{9,8},{10,11... | collective-permute-start | bytes 1179656 | tf_op jit(solution)/shard_map/ppermute | solution.py:238
  222.6 14.5 %collective-permute-start.49 = (f32[64,1536]{1,0:T(8,128)S(1)}, f32[64,1536]{1,0:T(8,128)S(1)}, u32[]{:S(2)}, u32[]{:S(2)}) collective-permute-start(f32[64,1536]{1,0:T(8,128)S(1)} %slice_add_fusion.1.refs_18_), channel_id=1, source_target_pairs={{0,2},{1,3},{2,0},{3,1},{4,6},{5,7},{6,4},{7,5},{8,10},{9,11},{10,... | collective-permute-start | bytes 1179656 | tf_op jit(solution)/shard_map/ppermute | solution.py:308
  (52 other events, 723.6 us)

commit v6 on v5

--- a/solution.py
+++ b/solution.py
@@ -308,8 +308,7 @@
                 sums.append([own, swapped, lax.ppermute(before, PLANE, ACROSS)])
             return sums
 
-        rates = jnp.exp(log_rate)
-        sums = product(spread([along(rates[:, cut]) for cut in cuts], False))
+        sums = product(spread([along(jnp.exp(log_rate[:, cut])) for cut in cuts], False))
         value, rates, first = step_kernel(
             step_size, False, 0, 2, base_stress, [log_rate[:, cuts[0]]], state, sums, None, *labels
         )

time: 260 us -> 263 us (1.012)
  other arithmetic: 1.96 us -> 4.89 us
    select_n x8, other arithmetic: 0.62 us -> 3.66 us  [shift(): sent = jnp.where(beside, second, first)]
where the time goes in v6:
time: 263 us; the launch traced here: 262 us
  waiting for transfers between devices  116 us (44%)
  Pallas kernels  74.3 us (28%)
  starting transfers between devices  62.7 us (24%)
  other arithmetic  4.89 us (2%)
  local copies, waits for them, and re-layouts  2.63 us (1%)
    pallas_call x4, Pallas kernels, rates_times(): pl.pallas_call(body, grid=(steps,), in_specs=[pl.BlockSpec(memory_space=p...  55.4 us
    ppermute x8, waiting for transfers between devices, shift(): got = lax.ppermute(sent, PLANE, ACROSS)  26.7 us
    ppermute x4, waiting for transfers between devices, spread_three(): return lax.ppermute(two[1], 'row', OUTER)  22.5 us
    ppermute x4, starting transfers between devices, spread_two(): lax.ppermute(near[1], 'row', OUTER)  21.3 us
    ppermute x4, waiting for transfers between devices, product(): sums.append([own, swapped, lax.ppermute(before, PLANE, ACROSS)])  20.8 us
    ppermute x4, waiting for transfers between devices, spread_two(): lax.ppermute(near[1], 'row', OUTER)  20.6 us
    pallas_call x3, Pallas kernels, step_kernel(): pl.pallas_call(body, grid=(1,), in_specs=[whole(base.shape), pl.BlockSpec...  19 us
    ppermute x4, waiting for transfers between devices, spread_one(): lax.ppermute(rates, 'row', OUTER)  13.1 us
  transfers between devices with their start and end apart: 52, of which 23 were waited for; matrix products, arithmetic and copies ran while one was open for 1% of the time, Pallas kernels for 13%

profile of v6, /device:TPU:0, one launch (start us, length us, event | category | flops | bytes accessed | tf_op | source)
XLA Modules:
  0.0 261.7 jit_solution(15324476085064600185)
XLA Ops:
  2.4 5.9 %collective-permute-start.13 = (f32[64,1536]{1,0:T(8,128)S(1)}, f32[64,1536]{1,0:T(8,128)S(1)}, u32[]{:S(2)}, u32[]{:S(2)}) collective-permute-start(f32[64,1536]{1,0:T(8,128)S(1)} %slice_exponential_fusion), channel_id=1, source_target_pairs={{0,4},{4,0},{8,12},{12,8},{1,5},{5,1},{9,13},{13,9},{2,6},{6,2},{1... | collective-permute-start | bytes 1179656 | tf_op jit(solution)/shard_map/ppermute | solution.py:220
  8.3 9.2 %collective-permute-start.12 = (f32[64,1536]{1,0:T(8,128)S(1)}, f32[64,1536]{1,0:T(8,128)S(1)}, u32[]{:S(2)}, u32[]{:S(2)}) collective-permute-start(f32[64,1536]{1,0:T(8,128)S(1)} %collective-permute-done.11), channel_id=1, source_target_pairs={{0,4},{4,0},{8,12},{12,8},{1,5},{5,1},{9,13},{13,9},{2,6},{6,2},{1... | collective-permute-start | bytes 1179656 | tf_op jit(solution)/shard_map/ppermute | solution.py:224
  18.1 7.6 %collective-permute-done.12 = f32[64,1536]{1,0:T(8,128)S(1)} collective-permute-done((f32[64,1536]{1,0:T(8,128)S(1)}, f32[64,1536]{1,0:T(8,128)S(1)}, u32[]{:S(2)}, u32[]{:S(2)}) %collective-permute-start.12) | collective-permute-done | bytes 393248 | tf_op jit(solution)/shard_map/ppermute | solution.py:224
  30.3 3.1 %collective-permute-start.15 = (f32[64,1536]{1,0:T(8,128)S(1)}, f32[64,1536]{1,0:T(8,128)S(1)}, u32[]{:S(2)}, u32[]{:S(2)}) collective-permute-start(f32[64,1536]{1,0:T(8,128)S(1)} %collective-permute-done.14), channel_id=1, source_target_pairs={{0,4},{4,0},{8,12},{12,8},{1,5},{5,1},{9,13},{13,9},{2,6},{6,2},{1... | collective-permute-start | bytes 1179656 | tf_op jit(solution)/shard_map/ppermute | solution.py:228
  34.9 5.0 %collective-permute-done.2 = f32[64,1536]{1,0:T(8,128)S(1)} collective-permute-done((f32[64,1536]{1,0:T(8,128)S(1)}, f32[64,1536]{1,0:T(8,128)S(1)}, u32[]{:S(2)}, u32[]{:S(2)}) %collective-permute-start.2) | collective-permute-done | bytes 393248 | tf_op jit(solution)/shard_map/ppermute | solution.py:220
  40.6 4.6 %collective-permute-start.1 = (f32[64,1536]{1,0:T(8,128)S(1)}, f32[64,1536]{1,0:T(8,128)S(1)}, u32[]{:S(2)}, u32[]{:S(2)}) collective-permute-start(f32[64,1536]{1,0:T(8,128)S(1)} %collective-permute-done), channel_id=1, source_target_pairs={{0,4},{4,0},{8,12},{12,8},{1,5},{5,1},{9,13},{13,9},{2,6},{6,2},{1... | collective-permute-start | bytes 1179656 | tf_op jit(solution)/shard_map/ppermute | solution.py:224
  45.2 3.1 %collective-permute-done.15 = f32[64,1536]{1,0:T(8,128)S(1)} collective-permute-done((f32[64,1536]{1,0:T(8,128)S(1)}, f32[64,1536]{1,0:T(8,128)S(1)}, u32[]{:S(2)}, u32[]{:S(2)}) %collective-permute-start.15) | collective-permute-done | bytes 393248 | tf_op jit(solution)/shard_map/ppermute | solution.py:228
  50.5 3.6 %collective-permute-done.1 = f32[64,1536]{1,0:T(8,128)S(1)} collective-permute-done((f32[64,1536]{1,0:T(8,128)S(1)}, f32[64,1536]{1,0:T(8,128)S(1)}, u32[]{:S(2)}, u32[]{:S(2)}) %collective-permute-start.1) | collective-permute-done | bytes 393248 | tf_op jit(solution)/shard_map/ppermute | solution.py:224
  56.8 5.6 %collective-permute-done.4 = f32[64,1536]{1,0:T(8,128)S(1)} collective-permute-done((f32[64,1536]{1,0:T(8,128)S(1)}, f32[64,1536]{1,0:T(8,128)S(1)}, u32[]{:S(2)}, u32[]{:S(2)}) %collective-permute-start.4) | collective-permute-done | bytes 393248 | tf_op jit(solution)/shard_map/ppermute | solution.py:228
  65.3 9.0 %collective-permute-done.7.refs_4_ = f32[64,1536]{1,0:T(8,128)} collective-permute-done((f32[64,1536]{1,0:T(8,128)S(1)}, f32[64,1536]{1,0:T(8,128)}, u32[]{:S(2)}, u32[]{:S(2)}) %collective-permute-start.7) | collective-permute-done | bytes 393248 | tf_op jit(solution)/shard_map/ppermute | solution.py:237
  74.3 4.1 %collective-permute-done.8.refs_5_ = f32[64,1536]{1,0:T(8,128)S(1)} collective-permute-done((f32[64,1536]{1,0:T(8,128)S(1)}, f32[64,1536]{1,0:T(8,128)S(1)}, u32[]{:S(2)}, u32[]{:S(2)}) %collective-permute-start.8) | collective-permute-done | bytes 393248 | tf_op jit(solution)/shard_map/ppermute | solution.py:237
  81.0 13.8 %shard_map.86 = (f32[64,1536]{1,0:T(8,128)S(1)}, f32[64,1536]{1,0:T(8,128)S(1)}, f32[128,1536]{1,0:T(8,128)S(1)}) custom-call(s32[1]{0:T(128)} %bitcast.choice_ref, f32[64,1536]{1,0:T(8,128)} %copy-done.6, f32[64,1536]{1,0:T(8,128)} %copy-done.8, f32[64,1536]{1,0:T(8,128)} %copy-done.22, f32[64,1536]{1,0:T(8,128)} %collective-permute-done.6.refs_3_, ...), custom_call_target="tpu_custom_call" | custom-call | flops 14495514624 | bytes 18874368 | tf_op jit(solution)/shard_map/pallas_call | solution.py:182
  98.8 13.8 %shard_map.87 = (f32[64,1536]{1,0:T(8,128)S(1)}, f32[64,1536]{1,0:T(8,128)S(1)}, f32[128,1536]{1,0:T(8,128)S(1)}) custom-call(s32[1]{0:T(128)} %bitcast.choice_ref, f32[64,1536]{1,0:T(8,128)} %copy-done.6, f32[64,1536]{1,0:T(8,128)} %copy-done.8, f32[64,1536]{1,0:T(8,128)} %copy-done.22, f32[64,1536]{1,0:T(8,128)} %collective-permute-done.6.refs_3_, ...), custom_call_target="tpu_custom_call" | custom-call | flops 14495514624 | bytes 18874368 | tf_op jit(solution)/shard_map/pallas_call | solution.py:182
  112.9 2.3 collective-permute-done.24.refs_7_
  116.5 10.8 %collective-permute-done.25.refs_8_ = f32[64,1536]{1,0:T(8,128)S(1)} collective-permute-done((f32[64,1536]{1,0:T(8,128)}, f32[64,1536]{1,0:T(8,128)S(1)}, u32[]{:S(2)}, u32[]{:S(2)}) %collective-permute-start.25) | collective-permute-done | bytes 393248 | tf_op jit(solution)/shard_map/ppermute | solution.py:308
  127.4 5.2 %shard_map.89 = (f32[64,1536]{1,0:T(8,128)S(1)}, f32[64,1536]{1,0:T(8,128)S(1)}) custom-call(f32[64,3072]{1,0:T(8,128)} %refs_0_.5, f32[64,3072]{1,0:T(8,128)} %refs_1_.5, f32[64,1536]{1,0:T(8,128)} %get-tuple-element.52.refs_2_, f32[64,1536]{1,0:T(8,128)S(1)} %get-tuple-element.19.refs_17_.refs_3_, f32[128,1536]{1,0:T(8,128)S(1)} %collective-permute-done.22.refs_4_, ...), custom_call_target="tpu_custom_call" | custom-call | flops 19660800 | bytes 5505024 | tf_op jit(solution)/shard_map/pallas_call | solution.py:110
  133.2 4.1 %collective-permute-start.39 = (f32[64,1536]{1,0:T(8,128)S(1)}, f32[64,1536]{1,0:T(8,128)S(1)}, u32[]{:S(2)}, u32[]{:S(2)}) collective-permute-start(f32[64,1536]{1,0:T(8,128)S(1)} %get-tuple-element.28), channel_id=1, source_target_pairs={{0,4},{4,0},{8,12},{12,8},{1,5},{5,1},{9,13},{13,9},{2,6},{6,2},{1... | collective-permute-start | bytes 1179656 | tf_op jit(solution)/shard_map/ppermute | solution.py:220
  137.3 5.2 %shard_map.88 = (f32[64,1536]{1,0:T(8,128)S(1)}, f32[64,1536]{1,0:T(8,128)S(1)}, f32[64,3072]{1,0:T(8,128)S(1)}) custom-call(f32[64,3072]{1,0:T(8,128)} %refs_0_.5, f32[64,3072]{1,0:T(8,128)} %refs_1_.5, f32[64,1536]{1,0:T(8,128)} %get-tuple-element.54.refs_2_, f32[64,1536]{1,0:T(8,128)S(1)} %get-tuple-element.19.refs_17_.refs_3_, ...), custom_call_target="tpu_custom_call" | custom-call | flops 19660800 | bytes 5505024 | tf_op jit(solution)/shard_map/pallas_call | solution.py:110
  143.3 3.7 %collective-permute-start.38 = (f32[64,1536]{1,0:T(8,128)S(1)}, f32[64,1536]{1,0:T(8,128)S(1)}, u32[]{:S(2)}, u32[]{:S(2)}) collective-permute-start(f32[64,1536]{1,0:T(8,128)S(1)} %collective-permute-done.37), channel_id=1, source_target_pairs={{0,4},{4,0},{8,12},{12,8},{1,5},{5,1},{9,13},{13,9},{2,6},{6,2},{1... | collective-permute-start | bytes 1179656 | tf_op jit(solution)/shard_map/ppermute | solution.py:224
  148.0 7.7 %collective-permute-done.28 = f32[64,1536]{1,0:T(8,128)S(1)} collective-permute-done((f32[64,1536]{1,0:T(8,128)S(1)}, f32[64,1536]{1,0:T(8,128)S(1)}, u32[]{:S(2)}, u32[]{:S(2)}) %collective-permute-start.28) | collective-permute-done | bytes 393248 | tf_op jit(solution)/shard_map/ppermute | solution.py:220
  156.7 3.8 %collective-permute-start.27 = (f32[64,1536]{1,0:T(8,128)S(1)}, f32[64,1536]{1,0:T(8,128)S(1)}, u32[]{:S(2)}, u32[]{:S(2)}) collective-permute-start(f32[64,1536]{1,0:T(8,128)S(1)} %collective-permute-done.26), channel_id=1, source_target_pairs={{0,4},{4,0},{8,12},{12,8},{1,5},{5,1},{9,13},{13,9},{2,6},{6,2},{1... | collective-permute-start | bytes 1179656 | tf_op jit(solution)/shard_map/ppermute | solution.py:224
  160.4 3.8 %collective-permute-done.38 = f32[64,1536]{1,0:T(8,128)S(1)} collective-permute-done((f32[64,1536]{1,0:T(8,128)S(1)}, f32[64,1536]{1,0:T(8,128)S(1)}, u32[]{:S(2)}, u32[]{:S(2)}) %collective-permute-start.38) | collective-permute-done | bytes 393248 | tf_op jit(solution)/shard_map/ppermute | solution.py:224
  167.0 5.7 %collective-permute-done.27 = f32[64,1536]{1,0:T(8,128)S(1)} collective-permute-done((f32[64,1536]{1,0:T(8,128)S(1)}, f32[64,1536]{1,0:T(8,128)S(1)}, u32[]{:S(2)}, u32[]{:S(2)}) %collective-permute-start.27) | collective-permute-done | bytes 393248 | tf_op jit(solution)/shard_map/ppermute | solution.py:224
  173.2 6.1 %collective-permute-done.41 = f32[64,1536]{1,0:T(8,128)S(1)} collective-permute-done((f32[64,1536]{1,0:T(8,128)S(1)}, f32[64,1536]{1,0:T(8,128)S(1)}, u32[]{:S(2)}, u32[]{:S(2)}) %collective-permute-start.41) | collective-permute-done | bytes 393248 | tf_op jit(solution)/shard_map/ppermute | solution.py:228
  181.2 7.6 %collective-permute-done.30 = f32[64,1536]{1,0:T(8,128)S(1)} collective-permute-done((f32[64,1536]{1,0:T(8,128)S(1)}, f32[64,1536]{1,0:T(8,128)S(1)}, u32[]{:S(2)}, u32[]{:S(2)}) %collective-permute-start.30) | collective-permute-done | bytes 393248 | tf_op jit(solution)/shard_map/ppermute | solution.py:228
  191.6 9.2 %collective-permute-done.45.refs_13_ = f32[64,1536]{1,0:T(8,128)S(1)} collective-permute-done((f32[64,1536]{1,0:T(8,128)S(1)}, f32[64,1536]{1,0:T(8,128)S(1)}, u32[]{:S(2)}, u32[]{:S(2)}) %collective-permute-start.45) | collective-permute-done | bytes 393248 | tf_op jit(solution)/shard_map/ppermute | solution.py:237
  201.3 4.3 %collective-permute-done.34.refs_5_ = f32[64,1536]{1,0:T(8,128)S(1)} collective-permute-done((f32[64,1536]{1,0:T(8,128)S(1)}, f32[64,1536]{1,0:T(8,128)S(1)}, u32[]{:S(2)}, u32[]{:S(2)}) %collective-permute-start.34) | collective-permute-done | bytes 393248 | tf_op jit(solution)/shard_map/ppermute | solution.py:237
  208.3 13.8 %shard_map.90 = (f32[64,1536]{1,0:T(8,128)S(1)}, f32[64,1536]{1,0:T(8,128)S(1)}, f32[128,1536]{1,0:T(8,128)S(1)}) custom-call(s32[1]{0:T(128)} %bitcast.choice_ref, f32[64,1536]{1,0:T(8,128)} %copy-done.7, f32[64,1536]{1,0:T(8,128)} %copy-done.10, f32[64,1536]{1,0:T(8,128)} %copy-done.21, f32[64,1536]{1,0:T(8,128)} %copy-done.29, f32[64,1536]{1,0:T(8,128)} %copy-done.19, ...), custom_call_target="tpu_custom_call" | custom-call | flops 14495514624 | bytes 18874368 | tf_op jit(solution)/shard_map/pallas_call | solution.py:182
  225.4 13.8 %shard_map.91 = (f32[64,1536]{1,0:T(8,128)S(1)}, f32[64,1536]{1,0:T(8,128)S(1)}, f32[128,1536]{1,0:T(8,128)S(1)}) custom-call(s32[1]{0:T(128)} %bitcast.choice_ref, f32[64,1536]{1,0:T(8,128)} %copy-done.7, f32[64,1536]{1,0:T(8,128)} %copy-done.10, f32[64,1536]{1,0:T(8,128)} %copy-done.21, f32[64,1536]{1,0:T(8,128)} %copy-done.29, f32[64,1536]{1,0:T(8,128)} %copy-done.19, ...), custom_call_target="tpu_custom_call" | custom-call | flops 14495514624 | bytes 18874368 | tf_op jit(solution)/shard_map/pallas_call | solution.py:182
  239.5 2.3 collective-permute-done.50.refs_8_
  243.1 9.9 %collective-permute-done.51.refs_9_ = f32[64,1536]{1,0:T(8,128)S(1)} collective-permute-done((f32[64,1536]{1,0:T(8,128)S(1)}, f32[64,1536]{1,0:T(8,128)S(1)}, u32[]{:S(2)}, u32[]{:S(2)}) %collective-permute-start.51) | collective-permute-done | bytes 393248 | tf_op jit(solution)/shard_map/ppermute | solution.py:308
  253.0 8.7 %shard_map.92 = (f32[64,3072]{1,0:T(8,128)}, f32[64,3072]{1,0:T(8,128)}) custom-call(f32[64,3072]{1,0:T(8,128)S(1)} %copy-done, f32[64,3072]{1,0:T(8,128)S(1)} %copy-done.1, f32[64,1536]{1,0:T(8,128)S(1)} %get-tuple-element.25.refs_2_, f32[64,1536]{1,0:T(8,128)S(1)} %get-tuple-element.26.refs_3_, f32[64,1536]{1,0:T(8,128)S(1)} %get-tuple-element.29.refs_17_.refs_4_, ...), custom_call_target="tpu_custom_call" | custom-call | flops 39321600 | bytes 5505024 | tf_op jit(solution)/shard_map/pallas_call | solution.py:110
  (165 shorter events, 43.7 us)
Async XLA Ops:
  2.4 15.1 %collective-permute-start.13 = (f32[64,1536]{1,0:T(8,128)S(1)}, f32[64,1536]{1,0:T(8,128)S(1)}, u32[]{:S(2)}, u32[]{:S(2)}) collective-permute-start(f32[64,1536]{1,0:T(8,128)S(1)} %slice_exponential_fusion), channel_id=1, source_target_pairs={{0,4},{4,0},{8,12},{12,8},{1,5},{5,1},{9,13},{13,9},{2,6},{6,2},{1... | collective-permute-start | bytes 1179656 | tf_op jit(solution)/shard_map/ppermute | solution.py:220
  8.3 17.4 %collective-permute-start.12 = (f32[64,1536]{1,0:T(8,128)S(1)}, f32[64,1536]{1,0:T(8,128)S(1)}, u32[]{:S(2)}, u32[]{:S(2)}) collective-permute-start(f32[64,1536]{1,0:T(8,128)S(1)} %collective-permute-done.11), channel_id=1, source_target_pairs={{0,4},{4,0},{8,12},{12,8},{1,5},{5,1},{9,13},{13,9},{2,6},{6,2},{1... | collective-permute-start | bytes 1179656 | tf_op jit(solution)/shard_map/ppermute | solution.py:224
  17.5 12.8 %collective-permute-start.14 = (f32[64,1536]{1,0:T(8,128)S(1)}, f32[64,1536]{1,0:T(8,128)S(1)}, u32[]{:S(2)}, u32[]{:S(2)}) collective-permute-start(f32[64,1536]{1,0:T(8,128)S(1)} %collective-permute-done.13), channel_id=1, source_target_pairs={{0,0},{4,8},{8,4},{12,12},{1,1},{5,9},{9,5},{13,13},{2,2},{6,10},{... | collective-permute-start | bytes 1179656 | tf_op jit(solution)/shard_map/ppermute | solution.py:224
  27.8 12.1 %collective-permute-start.2 = (f32[64,1536]{1,0:T(8,128)S(1)}, f32[64,1536]{1,0:T(8,128)S(1)}, u32[]{:S(2)}, u32[]{:S(2)}) collective-permute-start(f32[64,1536]{1,0:T(8,128)S(1)} %get-tuple-element.53), channel_id=1, source_target_pairs={{0,4},{4,0},{8,12},{12,8},{1,5},{5,1},{9,13},{13,9},{2,6},{6,2},{1... | collective-permute-start | bytes 1179656 | tf_op jit(solution)/shard_map/ppermute | solution.py:220
  30.3 18.0 %collective-permute-start.15 = (f32[64,1536]{1,0:T(8,128)S(1)}, f32[64,1536]{1,0:T(8,128)S(1)}, u32[]{:S(2)}, u32[]{:S(2)}) collective-permute-start(f32[64,1536]{1,0:T(8,128)S(1)} %collective-permute-done.14), channel_id=1, source_target_pairs={{0,4},{4,0},{8,12},{12,8},{1,5},{5,1},{9,13},{13,9},{2,6},{6,2},{1... | collective-permute-start | bytes 1179656 | tf_op jit(solution)/shard_map/ppermute | solution.py:228
  33.4 16.5 %collective-permute-start.18 = (f32[64,1536]{1,0:T(8,128)S(1)}, f32[64,1536]{1,0:T(8,128)S(1)}, u32[]{:S(2)}, u32[]{:S(2)}) collective-permute-start(f32[64,1536]{1,0:T(8,128)S(1)} %get-tuple-element.36), channel_id=1, source_target_pairs={{0,2},{1,3},{2,0},{3,1},{4,6},{5,7},{6,4},{7,5},{8,10},{9,11},{10,... | collective-permute-start | bytes 1179656 | tf_op jit(solution)/shard_map/ppermute | solution.py:237
  34.9 29.1 %collective-permute-start.16 = (f32[64,1536]{1,0:T(8,128)S(1)}, f32[64,1536]{1,0:T(8,128)S(1)}, u32[]{:S(2)}, u32[]{:S(2)}) collective-permute-start(f32[64,1536]{1,0:T(8,128)S(1)} %get-tuple-element.37.refs_8_), channel_id=1, source_target_pairs={{0,1},{1,0},{2,3},{3,2},{4,5},{5,4},{6,7},{7,6},{8,9},{9,8},{10,11... | collective-permute-start | bytes 1179656 | tf_op jit(solution)/shard_map/ppermute | solution.py:238
  40.6 13.4 %collective-permute-start.1 = (f32[64,1536]{1,0:T(8,128)S(1)}, f32[64,1536]{1,0:T(8,128)S(1)}, u32[]{:S(2)}, u32[]{:S(2)}) collective-permute-start(f32[64,1536]{1,0:T(8,128)S(1)} %collective-permute-done), channel_id=1, source_target_pairs={{0,4},{4,0},{8,12},{12,8},{1,5},{5,1},{9,13},{13,9},{2,6},{6,2},{1... | collective-permute-start | bytes 1179656 | tf_op jit(solution)/shard_map/ppermute | solution.py:224
  48.4 16.3 %collective-permute-start.19 = (f32[64,1536]{1,0:T(8,128)S(1)}, f32[64,1536]{1,0:T(8,128)}, u32[]{:S(2)}, u32[]{:S(2)}) collective-permute-start(f32[64,1536]{1,0:T(8,128)S(1)} %get-tuple-element.48), channel_id=1, source_target_pairs={{0,2},{1,3},{2,0},{3,1},{4,6},{5,7},{6,4},{7,5},{8,10},{9,11},{10,... | collective-permute-start | bytes 1179656 | tf_op jit(solution)/shard_map/ppermute | solution.py:237
  49.9 14.7 %collective-permute-start.17 = (f32[64,1536]{1,0:T(8,128)S(1)}, f32[64,1536]{1,0:T(8,128)S(1)}, u32[]{:S(2)}, u32[]{:S(2)}) collective-permute-start(f32[64,1536]{1,0:T(8,128)S(1)} %get-tuple-element.49.refs_9_), channel_id=1, source_target_pairs={{0,1},{1,0},{2,3},{3,2},{4,5},{5,4},{6,7},{7,6},{8,9},{9,8},{10,11... | collective-permute-start | bytes 1179656 | tf_op jit(solution)/shard_map/ppermute | solution.py:238
  50.0 15.2 %collective-permute-start.20 = (f32[64,1536]{1,0:T(8,128)S(1)}, f32[64,1536]{1,0:T(8,128)S(1)}, u32[]{:S(2)}, u32[]{:S(2)}) collective-permute-start(f32[64,1536]{1,0:T(8,128)S(1)} %collective-permute-done.18.refs_12_), channel_id=1, source_target_pairs={{0,1},{1,0},{2,3},{3,2},{4,5},{5,4},{6,7},{7,6},{8,9},{9,8},{10,11... | collective-permute-start | bytes 1179656 | tf_op jit(solution)/shard_map/ppermute | solution.py:238
  64.0 14.3 %collective-permute-start.8 = (f32[64,1536]{1,0:T(8,128)S(1)}, f32[64,1536]{1,0:T(8,128)S(1)}, u32[]{:S(2)}, u32[]{:S(2)}) collective-permute-start(f32[64,1536]{1,0:T(8,128)S(1)} %get-tuple-element.50), channel_id=1, source_target_pairs={{0,2},{1,3},{2,0},{3,1},{4,6},{5,7},{6,4},{7,5},{8,10},{9,11},{10,... | collective-permute-start | bytes 1179656 | tf_op jit(solution)/shard_map/ppermute | solution.py:237
  64.6 13.9 %collective-permute-start.5 = (f32[64,1536]{1,0:T(8,128)S(1)}, f32[64,1536]{1,0:T(8,128)S(1)}, u32[]{:S(2)}, u32[]{:S(2)}) collective-permute-start(f32[64,1536]{1,0:T(8,128)S(1)} %get-tuple-element.39.refs_0_), channel_id=1, source_target_pairs={{0,1},{1,0},{2,3},{3,2},{4,5},{5,4},{6,7},{7,6},{8,9},{9,8},{10,11... | collective-permute-start | bytes 1179656 | tf_op jit(solution)/shard_map/ppermute | solution.py:238
  64.7 13.8 %collective-permute-start.21 = (f32[64,1536]{1,0:T(8,128)}, f32[64,1536]{1,0:T(8,128)S(1)}, u32[]{:S(2)}, u32[]{:S(2)}) collective-permute-start(f32[64,1536]{1,0:T(8,128)} %collective-permute-done.19.refs_13_), channel_id=1, source_target_pairs={{0,1},{1,0},{2,3},{3,2},{4,5},{5,4},{6,7},{7,6},{8,9},{9,8},{10,11... | collective-permute-start | bytes 1179656 | tf_op jit(solution)/shard_map/ppermute | solution.py:238
  65.2 13.4 %collective-permute-start.6 = (f32[64,1536]{1,0:T(8,128)S(1)}, f32[64,1536]{1,0:T(8,128)}, u32[]{:S(2)}, u32[]{:S(2)}) collective-permute-start(f32[64,1536]{1,0:T(8,128)S(1)} %get-tuple-element.51.refs_1_), channel_id=1, source_target_pairs={{0,1},{1,0},{2,3},{3,2},{4,5},{5,4},{6,7},{7,6},{8,9},{9,8},{10,11... | collective-permute-start | bytes 1179656 | tf_op jit(solution)/shard_map/ppermute | solution.py:238
  97.2 15.4 %collective-permute-start.23 = (f32[64,1536]{1,0:T(8,128)S(1)}, f32[64,1536]{1,0:T(8,128)S(1)}, u32[]{:S(2)}, u32[]{:S(2)}) collective-permute-start(f32[64,1536]{1,0:T(8,128)S(1)} %slice_add_fusion.3.refs_18_), channel_id=1, source_target_pairs={{0,2},{1,3},{2,0},{3,1},{4,6},{5,7},{6,4},{7,5},{8,10},{9,11},{10,... | collective-permute-start | bytes 1179656 | tf_op jit(solution)/shard_map/ppermute | solution.py:308
  133.2 14.1 %collective-permute-start.39 = (f32[64,1536]{1,0:T(8,128)S(1)}, f32[64,1536]{1,0:T(8,128)S(1)}, u32[]{:S(2)}, u32[]{:S(2)}) collective-permute-start(f32[64,1536]{1,0:T(8,128)S(1)} %get-tuple-element.28), channel_id=1, source_target_pairs={{0,4},{4,0},{8,12},{12,8},{1,5},{5,1},{9,13},{13,9},{2,6},{6,2},{1... | collective-permute-start | bytes 1179656 | tf_op jit(solution)/shard_map/ppermute | solution.py:220
  142.5 13.3 %collective-permute-start.28 = (f32[64,1536]{1,0:T(8,128)S(1)}, f32[64,1536]{1,0:T(8,128)S(1)}, u32[]{:S(2)}, u32[]{:S(2)}) collective-permute-start(f32[64,1536]{1,0:T(8,128)S(1)} %get-tuple-element.27), channel_id=1, source_target_pairs={{0,4},{4,0},{8,12},{12,8},{1,5},{5,1},{9,13},{13,9},{2,6},{6,2},{1... | collective-permute-start | bytes 1179656 | tf_op jit(solution)/shard_map/ppermute | solution.py:220
  142.6 14.1 %collective-permute-start.26 = (f32[64,1536]{1,0:T(8,128)S(1)}, f32[64,1536]{1,0:T(8,128)S(1)}, u32[]{:S(2)}, u32[]{:S(2)}) collective-permute-start(f32[64,1536]{1,0:T(8,128)S(1)} %get-tuple-element.27), channel_id=1, source_target_pairs={{0,0},{4,8},{8,4},{12,12},{1,1},{5,9},{9,5},{13,13},{2,2},{6,10},{... | collective-permute-start | bytes 1179656 | tf_op jit(solution)/shard_map/ppermute | solution.py:220
  143.3 20.9 %collective-permute-start.38 = (f32[64,1536]{1,0:T(8,128)S(1)}, f32[64,1536]{1,0:T(8,128)S(1)}, u32[]{:S(2)}, u32[]{:S(2)}) collective-permute-start(f32[64,1536]{1,0:T(8,128)S(1)} %collective-permute-done.37), channel_id=1, source_target_pairs={{0,4},{4,0},{8,12},{12,8},{1,5},{5,1},{9,13},{13,9},{2,6},{6,2},{1... | collective-permute-start | bytes 1179656 | tf_op jit(solution)/shard_map/ppermute | solution.py:224
  147.4 17.6 %collective-permute-start.40 = (f32[64,1536]{1,0:T(8,128)S(1)}, f32[64,1536]{1,0:T(8,128)S(1)}, u32[]{:S(2)}, u32[]{:S(2)}) collective-permute-start(f32[64,1536]{1,0:T(8,128)S(1)} %collective-permute-done.39), channel_id=1, source_target_pairs={{0,0},{4,8},{8,4},{12,12},{1,1},{5,9},{9,5},{13,13},{2,2},{6,10},{... | collective-permute-start | bytes 1179656 | tf_op jit(solution)/shard_map/ppermute | solution.py:224
  155.8 17.4 %collective-permute-start.29 = (f32[64,1536]{1,0:T(8,128)S(1)}, f32[64,1536]{1,0:T(8,128)S(1)}, u32[]{:S(2)}, u32[]{:S(2)}) collective-permute-start(f32[64,1536]{1,0:T(8,128)S(1)} %collective-permute-done.28), channel_id=1, source_target_pairs={{0,0},{4,8},{8,4},{12,12},{1,1},{5,9},{9,5},{13,13},{2,2},{6,10},{... | collective-permute-start | bytes 1179656 | tf_op jit(solution)/shard_map/ppermute | solution.py:224
  156.7 16.0 %collective-permute-start.27 = (f32[64,1536]{1,0:T(8,128)S(1)}, f32[64,1536]{1,0:T(8,128)S(1)}, u32[]{:S(2)}, u32[]{:S(2)}) collective-permute-start(f32[64,1536]{1,0:T(8,128)S(1)} %collective-permute-done.26), channel_id=1, source_target_pairs={{0,4},{4,0},{8,12},{12,8},{1,5},{5,1},{9,13},{13,9},{2,6},{6,2},{1... | collective-permute-start | bytes 1179656 | tf_op jit(solution)/shard_map/ppermute | solution.py:224
  164.3 25.2 %collective-permute-start.44 = (f32[64,1536]{1,0:T(8,128)S(1)}, f32[64,1536]{1,0:T(8,128)S(1)}, u32[]{:S(2)}, u32[]{:S(2)}) collective-permute-start(f32[64,1536]{1,0:T(8,128)S(1)} %get-tuple-element.42), channel_id=1, source_target_pairs={{0,2},{1,3},{2,0},{3,1},{4,6},{5,7},{6,4},{7,5},{8,10},{9,11},{10,... | collective-permute-start | bytes 1179656 | tf_op jit(solution)/shard_map/ppermute | solution.py:237
  164.9 24.7 %collective-permute-start.42 = (f32[64,1536]{1,0:T(8,128)S(1)}, f32[64,1536]{1,0:T(8,128)S(1)}, u32[]{:S(2)}, u32[]{:S(2)}) collective-permute-start(f32[64,1536]{1,0:T(8,128)S(1)} %get-tuple-element.43.refs_8_), channel_id=1, source_target_pairs={{0,1},{1,0},{2,3},{3,2},{4,5},{5,4},{6,7},{7,6},{8,9},{9,8},{10,11... | collective-permute-start | bytes 1179656 | tf_op jit(solution)/shard_map/ppermute | solution.py:238
  164.9 14.4 %collective-permute-start.41 = (f32[64,1536]{1,0:T(8,128)S(1)}, f32[64,1536]{1,0:T(8,128)S(1)}, u32[]{:S(2)}, u32[]{:S(2)}) collective-permute-start(f32[64,1536]{1,0:T(8,128)S(1)} %collective-permute-done.40), channel_id=1, source_target_pairs={{0,4},{4,0},{8,12},{12,8},{1,5},{5,1},{9,13},{13,9},{2,6},{6,2},{1... | collective-permute-start | bytes 1179656 | tf_op jit(solution)/shard_map/ppermute | solution.py:228
  172.7 18.3 %collective-permute-start.33 = (f32[64,1536]{1,0:T(8,128)S(1)}, f32[64,1536]{1,0:T(8,128)S(1)}, u32[]{:S(2)}, u32[]{:S(2)}) collective-permute-start(f32[64,1536]{1,0:T(8,128)S(1)} %get-tuple-element.46), channel_id=1, source_target_pairs={{0,2},{1,3},{2,0},{3,1},{4,6},{5,7},{6,4},{7,5},{8,10},{9,11},{10,... | collective-permute-start | bytes 1179656 | tf_op jit(solution)/shard_map/ppermute | solution.py:237
  173.2 18.0 %collective-permute-start.31 = (f32[64,1536]{1,0:T(8,128)S(1)}, f32[64,1536]{1,0:T(8,128)S(1)}, u32[]{:S(2)}, u32[]{:S(2)}) collective-permute-start(f32[64,1536]{1,0:T(8,128)S(1)} %get-tuple-element.47.refs_0_), channel_id=1, source_target_pairs={{0,1},{1,0},{2,3},{3,2},{4,5},{5,4},{6,7},{7,6},{8,9},{9,8},{10,11... | collective-permute-start | bytes 1179656 | tf_op jit(solution)/shard_map/ppermute | solution.py:238
  189.6 16.0 %collective-permute-start.34 = (f32[64,1536]{1,0:T(8,128)S(1)}, f32[64,1536]{1,0:T(8,128)S(1)}, u32[]{:S(2)}, u32[]{:S(2)}) collective-permute-start(f32[64,1536]{1,0:T(8,128)S(1)} %get-tuple-element.44), channel_id=1, source_target_pairs={{0,2},{1,3},{2,0},{3,1},{4,6},{5,7},{6,4},{7,5},{8,10},{9,11},{10,... | collective-permute-start | bytes 1179656 | tf_op jit(solution)/shard_map/ppermute | solution.py:237
  191.1 14.6 %collective-permute-start.32 = (f32[64,1536]{1,0:T(8,128)S(1)}, f32[64,1536]{1,0:T(8,128)S(1)}, u32[]{:S(2)}, u32[]{:S(2)}) collective-permute-start(f32[64,1536]{1,0:T(8,128)S(1)} %get-tuple-element.45.refs_1_), channel_id=1, source_target_pairs={{0,1},{1,0},{2,3},{3,2},{4,5},{5,4},{6,7},{7,6},{8,9},{9,8},{10,11... | collective-permute-start | bytes 1179656 | tf_op jit(solution)/shard_map/ppermute | solution.py:238
  191.2 14.5 %collective-permute-start.46 = (f32[64,1536]{1,0:T(8,128)S(1)}, f32[64,1536]{1,0:T(8,128)S(1)}, u32[]{:S(2)}, u32[]{:S(2)}) collective-permute-start(f32[64,1536]{1,0:T(8,128)S(1)} %collective-permute-done.44.refs_12_), channel_id=1, source_target_pairs={{0,1},{1,0},{2,3},{3,2},{4,5},{5,4},{6,7},{7,6},{8,9},{9,8},{10,11... | collective-permute-start | bytes 1179656 | tf_op jit(solution)/shard_map/ppermute | solution.py:238
  224.5 14.7 %collective-permute-start.49 = (f32[64,1536]{1,0:T(8,128)S(1)}, f32[64,1536]{1,0:T(8,128)S(1)}, u32[]{:S(2)}, u32[]{:S(2)}) collective-permute-start(f32[64,1536]{1,0:T(8,128)S(1)} %slice_add_fusion.1.refs_18_), channel_id=1, source_target_pairs={{0,2},{1,3},{2,0},{3,1},{4,6},{5,7},{6,4},{7,5},{8,10},{9,11},{10,... | collective-permute-start | bytes 1179656 | tf_op jit(solution)/shard_map/ppermute | solution.py:308
  (54 other events, 704.1 us)
